TPU v7x, 32 devices: a whole 2x2x4 slice. The times are simulated.
32 devices in a mesh: exp: 8 (over z, x), tp: 4 (over y, core).
Axes of the slice: x: 2, y: 2, z: 4, core: 2. Of those that a mesh axis runs over, the one named last changes fastest.
Arguments:
- tokens: bfloat16 [2048, 3584], P('exp', 'tp'), may hold values from -6 to 6
- cotangent: bfloat16 [2048, 3584], P('exp', 'tp'), may hold values from -3 to 3
- up_weight: bfloat16 [8, 3584, 2432], P('exp', None, 'tp'), may hold values from -0.09375 to 0.09375
- down_weight: bfloat16 [8, 2432, 3584], P('exp', 'tp'), may hold values from -0.125 to 0.125
- expert_ids: int32 [2048, 2], P('exp'), may hold values from 0 to 7, all different within a row; in each aligned block of 256 rows (0 to 255, 256 to 511, ...) at most 128 rows name the same one
- gate_probs: bfloat16 [2048, 2], P('exp'), may hold values from 0.049804688 to 0.94921875
Outputs:
- token_grad: bfloat16 [2048, 3584], P('exp', 'tp')
- up_grad: bfloat16 [8, 3584, 2432], P('exp', None, 'tp')
- down_grad: bfloat16 [8, 2432, 3584], P('exp', 'tp')
Inputs may be any that keep to these rules, and one draw needn't show every extreme that they name: `expert_ids`: each row names 2 different experts. Among the 256 rows of one index of exp no expert is named more than 128 times, a bound that some block reaches.
All inputs are finite; a program needn't handle non-finite values.
Results may differ from a plain program's by a relative error of at most 0.019.
Values may be sent and summed in bfloat16 or wider, within the bound.
No kernel may reach another device: no remote copies, remote signals or barrier semaphores. Data moves between devices by JAX's collectives and lax.ppermute only.
A program may use at most 128 MiB of HBM per device.

v0:
```python
import jax
import jax.numpy as jnp
from jax import lax
from jax.sharding import PartitionSpec as P


def prefix(value, axis, join, neutral):
    count, mine = (lax.axis_size(axis), lax.axis_index(axis))
    pieces = lax.all_gather(value, axis)
    total = jnp.full_like(value, 0) + jnp.asarray(neutral, value.dtype)

    def step(position, total):
        longer = join(total, pieces[position])
        return jnp.where(position < mine, longer, total)

    return lax.fori_loop(0, count - 1, step, total)


def silu_parts(hidden):
    sigma = jax.nn.sigmoid(hidden)
    return (hidden * sigma, sigma * (1.0 + hidden * (1.0 - sigma)))


def add_counts(earlier, later):
    return earlier + later


def expert_terms(inputs, cotan_rows, probs_rows, w_up, w_down):
    routed = (probs_rows.astype(jnp.float32)[:, None] * cotan_rows.astype(jnp.float32)).astype(
        jnp.bfloat16
    )
    hidden = jnp.dot(inputs, w_up, preferred_element_type=jnp.float32)
    act_full, slope = silu_parts(hidden)
    act = act_full.astype(jnp.bfloat16)
    d_act = lax.dot_general(
        routed, w_down, (((1,), (1,)), ((), ())), preferred_element_type=jnp.float32
    )
    d_hidden = (d_act * slope).astype(jnp.bfloat16)
    grad_up = lax.dot_general(
        inputs, d_hidden, (((0,), (0,)), ((), ())), preferred_element_type=jnp.float32
    ).astype(jnp.bfloat16)
    grad_down = lax.dot_general(
        act, routed, (((0,), (0,)), ((), ())), preferred_element_type=jnp.float32
    ).astype(jnp.bfloat16)
    term = lax.dot_general(
        d_hidden, w_up, (((1,), (1,)), ((), ())), preferred_element_type=jnp.float32
    )
    return (grad_up, grad_down, term)


def per_device(tokens, cotangent, up_weight, down_weight, expert_ids, gate_probs):
    tok_count, top_count = expert_ids.shape
    exp_local = up_weight.shape[0]
    n_exp = lax.axis_size("exp")
    experts = n_exp * exp_local
    slot_size = 4 * tok_count // experts
    capacity = 5 * tok_count * n_exp // (2 * experts)
    flat_ids = expert_ids.reshape(-1)
    pairs = flat_ids.shape[0]
    onehot = (flat_ids[:, None] == jnp.arange(experts, dtype=jnp.int32)[None, :]).astype(jnp.int32)
    local_rank = jnp.sum(onehot * (jnp.cumsum(onehot, axis=0) - 1), axis=1)
    counts = jnp.sum(onehot, axis=0)
    before = prefix(counts, "exp", add_counts, jnp.zeros_like(counts))
    ranks = local_rank + jnp.sum(onehot * before[None, :], axis=1).astype(jnp.int32)
    keep = ranks < capacity
    buffer_rows = experts * slot_size
    target = jnp.where(keep, flat_ids * slot_size + local_rank, buffer_rows)
    source = (
        jnp.zeros((buffer_rows + 1,), jnp.int32)
        .at[target]
        .set(jnp.arange(pairs, dtype=jnp.int32))[:-1]
    )
    filled = jnp.zeros((buffer_rows + 1,), jnp.int32).at[target].set(1)[:-1] > 0
    token_rows = source // top_count
    send_probs = jnp.where(
        filled, gate_probs.reshape(-1)[source], jnp.zeros_like(gate_probs[0, :1])
    )
    full_tokens, full_cotan = (
        lax.all_gather(tokens, "tp", axis=1, tiled=True),
        lax.all_gather(cotangent, "tp", axis=1, tiled=True),
    )
    send_x = jnp.where(filled[:, None], full_tokens[token_rows], jnp.zeros_like(full_tokens[:1]))
    send_dy = jnp.where(filled[:, None], full_cotan[token_rows], jnp.zeros_like(full_cotan[:1]))
    got_x, got_dy, got_probs = (
        lax.all_to_all(send_x, "exp", split_axis=0, concat_axis=0, tiled=True),
        lax.all_to_all(send_dy, "exp", split_axis=0, concat_axis=0, tiled=True),
        lax.all_to_all(send_probs, "exp", split_axis=0, concat_axis=0, tiled=True),
    )
    width = got_x.shape[1]
    view_x = got_x.reshape(n_exp, exp_local, slot_size, width)
    view_dy = got_dy.reshape(n_exp, exp_local, slot_size, width)
    view_p = got_probs.reshape(n_exp, exp_local, slot_size)
    rows_x = view_x[:, 0].reshape(-1, width)
    rows_dy = view_dy[:, 0].reshape(-1, width)
    rows_p = view_p[:, 0].reshape(-1)
    grad_up, grad_down, term = expert_terms(rows_x, rows_dy, rows_p, up_weight[0], down_weight[0])
    grads_up = [grad_up]
    grads_down = [grad_down]
    terms = [term.reshape(n_exp, slot_size, width)]
    term_all = jnp.stack(terms, axis=1).reshape(buffer_rows, width)
    safe_target = jnp.minimum(target, buffer_rows - 1)
    summed = lax.psum_scatter(
        term_all.astype(jnp.bfloat16), "tp", scatter_dimension=1, tiled=True
    ).astype(jnp.float32)
    returned = lax.all_to_all(
        summed.astype(jnp.bfloat16), "exp", split_axis=0, concat_axis=0, tiled=True
    ).astype(summed.dtype)
    per_pair = jnp.where(keep[:, None], returned[safe_target], jnp.float32(0.0))
    token_grad = jnp.sum(per_pair.reshape(tok_count, top_count, -1), axis=1).astype(jnp.bfloat16)
    return (token_grad, jnp.stack(grads_up, axis=0), jnp.stack(grads_down, axis=0))


def solution(mesh):
    placed = (
        P("exp", "tp"),
        P("exp", "tp"),
        P("exp", None, "tp"),
        P("exp", "tp", None),
        P("exp", None),
        P("exp", None),
    )
    return jax.shard_map(
        per_device,
        mesh=mesh,
        in_specs=placed,
        out_specs=(P("exp", "tp"), P("exp", None, "tp"), P("exp", "tp", None)),
        check_vma=False,
    )
```

profile of v0, /device:TPU:0, one launch (start us, length us, event | category | flops | bytes accessed | tf_op | source)
XLA Modules:
  0.0 586.6 jit_solution(13821780287359894006)
XLA Ops:
  7.2 0.0 all-gather.6.cloned.1.call-start
  7.2 0.7 all-gather.6.cloned.1.call-update
  7.9 0.0 all-gather.4.cloned.1.call-start
  7.9 0.7 all-gather.4.cloned.1.call-update
  8.7 0.8 copy.17
  9.5 0.1 eq.25
  9.6 0.1 eq.29
  9.8 0.1 convert_reduce_fusion
  9.9 1.2 dynamic-slice
  11.8 0.2 dynamic-update-slice
  12.0 13.1 %all-reduce = s32[64]{0:T(128)S(1)} all-reduce(s32[64]{0:T(128)S(1)} %dynamic-update-slice), channel_id=2, replica_groups=mesh['exp'=8,'tp'=4] {'exp'}, use_global_device_ids=true, to_apply=%add | all-reduce | flops 64 | bytes 512
  25.1 0.1 reshape.238
  25.2 1.1 reduce-window.6
  26.3 0.2 slice_reduce_fusion
  26.6 0.7 broadcast_multiply_fusion
  27.3 0.1 copy.19
  27.4 0.1 mul.61
  27.6 0.8 copy.20
  28.4 0.2 reshape.185
  28.5 0.3 while.14
  28.8 0.1 select_reduce_fusion.1
  29.0 2.5 scatter_custom_fusion.1
  31.4 2.5 scatter_custom_fusion
  33.9 6.8 %gather_fusion = bf16[1024]{0:T(1024)(128)(2,1)S(1)} fusion(bf16[512]{0:T(512)(128)(2,1)S(1)} %reshape.185, s32[1024]{0:T(1024)S(1)} %get-tuple-element.112), kind=kCustom, calls=%fused_computation | custom fusion | bytes 8192 | tf_op jit(solution)/shard_map/gather | solution.py:76
  40.7 0.6 copy.21
  41.3 3.3 all-to-all-start
  44.6 0.0 all-gather.6.cloned.1.call-done
  44.7 15.5 %gather_fusion.2 = bf16[1024,3584]{1,0:T(8,128)(2,1)} fusion(bf16[256,3584]{1,0:T(8,128)(2,1)} %all-gather.6.cloned.1.call-done, s32[1024]{0:T(1024)S(1)} %get-tuple-element.113), kind=kCustom, calls=%fused_computation.2 | custom fusion | bytes 14684160 | tf_op jit(solution)/shard_map/gather | solution.py:82
  60.2 0.0 all-gather.4.cloned.1.call-done
  60.2 15.5 %gather_fusion.1 = bf16[1024,3584]{1,0:T(8,128)(2,1)} fusion(bf16[256,3584]{1,0:T(8,128)(2,1)} %all-gather.4.cloned.1.call-done, s32[1024]{0:T(1024)S(1)} %get-tuple-element.113), kind=kCustom, calls=%fused_computation.1 | custom fusion | bytes 14684160 | tf_op jit(solution)/shard_map/gather | solution.py:83
  75.7 10.5 %broadcast_select_fusion.3 = (bf16[8,128,3584]{2,1,0:T(8,128)(2,1)}, bf16[8,128,3584]{2,1,0:T(8,128)(2,1)}) fusion(bf16[8,128,3584]{2,1,0:T(8,128)(2,1)} %bitcast.55, pred[8,128]{1,0:T(8,128)(4,1)S(1)} %bitcast.68, bf16[8,128,3584]{2,1,0:T(8,128)(2,1)} %bitcast.54), kind=kLoop, calls=%fused_computation.13 | loop fusion | flops 7340032 | bytes 29361152 | tf_op jit(solution)/shard_map/jit(_where)/select_n | solution.py:83
  86.3 0.0 all-to-all-done
  86.3 163.7 %all_to_all.30 = bf16[8,128,3584]{2,1,0:T(8,128)(2,1)} all-to-all(bf16[8,128,3584]{2,1,0:T(8,128)(2,1)} %get-tuple-element.115), channel_id=1, replica_groups=mesh['exp'=8,'tp'=4] {'exp'}, dimensions={0} | all-to-all | bytes 14680064 | tf_op jit(solution)/shard_map/all_to_all | solution.py:85
  249.9 4.8 all-to-all-start.1
  254.8 0.2 reduce-scatter.4.cloned.1.call-start
  255.0 8.3 %fusion.4 = f32[1024,608]{0,1:T(8,128)S(1)} fusion(bf16[1024,3584]{1,0:T(8,128)(2,1)} %bitcast.57, bf16[1,3584,608]{1,2,0:T(8,128)(2,1)} %param.10), kind=kOutput, calls=%fused_computation.19 | convolution fusion | flops 4462739456 | bytes 14188544 | tf_op jit(solution)/shard_map/dot_general | solution.py:32
  263.3 0.0 copy-start.1
  263.3 150.3 %all-to-all-done.1 = bf16[8,128,3584]{2,1,0:T(8,128)(2,1)} async-done(((bf16[8,128,3584]{2,1,0:T(8,128)(2,1)}), bf16[8,128,3584]{2,1,0:T(8,128)(2,1)}, u32[]{:S(2)}, u32[]{:S(2)}) %all-to-all-start.1) | async-done | bytes 7340064 | tf_op jit(solution)/shard_map/all_to_all | solution.py:86
  413.6 5.3 multiply_convert_fusion
  418.9 0.0 copy-done.1
  418.9 7.3 %multiply_convert_fusion.2 = bf16[1024,608]{0,1:T(8,128)(2,1)S(1)} fusion(f32[1024,608]{0,1:T(8,128)S(1)} %fusion.4, bf16[1024,3584]{1,0:T(8,128)(2,1)S(1)} %bitcast.61, bf16[1,608,3584]{2,1,0:T(8,128)(2,1)} %param.11), kind=kOutput, calls=%fused_computation.24 | convolution fusion | flops 4468342784 | bytes 15433728 | tf_op jit(solution)/shard_map/dot_general | solution.py:35
  426.2 0.0 copy-start
  426.2 1.0 copy-done
  427.2 10.2 %convolution_convert_fusion = bf16[1024,3584]{1,0:T(8,128)(2,1)} fusion(bf16[1024,608]{0,1:T(8,128)(2,1)S(1)} %multiply_convert_fusion.2, bf16[1,3584,608]{1,2,0:T(8,128)(2,1)} %param.10), kind=kOutput, calls=%fused_computation.11 | convolution fusion | flops 4466409472 | bytes 12943360 | tf_op jit(solution)/shard_map/dot_general | solution.py:45
  437.5 10.4 %copy.22 = bf16[1024,3584]{0,1:T(8,128)(2,1)} copy(bf16[1024,3584]{1,0:T(8,128)(2,1)} %convolution_convert_fusion) | data formatting | bytes 14680064
  447.9 0.0 reduce-scatter.4.cloned.1.call-update
  448.0 0.2 lt.74
  448.1 9.4 %fusion = bf16[1024,3584]{1,0:T(8,128)(2,1)} fusion(f32[1024]{0:T(1024)S(1)} %bitcast.64, bf16[8,128,3584]{2,1,0:T(8,128)(2,1)} %all-to-all-done.1), kind=kLoop, calls=%fused_computation.9 | loop fusion | flops 11010048 | bytes 14684160 | tf_op jit(solution)/shard_map/convert_element_type | solution.py:29
  457.6 55.1 %reduce-scatter.4.cloned.1.call-done = bf16[896,1024]{1,0:T(8,128)(2,1)} async-done(((bf16[3584,1024]{1,0:T(8,128)(2,1)}), bf16[896,1024]{1,0:T(8,128)(2,1)}) %reduce-scatter.4.cloned.1.call-update) | async-done | bytes 1835024
  512.7 3.8 copy.23
  516.5 0.0 slice-start
  516.5 5.8 all-to-all-start.3
  522.3 0.0 slice-start.1
  522.3 0.0 copy-start.2
  522.3 10.3 %fusion.2 = bf16[1,3584,608]{1,2,0:T(8,128)(2,1)} fusion(bf16[1024,608]{0,1:T(8,128)(2,1)} %copy-done, bf16[1024,3584]{1,0:T(8,128)(2,1)} %bitcast.58), kind=kOutput, calls=%fused_computation.17 | convolution fusion | flops 4464918528 | bytes 12943360 | tf_op jit(solution)/shard_map/dot_general | solution.py:39
  532.6 0.0 slice-done
  532.6 0.0 slice-done.1
  532.6 0.0 copy-done.2
  532.6 6.9 %fusion.1 = bf16[1,608,3584]{2,1,0:T(8,128)(2,1)} fusion(bf16[1024,3584]{1,0:T(8,128)(2,1)S(1)} %bitcast.60, f32[1024,608]{0,1:T(8,128)S(1)} %copy-done.2), kind=kOutput, calls=%fused_computation.16 | convolution fusion | flops 4468031488 | bytes 14188544 | tf_op jit(solution)/shard_map/dot_general | solution.py:42
  539.5 25.5 %all-to-all-done.3 = bf16[8,128,896]{2,1,0:T(8,128)(2,1)} async-done(((bf16[8,128,896]{2,1,0:T(8,128)(2,1)}), bf16[8,128,896]{2,1,0:T(8,128)(2,1)}, u32[]{:S(2)}, u32[]{:S(2)}) %all-to-all-start.3) | async-done | bytes 1835040 | tf_op jit(solution)/shard_map/all_to_all | solution.py:105
  565.0 3.5 bitcast_convert_fusion
  568.5 4.7 gather_fusion.3
  573.2 2.3 gather.24
  575.5 4.6 select_reduce_fusion
  (22 shorter events, 0.2 us)
Async XLA Ops:
  7.2 37.5 %all-gather.6.cloned.1.call-start = ((), (), s32[]{:S(2)}) async-start(), calls=%async_computation.6 | async-start | bytes 2293760 | tf_op jit(solution)/shard_map/all_gather | solution.py:79
  7.9 52.3 %all-gather.4.cloned.1.call-start = ((), (), s32[]{:S(2)}) async-start(), calls=%async_computation.5 | async-start | bytes 2293760 | tf_op jit(solution)/shard_map/all_gather | solution.py:80
  41.3 44.9 %all-to-all-start = ((bf16[8,128,1]{1,2,0:T(2,128)(2,1)}), bf16[8,128,1]{1,2,0:T(2,128)(2,1)S(1)}, u32[]{:S(2)}, u32[]{:S(2)}) async-start(bf16[8,128,1]{1,2,0:T(2,128)(2,1)} %copy.21), calls=%async_computation | async-start | bytes 8192 | tf_op jit(solution)/shard_map/all_to_all | solution.py:87
  249.9 163.7 %all-to-all-start.1 = ((bf16[8,128,3584]{2,1,0:T(8,128)(2,1)}), bf16[8,128,3584]{2,1,0:T(8,128)(2,1)}, u32[]{:S(2)}, u32[]{:S(2)}) async-start(bf16[8,128,3584]{2,1,0:T(8,128)(2,1)} %get-tuple-element.114), calls=%async_computation.1 | async-start | bytes 14680064 | tf_op jit(solution)/shard_map/all_to_all | solution.py:86
  254.8 257.9 %reduce-scatter.4.cloned.1.call-start = ((), (), s32[]{:S(2)}) async-start(), calls=%async_computation.7 | async-start | bytes 9175040
  263.3 155.6 %copy-start.1 = (f32[1024,608]{0,1:T(8,128)}, f32[1024,608]{0,1:T(8,128)S(1)}, u32[]{:S(2)}) copy-start(f32[1024,608]{0,1:T(8,128)S(1)} %fusion.4) | copy-start | bytes 7471108
  426.2 1.0 copy-start
  516.5 16.1 %slice-start = ((s8[7340032]{0:T(1024)(128)(4,1)}), s8[3145728]{0:T(1024)(128)(4,1)S(1)}, s32[]{:S(2)}) async-start(s8[7340032]{0:T(1024)(128)(4,1)} %bitcast.59), calls=%async_computation.8 | async-start | bytes 6291456
  516.5 48.5 %all-to-all-start.3 = ((bf16[8,128,896]{2,1,0:T(8,128)(2,1)}), bf16[8,128,896]{2,1,0:T(8,128)(2,1)}, u32[]{:S(2)}, u32[]{:S(2)}) async-start(bf16[8,128,896]{2,1,0:T(8,128)(2,1)} %bitcast.15), calls=%async_computation.3 | async-start | bytes 3670016 | tf_op jit(solution)/shard_map/all_to_all | solution.py:105
  522.3 10.4 %slice-start.1 = ((s8[7340032]{0:T(1024)(128)(4,1)}), s8[4194304]{0:T(1024)(128)(4,1)S(1)}, s32[]{:S(2)}) async-start(s8[7340032]{0:T(1024)(128)(4,1)} %bitcast.59), calls=%async_computation.9 | async-start | bytes 8388608
  522.3 10.4 %copy-start.2 = (f32[1024,608]{0,1:T(8,128)S(1)}, f32[1024,608]{0,1:T(8,128)}, u32[]{:S(2)}) copy-start(f32[1024,608]{0,1:T(8,128)} %copy-done.1) | copy-start | bytes 7471108
Sparse Core Ops, SparseCore 0:
  9.6 23.8 all-gather.5
  35.0 21.1 all-gather.3
  448.1 64.5 reduce-scatter.3
where the time goes:
time: 588 us; the launch traced here: 587 us
  waiting for transfers between devices  232 us (39%)
  blocking collectives  177 us (30%)
  local copies, waits for them, and re-layouts  69.9 us (12%)
  matrix products  43.1 us (7%)
  other arithmetic  35.6 us (6%)
  between operations  14.7 us (2%)
  starting transfers between devices  14.2 us (2%)
    all_to_all x1, blocking collectives, per_device(): lax.all_to_all(send_x, 'exp', split_axis=0, concat_axis=0, tiled=True)  164 us
    all_to_all x1, waiting for transfers between devices, per_device(): lax.all_to_all(send_dy, 'exp', split_axis=0, concat_axis=0, tiled=True)  150 us
    unnamed x4, waiting for transfers between devices  56.5 us
    all_to_all x1, waiting for transfers between devices, per_device(): lax.all_to_all(summed.astype(jnp.bfloat16), 'exp', split_axis=0, concat_a...  25.5 us
    unnamed x17, local copies, waits for them, and re-layouts  18.4 us
    gather x1, local copies, waits for them, and re-layouts, per_device(): full_tokens[token_rows]  15.5 us
    gather x1, local copies, waits for them, and re-layouts, per_device(): full_cotan[token_rows]  15.5 us
    convert_element_type x2, other arithmetic, expert_terms(): (probs_rows.astype(jnp.float32)[:, None] * cotan_rows.astype(jnp.float32)...  14.7 us
  transfers between devices with their start and end apart: 6, of which 3 were waited for; matrix products, arithmetic and copies ran while one was open for 16% of the time, Pallas kernels for 0%

commit v1 on v0

v1 whole, which is shorter than its diff:
```python
import math

import jax
import jax.numpy as jnp
from jax import lax
from jax.sharding import PartitionSpec as P

BF = jnp.bfloat16
F32 = jnp.float32


def ring_order(count):
    if count <= 4:
        return list(range(0, count, 2)) + list(range(1, count, 2))[::-1]
    return list(range(count))


class Ring:
    def __init__(self, axis, size, count, stride):
        self.axis, self.count, self.stride = axis, count, stride
        self.order = ring_order(count)
        self.half = count // 2
        spot = {c: i for i, c in enumerate(self.order)}
        self.perms = {}
        for step in (1, -1):
            pairs = []
            for index in range(size):
                c = (index // stride) % count
                there = self.order[(spot[c] + step) % count]
                pairs.append((index, index + (there - c) * stride))
            self.perms[step] = pairs
        self.spot = [spot[c] for c in range(count)]

    def send(self, value, step):
        return lax.ppermute(value, self.axis, self.perms[step])

    def coordinate(self, mine, offset):
        place = jnp.asarray(self.spot, jnp.int32)[mine]
        return jnp.asarray(self.order, jnp.int32)[(place + offset) % self.count]

    def offsets(self):
        found = [0]
        for d in range(1, self.half):
            found += [-d, d]
        return found + ([self.half] if self.count > 1 else [])

    def gather(self, value, cut):
        blocks = {0: value}
        if self.count == 2:
            blocks[1] = self.send(value, 1)
        elif self.count > 2:
            up = down = value
            for d in range(1, self.half):
                up, down = self.send(up, 1), self.send(down, -1)
                blocks[-d], blocks[d] = up, down
            blocks[self.half] = jnp.concatenate(
                [self.send(up[:cut], 1), self.send(down[cut:], -1)], axis=0
            )
        return [blocks[o] for o in self.offsets()]

    def reduce(self, blocks, cut):
        term = dict(zip(self.offsets(), blocks))
        if self.count == 1:
            return term[0]
        if self.count == 2:
            return term[0] + self.send(term[1].astype(BF), 1).astype(F32)
        up = self.send(term[self.half][:cut].astype(BF), 1).astype(F32)
        down = self.send(term[self.half][cut:].astype(BF), -1).astype(F32)
        for d in range(self.half - 1, 0, -1):
            up_sum, down_sum = term[d], term[-d]
            if d == self.half - 1:
                up_sum = jnp.concatenate([up_sum[:cut] + up, up_sum[cut:]], axis=0)
                down_sum = jnp.concatenate([down_sum[:cut], down_sum[cut:] + down], axis=0)
            else:
                up_sum, down_sum = up_sum + up, down_sum + down
            up = self.send(up_sum.astype(BF), 1).astype(F32)
            down = self.send(down_sum.astype(BF), -1).astype(F32)
        return term[0] + up + down


def pick(onehot, rows):
    return jnp.dot(onehot, rows, preferred_element_type=F32).astype(BF)


def unpick(onehot, rows):
    return lax.dot_general(onehot, rows, (((0,), (0,)), ((), ())), preferred_element_type=F32)


def silu_parts(hidden):
    sigma = jax.nn.sigmoid(hidden)
    return (hidden * sigma, sigma * (1.0 + hidden * (1.0 - sigma)))


def after(value, *others):
    return lax.optimization_barrier((value,) + others)[0]


def per_device(tokens, cotangent, up_weight, down_weight, expert_ids, gate_probs):
    tok, top = expert_ids.shape
    width = tokens.shape[1]
    n_exp, n_tp = lax.axis_size("exp"), lax.axis_size("tp")
    experts = n_exp * up_weight.shape[0]
    slot = min(4 * tok // experts, tok)
    capacity = 5 * tok * n_exp // (2 * experts)
    nx = 2 ** (int(math.log2(n_exp)) // 2)
    nz = n_exp // nx
    nc = 2 if n_tp % 2 == 0 else 1
    ny = n_tp // nc
    zring, yring, cring = (
        Ring("exp", n_exp, nz, nx),
        Ring("tp", n_tp, ny, nc),
        Ring("tp", n_tp, nc, 1),
    )
    e, t = lax.axis_index("exp"), lax.axis_index("tp")
    z, x, y, c = e // nx, e % nx, t // nc, t % nc

    def cross(value, dx):
        pairs = [(i, i // nx * nx + (i % nx + dx) % nx) for i in range(n_exp)]
        return lax.ppermute(value, "exp", pairs)

    w_up, w_down = up_weight[0], down_weight[0]
    hid = w_up.shape[1]
    first = min(-(-width // 256) * 128, width)
    edges = [(0, first), (first, width)] if first < width else [(0, width)]

    head = 16
    meta = jnp.concatenate([expert_ids.astype(BF).T, gate_probs.T], axis=0)
    meta = jnp.pad(meta, ((0, head - 2 * top), (0, edges[0][1] - tok)))

    cuts = [tok // 2] * 4
    pieces = []
    held = {}
    for source, name in ((tokens, "x"), (cotangent, "dy")):
        for k, (lo, hi) in enumerate(edges):
            pieces.append((name, k, source[:, lo:hi]))
    previous = None
    for name, k, piece in pieces:
        if name == "x" and k == 0:
            piece = jnp.concatenate([meta, piece], axis=0)
            blocks = zring.gather(piece, head + tok // 2)
            info = [b[:head, :tok] for b in blocks]
            blocks = [b[head:] for b in blocks]
        else:
            if previous is not None:
                piece = after(piece, previous)
            blocks = zring.gather(piece, tok // 2)
        previous = blocks[min(1, len(blocks) - 1)]
        held[name, k] = jnp.concatenate(blocks, axis=0)

    info = jnp.stack(info, axis=0)
    ids, probs = info[:, :top], info[:, top : 2 * top]
    rows = jnp.arange(nx, dtype=jnp.int32)
    wanted = (z * nx + (x + rows) % nx).astype(BF)
    hit = ids[None] == wanted[:, None, None, None]
    match = jnp.any(hit, axis=2)
    weight = jnp.sum(jnp.where(hit, probs[None], jnp.zeros_like(probs[None])), axis=2)
    spot = jnp.arange(tok)
    below = (spot[:, None] < spot[None, :]).astype(BF)
    local = jnp.dot(
        match.astype(BF).reshape(nx * nz, tok), below, preferred_element_type=F32
    ).astype(jnp.int32)
    local = jnp.where(match, local.reshape(nx, nz, tok), -1)
    count = jnp.sum(match.astype(F32), axis=2)

    rank_of_slot = jnp.arange(slot, dtype=jnp.int32)[:, None]
    pick_out, pick_out_w = [], []
    for dx in range(1, nx):
        onehot = local[dx][:, None, :] == rank_of_slot[None]
        pick_out.append(onehot.astype(BF))
        pick_out_w.append(jnp.where(onehot, weight[dx][:, None, :], jnp.zeros((), BF)))

    def slots(onehot, rows):
        rows = rows.reshape(nz, tok, -1)
        out = lax.dot_general(
            onehot, rows, (((2,), (1,)), ((0,), (0,))), preferred_element_type=F32
        )
        return out.astype(BF).reshape(nz * slot, -1)

    arrived = {}
    others = [count[0]]
    for name, k, _ in pieces:
        got = []
        for dx in range(1, nx):
            out = slots((pick_out if name == "x" else pick_out_w)[dx - 1], held[name, k])
            if name == "x" and k == 0:
                line = jnp.pad(count[dx][None].astype(BF), ((0, head - 1), (0, out.shape[1] - nz)))
                back = cross(jnp.concatenate([line, out], axis=0), dx)
                others.append(back[0, :nz].astype(F32))
                back = back[head:]
            else:
                back = cross(out, dx)
            got.append(back)
        arrived[name, k] = got

    zs = zring.coordinate(z, jnp.asarray(zring.offsets(), jnp.int32))
    number = jnp.stack([zs * nx + (x - dx) % nx for dx in range(nx)], axis=0)
    counts = jnp.stack(others, axis=0)
    earlier = number.reshape(-1)[None, :] < number.reshape(-1)[:, None]
    base = jnp.sum(jnp.where(earlier, counts.reshape(-1)[None, :], 0.0), axis=1)
    base = base.astype(jnp.int32).reshape(nx, nz)
    counts = counts.astype(jnp.int32)
    place = jnp.arange(capacity, dtype=jnp.int32)[:, None]
    rank = jnp.where(match[0], local[0] + base[0][:, None], -1).reshape(1, nz * tok)
    own = rank == place
    pick_own = own.astype(BF)
    pick_own_w = jnp.where(own, weight[0].reshape(1, nz * tok), jnp.zeros((), BF))
    lane = jnp.arange(slot, dtype=jnp.int32)[None, :]
    pick_in = []
    for dx in range(1, nx):
        there = jnp.where(lane < counts[dx][:, None], base[dx][:, None] + lane, -1)
        pick_in.append((there.reshape(1, nz * slot) == place).astype(BF))

    full = {}
    for name in ("x", "dy"):
        whole = jnp.zeros((capacity, n_tp * width), BF)
        for k, (lo, hi) in enumerate(edges):
            part = pick(pick_own if name == "x" else pick_own_w, held[name, k])
            for onehot, back in zip(pick_in, arrived[name, k]):
                part = part + pick(onehot, back)
            for oy, by_y in zip(yring.offsets(), yring.gather(part, capacity // 2)):
                for oc, by_c in zip(cring.offsets(), cring.gather(by_y, capacity // 2)):
                    index = yring.coordinate(y, oy) * nc + cring.coordinate(c, oc)
                    whole = lax.dynamic_update_slice(whole, by_c, (0, index * width + lo))
        full[name] = whole

    inputs, routed = full["x"], full["dy"]
    hidden = jnp.dot(inputs, w_up, preferred_element_type=F32)
    act_full, slope = silu_parts(hidden)
    act = act_full.astype(BF)
    d_act = lax.dot_general(routed, w_down, (((1,), (1,)), ((), ())), preferred_element_type=F32)
    d_hidden = (d_act * slope).astype(BF)
    grad_up = unpick(inputs, d_hidden).astype(BF)
    grad_down = unpick(act, routed).astype(BF)

    results = []
    for lo, hi in edges:
        by_y = []
        for oy in yring.offsets():
            by_c = []
            for oc in cring.offsets():
                index = yring.coordinate(y, oy) * nc + cring.coordinate(c, oc)
                part = lax.dynamic_slice(w_up, (index * width + lo, 0), (hi - lo, hid))
                by_c.append(
                    lax.dot_general(
                        d_hidden, part, (((1,), (1,)), ((), ())), preferred_element_type=F32
                    )
                )
            by_y.append(cring.reduce(by_c, capacity // 2))
        total = yring.reduce(by_y, capacity // 2).astype(BF)
        mine = unpick(pick_own, total).reshape(nz, tok, hi - lo)
        for dx in range(1, nx):
            out = unpick(pick_in[dx - 1], total).astype(BF)
            back = cross(out, -dx).reshape(nz, slot, hi - lo)
            mine = mine + lax.dot_general(
                pick_out[dx - 1], back, (((1,), (1,)), ((0,), (0,))), preferred_element_type=F32
            )
        results.append(zring.reduce([mine[i] for i in range(nz)], tok // 2).astype(BF))
    token_grad = jnp.concatenate(results, axis=1)
    return (token_grad, grad_up[None], grad_down[None])


def solution(mesh):
    placed = (
        P("exp", "tp"),
        P("exp", "tp"),
        P("exp", None, "tp"),
        P("exp", "tp", None),
        P("exp", None),
        P("exp", None),
    )
    return jax.shard_map(
        per_device,
        mesh=mesh,
        in_specs=placed,
        out_specs=(P("exp", "tp"), P("exp", None, "tp"), P("exp", "tp", None)),
        check_vma=False,
    )
```

time: 588 us -> 246 us (0.42)
  blocking collectives: 177 us -> 0 us
  waiting for transfers between devices: 232 us -> 115 us
  local copies, waits for them, and re-layouts: 69.9 us -> 24.9 us
  starting transfers between devices: 14.2 us -> 45.7 us
  other arithmetic: 35.6 us -> 9.01 us
  between operations: 14.7 us -> 1.41 us
  matrix products: 43.1 us -> 49.8 us
    all_to_all x3 -> x0, waiting for transfers between devices: 176 us -> none  [the longest x1 150 us: per_device(): lax.all_to_all(send_dy, 'exp', split_axis=0, concat_axis=0, tiled=True)]
    all_to_all x1 -> x0, blocking collectives: 164 us -> none  [per_device(): lax.all_to_all(send_x, 'exp', split_axis=0, concat_axis=0, tiled=True)]
    ppermute x0 -> x48, waiting for transfers between devices: none -> 115 us  [the longest x42 112 us: send(): return lax.ppermute(value, self.axis, self.perms[step])]
    unnamed x4 -> x0, waiting for transfers between devices: 56.5 us -> none
    ppermute x0 -> x48, starting transfers between devices: none -> 45.7 us  [the longest x42 37.5 us: send(): return lax.ppermute(value, self.axis, self.perms[step])]
    gather x5 -> x1, local copies, waits for them, and re-layouts: 44.8 us -> 1.3 us  [coordinate(): return jnp.asarray(self.order, jnp.int32)[(place + offset) % self.count]]
    convert_element_type x5 -> x8, other arithmetic: 18.3 us -> 1.35 us  [the longest x1 0.66 us: per_device(): others.append(back[0, :nz].astype(F32))]
    all_to_all x3 -> x0, starting transfers between devices: 13.9 us -> none  [the longest x1 5.76 us: per_device(): lax.all_to_all(summed.astype(jnp.bfloat16), 'exp', split_axis=0, concat_a...]
  transfers between devices with their start and end apart: 6 -> 48, of which waited for: 3 -> 23; matrix products, arithmetic and copies ran while one was open for 16% -> 25% of each run, Pallas kernels for 0% -> 0%
where the time goes in v1:
time: 246 us; the launch traced here: 245 us
  waiting for transfers between devices  115 us (47%)
  matrix products  49.8 us (20%)
  starting transfers between devices  45.7 us (19%)
  local copies, waits for them, and re-layouts  24.9 us (10%)
  other arithmetic  9.01 us (4%)
    ppermute x42, waiting for transfers between devices, send(): return lax.ppermute(value, self.axis, self.perms[step])  112 us
    ppermute x42, starting transfers between devices, send(): return lax.ppermute(value, self.axis, self.perms[step])  37.5 us
    dot_general x6, matrix products, unpick(): lax.dot_general(onehot, rows, (((0,), (0,)), ((), ())), preferred_element...  15.9 us
    dot_general x8, matrix products, pick(): return jnp.dot(onehot, rows, preferred_element_type=F32).astype(BF)  10.3 us
    dynamic_update_slice x12, local copies, waits for them, and re-layouts, per_device(): whole = lax.dynamic_update_slice(whole, by_c, (0, index * width + lo))  8.3 us
    ppermute x6, starting transfers between devices, cross(): return lax.ppermute(value, 'exp', pairs)  8.2 us
    dot_general x1, matrix products, per_device(): hidden = jnp.dot(inputs, w_up, preferred_element_type=F32)  6.78 us
    dot_general x1, matrix products, per_device(): lax.dot_general(routed, w_down, (((1,), (1,)), ((), ())), preferred_eleme...  6.14 us
  transfers between devices with their start and end apart: 48, of which 23 were waited for; matrix products, arithmetic and copies ran while one was open for 25% of the time, Pallas kernels for 0%

profile of v1, /device:TPU:0, one launch (start us, length us, event | category | flops | bytes accessed | tf_op | source)
XLA Modules:
  0.0 245.5 jit_solution(5200923475787086425)
XLA Ops:
  0.6 1.0 slice.199
  3.0 4.1 %collective-permute-start = (bf16[272,512]{1,0:T(8,128)(2,1)S(1)}, bf16[272,512]{1,0:T(8,128)(2,1)S(1)}, u32[]{:S(2)}, u32[]{:S(2)}) collective-permute-start(bf16[272,512]{1,0:T(8,128)(2,1)S(1)} %pad_maximum_fusion.1), channel_id=1, source_target_pairs={{0,16},{4,20},{8,0},{12,4},{16,24},{20,28},{24,8},{28,12},{1,17},{... | collective-permute-start | bytes 835592 | tf_op jit(solution)/shard_map/ppermute | solution.py:35
  7.1 1.2 dynamic_slice.331
  8.3 1.3 compare_select_fusion.1
  9.7 1.3 gather_fusion
  12.1 1.0 slice.218
  13.0 1.0 slice.225
  14.7 3.0 %collective-permute-start.5 = (bf16[256,384]{1,0:T(8,128)(2,1)S(1)}, bf16[256,384]{1,0:T(8,128)(2,1)S(1)}, u32[]{:S(2)}, u32[]{:S(2)}) collective-permute-start(bf16[256,384]{1,0:T(8,128)(2,1)S(1)} %slice.219), channel_id=1, source_target_pairs={{0,16},{4,20},{8,0},{12,4},{16,24},{20,28},{24,8},{28,12},{1,17},{... | collective-permute-start | bytes 589832 | tf_op jit(solution)/shard_map/ppermute | solution.py:35
  17.7 3.0 %collective-permute-start.2 = (bf16[144,512]{1,0:T(8,128)(2,1)S(1)}, bf16[144,512]{1,0:T(8,128)(2,1)S(1)}, u32[]{:S(2)}, u32[]{:S(2)}) collective-permute-start(bf16[144,512]{1,0:T(8,128)(2,1)S(1)} %slice.258), channel_id=1, source_target_pairs={{0,16},{4,20},{8,0},{12,4},{16,24},{20,28},{24,8},{28,12},{1,17},{... | collective-permute-start | bytes 442376 | tf_op jit(solution)/shard_map/ppermute | solution.py:35
  20.6 1.4 collective-permute-done.1
  22.8 10.7 %collective-permute-done.2 = bf16[144,512]{1,0:T(8,128)(2,1)S(1)} collective-permute-done((bf16[144,512]{1,0:T(8,128)(2,1)S(1)}, bf16[144,512]{1,0:T(8,128)(2,1)S(1)}, u32[]{:S(2)}, u32[]{:S(2)}) %collective-permute-start.2) | collective-permute-done | bytes 147488 | tf_op jit(solution)/shard_map/ppermute | solution.py:35
  34.1 1.3 collective-permute-done.3
  35.4 1.0 fusion.50
  38.0 1.5 collective-permute-start.4
  40.6 1.5 collective-permute-start.7
  42.1 1.5 collective-permute-start.26
  45.2 1.0 constant_dynamic-update-slice_fusion.13
  46.1 1.0 constant_dynamic-update-slice_fusion.12
  47.1 9.3 %collective-permute-done.26 = bf16[128,384]{1,0:T(8,128)(2,1)S(1)} collective-permute-done((bf16[128,384]{1,0:T(8,128)(2,1)S(1)}, bf16[128,384]{1,0:T(8,128)(2,1)S(1)}, u32[]{:S(2)}, u32[]{:S(2)}) %collective-permute-start.26) | collective-permute-done | bytes 98336 | tf_op jit(solution)/shard_map/ppermute | solution.py:35
  56.4 2.2 collective-permute-done.27
  58.6 1.3 convolution_convert_fusion.10
  61.1 1.5 collective-permute-start.9
  62.7 1.5 collective-permute-start.14
  64.2 5.5 %collective-permute-done.8 = bf16[128,512]{1,0:T(8,128)(2,1)S(1)} collective-permute-done((bf16[128,512]{1,0:T(8,128)(2,1)S(1)}, bf16[128,512]{1,0:T(8,128)(2,1)S(1)}, u32[]{:S(2)}, u32[]{:S(2)}) %collective-permute-start.8) | collective-permute-done | bytes 131104 | tf_op jit(solution)/shard_map/ppermute | solution.py:35
  69.7 1.2 collective-permute-done.9
  70.9 1.5 convolution_convert_fusion.6
  72.4 1.5 collective-permute-start.10
  73.9 2.4 collective-permute-done.14
  77.6 1.6 collective-permute-start.17
  82.1 1.6 convolution_convert_fusion.4
  84.9 1.6 collective-permute-start.23
  88.1 1.5 collective-permute-start.18
  89.7 1.6 convolution_convert_fusion.5
  91.2 2.4 broadcast.169.clone.1
  93.7 1.7 constant_dynamic-update-slice_fusion.30
  95.9 1.5 fusion.38
  97.5 5.1 %collective-permute-done.23 = bf16[640,512]{1,0:T(8,128)(2,1)S(1)} collective-permute-done((bf16[640,512]{1,0:T(8,128)(2,1)S(1)}, bf16[640,512]{1,0:T(8,128)(2,1)S(1)}, u32[]{:S(2)}, u32[]{:S(2)}) %collective-permute-start.23) | collective-permute-done | bytes 655392 | tf_op jit(solution)/shard_map/ppermute | solution.py:35
  103.2 12.9 %collective-permute-done.12 = bf16[640,512]{1,0:T(8,128)(2,1)S(1)} collective-permute-done((bf16[640,512]{1,0:T(8,128)(2,1)S(1)}, bf16[640,512]{1,0:T(8,128)(2,1)S(1)}, u32[]{:S(2)}, u32[]{:S(2)}) %collective-permute-start.12) | collective-permute-done | bytes 655392 | tf_op jit(solution)/shard_map/ppermute | solution.py:35
  119.5 1.6 collective-permute-start.30
  122.0 1.7 constant_dynamic-update-slice_fusion.29
  124.6 9.1 %collective-permute-done.30 = bf16[640,384]{1,0:T(8,128)(2,1)S(1)} collective-permute-done((bf16[640,384]{1,0:T(8,128)(2,1)S(1)}, bf16[640,384]{1,0:T(8,128)(2,1)S(1)}, u32[]{:S(2)}, u32[]{:S(2)}) %collective-permute-start.30) | collective-permute-done | bytes 491552 | tf_op jit(solution)/shard_map/ppermute | solution.py:35
  135.4 7.8 %collective-permute-done.20 = bf16[640,384]{1,0:T(8,128)(2,1)S(1)} collective-permute-done((bf16[640,384]{1,0:T(8,128)(2,1)S(1)}, bf16[640,384]{1,0:T(8,128)(2,1)S(1)}, u32[]{:S(2)}, u32[]{:S(2)}) %collective-permute-start.20) | collective-permute-done | bytes 491552 | tf_op jit(solution)/shard_map/ppermute | solution.py:35
  145.9 6.8 %fusion.2 = f32[640,608]{0,1:T(8,128)S(1)} fusion(bf16[640,3584]{1,0:T(8,128)(2,1)} %constant_dynamic-update-slice_fusion.25, bf16[1,3584,608]{1,2,0:T(8,128)(2,1)} %param.107), kind=kOutput, calls=%fused_computation.5 | convolution fusion | flops 2789212160 | bytes 10502144 | tf_op jit(solution)/shard_map/dot_general | solution.py:227
  153.6 7.5 %fusion = bf16[1,608,3584]{2,1,0:T(8,128)(2,1)} fusion(bf16[640,3584]{1,0:T(8,128)(2,1)} %constant_dynamic-update-slice_fusion.17, f32[640,608]{0,1:T(8,128)S(1)} %fusion.2), kind=kOutput, calls=%fused_computation.3 | convolution fusion | flops 2793336832 | bytes 10502144 | tf_op jit(solution)/shard_map/dot_general | solution.py:86
  161.1 6.1 %multiply_convert_fusion.1 = bf16[640,608]{0,1:T(8,128)(2,1)S(1)} fusion(f32[640,608]{0,1:T(8,128)S(1)} %fusion.2, bf16[640,3584]{1,0:T(8,128)(2,1)} %constant_dynamic-update-slice_fusion.17, bf16[1,608,3584]{2,1,0:T(8,128)(2,1)S(1)} %bitcast.191), kind=kOutput, calls=%fused_computation.20 | convolution fusion | flops 2792714240 | bytes 11280384 | tf_op jit(solution)/shard_map/dot_general | solution.py:230
  173.2 1.5 collective-permute-start.42
  176.8 10.5 %collective-permute-done.42 = bf16[640,384]{1,0:T(8,128)(2,1)S(1)} collective-permute-done((bf16[640,384]{1,0:T(8,128)(2,1)S(1)}, bf16[640,384]{1,0:T(8,128)(2,1)S(1)}, u32[]{:S(2)}, u32[]{:S(2)}) %collective-permute-start.42) | collective-permute-done | bytes 491552 | tf_op jit(solution)/shard_map/ppermute | solution.py:35
  188.1 1.6 collective-permute-start.43
  189.7 1.0 fusion.6
  190.7 10.0 %collective-permute-done.34 = bf16[640,512]{1,0:T(8,128)(2,1)S(1)} collective-permute-done((bf16[640,512]{1,0:T(8,128)(2,1)S(1)}, bf16[640,512]{1,0:T(8,128)(2,1)S(1)}, u32[]{:S(2)}, u32[]{:S(2)}) %collective-permute-start.34) | collective-permute-done | bytes 655392 | tf_op jit(solution)/shard_map/ppermute | solution.py:35
  201.7 1.6 collective-permute-start.35
  204.0 1.6 collective-permute-start.44
  206.1 1.0 fusion.7
  207.1 1.6 collective-permute-done.44
  208.7 3.3 %collective-permute-done.46 = bf16[128,384]{1,0:T(8,128)(2,1)S(1)} collective-permute-done((bf16[128,384]{1,0:T(8,128)(2,1)S(1)}, bf16[128,384]{1,0:T(8,128)(2,1)S(1)}, u32[]{:S(2)}, u32[]{:S(2)}) %collective-permute-start.46) | collective-permute-done | bytes 98336 | tf_op jit(solution)/shard_map/ppermute | solution.py:35
  212.0 3.1 %collective-permute-done.35 = bf16[512,512]{1,0:T(8,128)(2,1)S(1)} collective-permute-done((bf16[512,512]{1,0:T(8,128)(2,1)S(1)}, bf16[512,512]{1,0:T(8,128)(2,1)S(1)}, u32[]{:S(2)}, u32[]{:S(2)}) %collective-permute-start.35) | collective-permute-done | bytes 524320 | tf_op jit(solution)/shard_map/ppermute | solution.py:119
  216.2 1.6 collective-permute-start.36
  218.3 2.5 %collective-permute-start.45 = (bf16[256,384]{1,0:T(8,128)(2,1)S(1)}, bf16[256,384]{1,0:T(8,128)(2,1)S(1)}, u32[]{:S(2)}, u32[]{:S(2)}) collective-permute-start(bf16[256,384]{1,0:T(8,128)(2,1)S(1)} %pad_maximum_fusion.4), channel_id=1, source_target_pairs={{0,16},{4,20},{8,0},{12,4},{16,24},{20,28},{24,8},{28,12},{1,17},{... | collective-permute-start | bytes 589832 | tf_op jit(solution)/shard_map/ppermute | solution.py:35
  220.9 3.2 %collective-permute-done.36 = bf16[128,512]{1,0:T(8,128)(2,1)S(1)} collective-permute-done((bf16[128,512]{1,0:T(8,128)(2,1)S(1)}, bf16[128,512]{1,0:T(8,128)(2,1)S(1)}, u32[]{:S(2)}, u32[]{:S(2)}) %collective-permute-start.36) | collective-permute-done | bytes 131104 | tf_op jit(solution)/shard_map/ppermute | solution.py:35
  224.1 5.3 %collective-permute-done.38 = bf16[128,512]{1,0:T(8,128)(2,1)S(1)} collective-permute-done((bf16[128,512]{1,0:T(8,128)(2,1)S(1)}, bf16[128,512]{1,0:T(8,128)(2,1)S(1)}, u32[]{:S(2)}, u32[]{:S(2)}) %collective-permute-start.38) | collective-permute-done | bytes 131104 | tf_op jit(solution)/shard_map/ppermute | solution.py:35
  229.6 2.1 collective-permute-start.39
  231.7 5.1 %fusion.1 = bf16[1,3584,608]{1,2,0:T(8,128)(2,1)} fusion(bf16[640,608]{0,1:T(8,128)(2,1)S(1)} %multiply_convert_fusion.1, bf16[640,3584]{1,0:T(8,128)(2,1)S(1)} %bitcast.173), kind=kOutput, calls=%fused_computation.4 | convolution fusion | flops 2791391232 | bytes 9723904 | tf_op jit(solution)/shard_map/dot_general | solution.py:86
  236.8 2.4 collective-permute-done.47
  239.3 5.2 %collective-permute-done.39 = bf16[256,512]{1,0:T(8,128)(2,1)S(1)} collective-permute-done((bf16[256,512]{1,0:T(8,128)(2,1)S(1)}, bf16[256,512]{1,0:T(8,128)(2,1)S(1)}, u32[]{:S(2)}, u32[]{:S(2)}) %collective-permute-start.39) | collective-permute-done | bytes 262176 | tf_op jit(solution)/shard_map/ppermute | solution.py:35
  (197 shorter events, 42.3 us)
Async XLA Ops:
  3.0 11.7 %collective-permute-start = (bf16[272,512]{1,0:T(8,128)(2,1)S(1)}, bf16[272,512]{1,0:T(8,128)(2,1)S(1)}, u32[]{:S(2)}, u32[]{:S(2)}) collective-permute-start(bf16[272,512]{1,0:T(8,128)(2,1)S(1)} %pad_maximum_fusion.1), channel_id=1, source_target_pairs={{0,16},{4,20},{8,0},{12,4},{16,24},{20,28},{24,8},{28,12},{1,17},{... | collective-permute-start | bytes 835592 | tf_op jit(solution)/shard_map/ppermute | solution.py:35
  7.1 15.0 %collective-permute-start.1 = (bf16[272,512]{1,0:T(8,128)(2,1)S(1)}, bf16[272,512]{1,0:T(8,128)(2,1)S(1)}, u32[]{:S(2)}, u32[]{:S(2)}) collective-permute-start(bf16[272,512]{1,0:T(8,128)(2,1)S(1)} %pad_maximum_fusion.1), channel_id=1, source_target_pairs={{0,8},{4,12},{8,24},{12,28},{16,0},{20,4},{24,16},{28,20},{1,9},{5... | collective-permute-start | bytes 835592 | tf_op jit(solution)/shard_map/ppermute | solution.py:35
  14.7 25.4 %collective-permute-start.5 = (bf16[256,384]{1,0:T(8,128)(2,1)S(1)}, bf16[256,384]{1,0:T(8,128)(2,1)S(1)}, u32[]{:S(2)}, u32[]{:S(2)}) collective-permute-start(bf16[256,384]{1,0:T(8,128)(2,1)S(1)} %slice.219), channel_id=1, source_target_pairs={{0,16},{4,20},{8,0},{12,4},{16,24},{20,28},{24,8},{28,12},{1,17},{... | collective-permute-start | bytes 589832 | tf_op jit(solution)/shard_map/ppermute | solution.py:35
  17.7 26.0 %collective-permute-start.25 = (bf16[256,384]{1,0:T(8,128)(2,1)S(1)}, bf16[256,384]{1,0:T(8,128)(2,1)}, u32[]{:S(2)}, u32[]{:S(2)}) collective-permute-start(bf16[256,384]{1,0:T(8,128)(2,1)S(1)} %slice.219), channel_id=1, source_target_pairs={{0,8},{4,12},{8,24},{12,28},{16,0},{20,4},{24,16},{28,20},{1,9},{5... | collective-permute-start | bytes 589832 | tf_op jit(solution)/shard_map/ppermute | solution.py:35
  17.7 15.8 %collective-permute-start.2 = (bf16[144,512]{1,0:T(8,128)(2,1)S(1)}, bf16[144,512]{1,0:T(8,128)(2,1)S(1)}, u32[]{:S(2)}, u32[]{:S(2)}) collective-permute-start(bf16[144,512]{1,0:T(8,128)(2,1)S(1)} %slice.258), channel_id=1, source_target_pairs={{0,16},{4,20},{8,0},{12,4},{16,24},{20,28},{24,8},{28,12},{1,17},{... | collective-permute-start | bytes 442376 | tf_op jit(solution)/shard_map/ppermute | solution.py:35
  22.1 13.3 %collective-permute-start.3 = (bf16[128,512]{1,0:T(8,128)(2,1)S(1)}, bf16[128,512]{1,0:T(8,128)(2,1)}, u32[]{:S(2)}, u32[]{:S(2)}) collective-permute-start(bf16[128,512]{1,0:T(8,128)(2,1)S(1)} %slice.265), channel_id=1, source_target_pairs={{0,8},{4,12},{8,24},{12,28},{16,0},{20,4},{24,16},{28,20},{1,9},{5... | collective-permute-start | bytes 393224 | tf_op jit(solution)/shard_map/ppermute | solution.py:35
  33.4 0.7 copy-start.2
  37.1 2.4 copy-start.6
  38.0 42.2 %collective-permute-start.4 = (bf16[528,512]{1,0:T(8,128)(2,1)}, bf16[528,512]{1,0:T(8,128)(2,1)}, u32[]{:S(2)}, u32[]{:S(2)}) collective-permute-start(bf16[528,512]{1,0:T(8,128)(2,1)} %fusion.74), channel_id=1, source_target_pairs={{0,4},{4,0},{8,12},{12,8},{16,20},{20,16},{24,28},{28,24},{1,5},{5... | collective-permute-start | bytes 1622024 | tf_op jit(solution)/shard_map/ppermute | solution.py:119
  40.0 2.0 copy-start.1
  40.0 20.4 %collective-permute-start.6 = (bf16[256,512]{1,0:T(8,128)(2,1)S(1)}, bf16[256,512]{1,0:T(8,128)(2,1)S(1)}, u32[]{:S(2)}, u32[]{:S(2)}) collective-permute-start(bf16[256,512]{1,0:T(8,128)(2,1)S(1)} %slice.218), channel_id=1, source_target_pairs={{0,16},{4,20},{8,0},{12,4},{16,24},{20,28},{24,8},{28,12},{1,17},{... | collective-permute-start | bytes 786440 | tf_op jit(solution)/shard_map/ppermute | solution.py:35
  40.6 20.5 %collective-permute-start.7 = (bf16[256,512]{1,0:T(8,128)(2,1)S(1)}, bf16[256,512]{1,0:T(8,128)(2,1)S(1)}, u32[]{:S(2)}, u32[]{:S(2)}) collective-permute-start(bf16[256,512]{1,0:T(8,128)(2,1)S(1)} %slice.218), channel_id=1, source_target_pairs={{0,8},{4,12},{8,24},{12,28},{16,0},{20,4},{24,16},{28,20},{1,9},{5... | collective-permute-start | bytes 786440 | tf_op jit(solution)/shard_map/ppermute | solution.py:35
  42.1 14.3 %collective-permute-start.26 = (bf16[128,384]{1,0:T(8,128)(2,1)S(1)}, bf16[128,384]{1,0:T(8,128)(2,1)S(1)}, u32[]{:S(2)}, u32[]{:S(2)}) collective-permute-start(bf16[128,384]{1,0:T(8,128)(2,1)S(1)} %slice.274), channel_id=1, source_target_pairs={{0,16},{4,20},{8,0},{12,4},{16,24},{20,28},{24,8},{28,12},{1,17},{... | collective-permute-start | bytes 294920 | tf_op jit(solution)/shard_map/ppermute | solution.py:35
  44.5 14.1 %collective-permute-start.27 = (bf16[128,384]{1,0:T(8,128)(2,1)S(1)}, bf16[128,384]{1,0:T(8,128)(2,1)S(1)}, u32[]{:S(2)}, u32[]{:S(2)}) collective-permute-start(bf16[128,384]{1,0:T(8,128)(2,1)S(1)} %slice.275), channel_id=1, source_target_pairs={{0,8},{4,12},{8,24},{12,28},{16,0},{20,4},{24,16},{28,20},{1,9},{5... | collective-permute-start | bytes 294920 | tf_op jit(solution)/shard_map/ppermute | solution.py:35
  60.0 20.9 %slice-start.4 = ((f32[2,4]{1,0:T(2,128)}), f32[1,4]{1,0:T(1,128)S(1)}, s32[]{:S(2)}) async-start(f32[2,4]{1,0:T(2,128)} %copy-done.6), calls=%async_computation.4 | async-start | bytes 1024 | tf_op jit(solution)/shard_map/slice | solution.py:180
  60.0 35.4 %collective-permute-start.28 = (bf16[512,384]{1,0:T(8,128)(2,1)}, bf16[512,384]{1,0:T(8,128)(2,1)}, u32[]{:S(2)}, u32[]{:S(2)}) collective-permute-start(bf16[512,384]{1,0:T(8,128)(2,1)} %bitcast.21), channel_id=1, source_target_pairs={{0,4},{4,0},{8,12},{12,8},{16,20},{20,16},{24,28},{28,24},{1,5},{5... | collective-permute-start | bytes 1179656 | tf_op jit(solution)/shard_map/ppermute | solution.py:119
  60.5 9.2 %collective-permute-start.8 = (bf16[128,512]{1,0:T(8,128)(2,1)S(1)}, bf16[128,512]{1,0:T(8,128)(2,1)S(1)}, u32[]{:S(2)}, u32[]{:S(2)}) collective-permute-start(bf16[128,512]{1,0:T(8,128)(2,1)S(1)} %slice.268), channel_id=1, source_target_pairs={{0,16},{4,20},{8,0},{12,4},{16,24},{20,28},{24,8},{28,12},{1,17},{... | collective-permute-start | bytes 393224 | tf_op jit(solution)/shard_map/ppermute | solution.py:35
  61.1 9.8 %collective-permute-start.9 = (bf16[128,512]{1,0:T(8,128)(2,1)S(1)}, bf16[128,512]{1,0:T(8,128)(2,1)S(1)}, u32[]{:S(2)}, u32[]{:S(2)}) collective-permute-start(bf16[128,512]{1,0:T(8,128)(2,1)S(1)} %slice.269), channel_id=1, source_target_pairs={{0,8},{4,12},{8,24},{12,28},{16,0},{20,4},{24,16},{28,20},{1,9},{5... | collective-permute-start | bytes 393224 | tf_op jit(solution)/shard_map/ppermute | solution.py:35
  62.7 13.6 %collective-permute-start.14 = (bf16[256,384]{1,0:T(8,128)(2,1)S(1)}, bf16[256,384]{1,0:T(8,128)(2,1)S(1)}, u32[]{:S(2)}, u32[]{:S(2)}) collective-permute-start(bf16[256,384]{1,0:T(8,128)(2,1)S(1)} %slice.225), channel_id=1, source_target_pairs={{0,16},{4,20},{8,0},{12,4},{16,24},{20,28},{24,8},{28,12},{1,17},{... | collective-permute-start | bytes 589832 | tf_op jit(solution)/shard_map/ppermute | solution.py:35
  69.7 7.9 %collective-permute-start.15 = (bf16[256,384]{1,0:T(8,128)(2,1)S(1)}, bf16[256,384]{1,0:T(8,128)(2,1)S(1)}, u32[]{:S(2)}, u32[]{:S(2)}) collective-permute-start(bf16[256,384]{1,0:T(8,128)(2,1)S(1)} %slice.225), channel_id=1, source_target_pairs={{0,8},{4,12},{8,24},{12,28},{16,0},{20,4},{24,16},{28,20},{1,9},{5... | collective-permute-start | bytes 589832 | tf_op jit(solution)/shard_map/ppermute | solution.py:35
  72.4 17.3 %collective-permute-start.10 = (bf16[512,512]{1,0:T(8,128)(2,1)}, bf16[512,512]{1,0:T(8,128)(2,1)}, u32[]{:S(2)}, u32[]{:S(2)}) collective-permute-start(bf16[512,512]{1,0:T(8,128)(2,1)} %bitcast.16), channel_id=1, source_target_pairs={{0,4},{4,0},{8,12},{12,8},{16,20},{20,16},{24,28},{28,24},{1,5},{5... | collective-permute-start | bytes 1572872 | tf_op jit(solution)/shard_map/ppermute | solution.py:119
  76.9 8.0 %collective-permute-start.16 = (bf16[128,384]{1,0:T(8,128)(2,1)}, bf16[128,384]{1,0:T(8,128)(2,1)}, u32[]{:S(2)}, u32[]{:S(2)}) collective-permute-start(bf16[128,384]{1,0:T(8,128)(2,1)} %slice.271), channel_id=1, source_target_pairs={{0,16},{4,20},{8,0},{12,4},{16,24},{20,28},{24,8},{28,12},{1,17},{... | collective-permute-start | bytes 294920 | tf_op jit(solution)/shard_map/ppermute | solution.py:35
  77.6 9.8 %collective-permute-start.17 = (bf16[128,384]{1,0:T(8,128)(2,1)S(1)}, bf16[128,384]{1,0:T(8,128)(2,1)S(1)}, u32[]{:S(2)}, u32[]{:S(2)}) collective-permute-start(bf16[128,384]{1,0:T(8,128)(2,1)S(1)} %slice.272), channel_id=1, source_target_pairs={{0,8},{4,12},{8,24},{12,28},{16,0},{20,4},{24,16},{28,20},{1,9},{5... | collective-permute-start | bytes 294920 | tf_op jit(solution)/shard_map/ppermute | solution.py:35
  79.3 0.9 copy-start.3
  84.0 2.6 %copy-start.4 = (bf16[1024,384]{1,0:T(8,128)(2,1)S(1)}, bf16[1024,384]{1,0:T(8,128)(2,1)}, u32[]{:S(2)}) copy-start(bf16[1024,384]{1,0:T(8,128)(2,1)} %copy-done.3) | copy-start | bytes 2359300
  84.8 18.2 %collective-permute-start.22 = (bf16[640,512]{1,0:T(8,128)(2,1)S(1)}, bf16[640,512]{1,0:T(8,128)(2,1)S(1)}, u32[]{:S(2)}, u32[]{:S(2)}) collective-permute-start(bf16[640,512]{1,0:T(8,128)(2,1)S(1)} %get-tuple-element.38), channel_id=1, source_target_pairs={{0,1},{1,0},{2,3},{3,2},{4,5},{5,4},{6,7},{7,6},{8,9},{9,8},{10,11... | collective-permute-start | bytes 1966088 | tf_op jit(solution)/shard_map/ppermute | solution.py:35
  84.9 17.6 %collective-permute-start.23 = (bf16[640,512]{1,0:T(8,128)(2,1)S(1)}, bf16[640,512]{1,0:T(8,128)(2,1)S(1)}, u32[]{:S(2)}, u32[]{:S(2)}) collective-permute-start(bf16[640,512]{1,0:T(8,128)(2,1)S(1)} %get-tuple-element.38), channel_id=1, source_target_pairs={{0,2},{1,3},{2,0},{3,1},{4,6},{5,7},{6,4},{7,5},{8,10},{9,11},{10,... | collective-permute-start | bytes 1966088 | tf_op jit(solution)/shard_map/ppermute | solution.py:35
  88.1 14.4 %collective-permute-start.18 = (bf16[512,384]{1,0:T(8,128)(2,1)S(1)}, bf16[512,384]{1,0:T(8,128)(2,1)S(1)}, u32[]{:S(2)}, u32[]{:S(2)}) collective-permute-start(bf16[512,384]{1,0:T(8,128)(2,1)S(1)} %bitcast.192), channel_id=1, source_target_pairs={{0,4},{4,0},{8,12},{12,8},{16,20},{20,16},{24,28},{28,24},{1,5},{5... | collective-permute-start | bytes 1179656 | tf_op jit(solution)/shard_map/ppermute | solution.py:119
  91.2 2.4 copy-start.5
  95.4 20.7 %collective-permute-start.11 = (bf16[640,512]{1,0:T(8,128)(2,1)S(1)}, bf16[640,512]{1,0:T(8,128)(2,1)S(1)}, u32[]{:S(2)}, u32[]{:S(2)}) collective-permute-start(bf16[640,512]{1,0:T(8,128)(2,1)S(1)} %get-tuple-element.42), channel_id=1, source_target_pairs={{0,1},{1,0},{2,3},{3,2},{4,5},{5,4},{6,7},{7,6},{8,9},{9,8},{10,11... | collective-permute-start | bytes 1966088 | tf_op jit(solution)/shard_map/ppermute | solution.py:35
  95.4 20.7 %collective-permute-start.12 = (bf16[640,512]{1,0:T(8,128)(2,1)S(1)}, bf16[640,512]{1,0:T(8,128)(2,1)S(1)}, u32[]{:S(2)}, u32[]{:S(2)}) collective-permute-start(bf16[640,512]{1,0:T(8,128)(2,1)S(1)} %get-tuple-element.42), channel_id=1, source_target_pairs={{0,2},{1,3},{2,0},{3,1},{4,6},{5,7},{6,4},{7,5},{8,10},{9,11},{10,... | collective-permute-start | bytes 1966088 | tf_op jit(solution)/shard_map/ppermute | solution.py:35
  102.5 15.5 %collective-permute-start.24 = (bf16[640,512]{1,0:T(8,128)(2,1)S(1)}, bf16[640,512]{1,0:T(8,128)(2,1)S(1)}, u32[]{:S(2)}, u32[]{:S(2)}) collective-permute-start(bf16[640,512]{1,0:T(8,128)(2,1)S(1)} %collective-permute-done.23), channel_id=1, source_target_pairs={{0,1},{1,0},{2,3},{3,2},{4,5},{5,4},{6,7},{7,6},{8,9},{9,8},{10,11... | collective-permute-start | bytes 1966088 | tf_op jit(solution)/shard_map/ppermute | solution.py:35
  116.1 5.0 %collective-permute-start.13 = (bf16[640,512]{1,0:T(8,128)(2,1)S(1)}, bf16[640,512]{1,0:T(8,128)(2,1)S(1)}, u32[]{:S(2)}, u32[]{:S(2)}) collective-permute-start(bf16[640,512]{1,0:T(8,128)(2,1)S(1)} %collective-permute-done.12), channel_id=1, source_target_pairs={{0,1},{1,0},{2,3},{3,2},{4,5},{5,4},{6,7},{7,6},{8,9},{9,8},{10,11... | collective-permute-start | bytes 1966088 | tf_op jit(solution)/shard_map/ppermute | solution.py:35
  119.0 4.7 %copy-start = (bf16[640,3584]{1,0:T(8,128)(2,1)}, bf16[640,3584]{1,0:T(8,128)(2,1)S(1)}, u32[]{:S(2)}) copy-start(bf16[640,3584]{1,0:T(8,128)(2,1)S(1)} %get-tuple-element.39) | copy-start | bytes 13762564
  119.0 14.6 %collective-permute-start.29 = (bf16[640,384]{1,0:T(8,128)(2,1)S(1)}, bf16[640,384]{1,0:T(8,128)(2,1)S(1)}, u32[]{:S(2)}, u32[]{:S(2)}) collective-permute-start(bf16[640,384]{1,0:T(8,128)(2,1)S(1)} %get-tuple-element.40), channel_id=1, source_target_pairs={{0,1},{1,0},{2,3},{3,2},{4,5},{5,4},{6,7},{7,6},{8,9},{9,8},{10,11... | collective-permute-start | bytes 1474568 | tf_op jit(solution)/shard_map/ppermute | solution.py:35
  119.5 14.1 %collective-permute-start.30 = (bf16[640,384]{1,0:T(8,128)(2,1)S(1)}, bf16[640,384]{1,0:T(8,128)(2,1)S(1)}, u32[]{:S(2)}, u32[]{:S(2)}) collective-permute-start(bf16[640,384]{1,0:T(8,128)(2,1)S(1)} %get-tuple-element.40), channel_id=1, source_target_pairs={{0,2},{1,3},{2,0},{3,1},{4,6},{5,7},{6,4},{7,5},{8,10},{9,11},{10,... | collective-permute-start | bytes 1474568 | tf_op jit(solution)/shard_map/ppermute | solution.py:35
  123.7 19.6 %collective-permute-start.20 = (bf16[640,384]{1,0:T(8,128)(2,1)S(1)}, bf16[640,384]{1,0:T(8,128)(2,1)S(1)}, u32[]{:S(2)}, u32[]{:S(2)}) collective-permute-start(bf16[640,384]{1,0:T(8,128)(2,1)S(1)} %get-tuple-element.44), channel_id=1, source_target_pairs={{0,2},{1,3},{2,0},{3,1},{4,6},{5,7},{6,4},{7,5},{8,10},{9,11},{10,... | collective-permute-start | bytes 1474568 | tf_op jit(solution)/shard_map/ppermute | solution.py:35
  124.6 18.7 %collective-permute-start.19 = (bf16[640,384]{1,0:T(8,128)(2,1)S(1)}, bf16[640,384]{1,0:T(8,128)(2,1)S(1)}, u32[]{:S(2)}, u32[]{:S(2)}) collective-permute-start(bf16[640,384]{1,0:T(8,128)(2,1)S(1)} %get-tuple-element.44), channel_id=1, source_target_pairs={{0,1},{1,0},{2,3},{3,2},{4,5},{5,4},{6,7},{7,6},{8,9},{9,8},{10,11... | collective-permute-start | bytes 1474568 | tf_op jit(solution)/shard_map/ppermute | solution.py:35
  133.6 11.4 %collective-permute-start.31 = (bf16[640,384]{1,0:T(8,128)(2,1)S(1)}, bf16[640,384]{1,0:T(8,128)(2,1)S(1)}, u32[]{:S(2)}, u32[]{:S(2)}) collective-permute-start(bf16[640,384]{1,0:T(8,128)(2,1)S(1)} %collective-permute-done.30), channel_id=1, source_target_pairs={{0,1},{1,0},{2,3},{3,2},{4,5},{5,4},{6,7},{7,6},{8,9},{9,8},{10,11... | collective-permute-start | bytes 1474568 | tf_op jit(solution)/shard_map/ppermute | solution.py:35
  143.3 9.4 %collective-permute-start.21 = (bf16[640,384]{1,0:T(8,128)(2,1)S(1)}, bf16[640,384]{1,0:T(8,128)(2,1)S(1)}, u32[]{:S(2)}, u32[]{:S(2)}) collective-permute-start(bf16[640,384]{1,0:T(8,128)(2,1)S(1)} %collective-permute-done.20), channel_id=1, source_target_pairs={{0,1},{1,0},{2,3},{3,2},{4,5},{5,4},{6,7},{7,6},{8,9},{9,8},{10,11... | collective-permute-start | bytes 1474568 | tf_op jit(solution)/shard_map/ppermute | solution.py:35
  144.1 17.0 %slice-start.5 = ((s8[4358144]{0:T(1024)(128)(4,1)}), s8[4194304]{0:T(1024)(128)(4,1)S(1)}, s32[]{:S(2)}) async-start(s8[4358144]{0:T(1024)(128)(4,1)} %bitcast.190), calls=%async_computation.5 | async-start | bytes 8388608
  145.9 15.2 %slice-start.6 = ((s8[4358144]{0:T(1024)(128)(4,1)}), s8[163840]{0:T(1024)(128)(4,1)S(1)}, s32[]{:S(2)}) async-start(s8[4358144]{0:T(1024)(128)(4,1)} %bitcast.190), calls=%async_computation.6 | async-start | bytes 327680
  153.6 13.6 %slice-start.2 = ((s8[4358144]{0:T(1024)(128)(4,1)}), s8[163840]{0:T(1024)(128)(4,1)S(1)}, s32[]{:S(2)}) async-start(s8[4358144]{0:T(1024)(128)(4,1)} %bitcast.182), calls=%async_computation.2 | async-start | bytes 327680
  161.1 6.2 %slice-start.3 = ((s8[4358144]{0:T(1024)(128)(4,1)}), s8[4194304]{0:T(1024)(128)(4,1)S(1)}, s32[]{:S(2)}) async-start(s8[4358144]{0:T(1024)(128)(4,1)} %bitcast.182), calls=%async_computation.3 | async-start | bytes 8388608
  169.4 6.0 %collective-permute-start.33 = (bf16[640,512]{1,0:T(8,128)(2,1)S(1)}, bf16[640,512]{1,0:T(8,128)(2,1)S(1)}, u32[]{:S(2)}, u32[]{:S(2)}) collective-permute-start(bf16[640,512]{1,0:T(8,128)(2,1)S(1)} %convolution_convert_fusion.2), channel_id=1, source_target_pairs={{0,1},{1,0},{2,3},{3,2},{4,5},{5,4},{6,7},{7,6},{8,9},{9,8},{10,11... | collective-permute-start | bytes 1966088 | tf_op jit(solution)/shard_map/ppermute | solution.py:35
  170.0 2.4 collective-permute-start.41
  171.5 19.2 %collective-permute-start.32 = (bf16[640,512]{1,0:T(8,128)(2,1)S(1)}, bf16[640,512]{1,0:T(8,128)(2,1)S(1)}, u32[]{:S(2)}, u32[]{:S(2)}) collective-permute-start(bf16[640,512]{1,0:T(8,128)(2,1)S(1)} %convolution_convert_fusion.3), channel_id=1, source_target_pairs={{0,1},{1,0},{2,3},{3,2},{4,5},{5,4},{6,7},{7,6},{8,9},{9,8},{10,11... | collective-permute-start | bytes 1966088 | tf_op jit(solution)/shard_map/ppermute | solution.py:35
  172.0 4.7 %collective-permute-start.40 = (bf16[640,384]{1,0:T(8,128)(2,1)S(1)}, bf16[640,384]{1,0:T(8,128)(2,1)S(1)}, u32[]{:S(2)}, u32[]{:S(2)}) collective-permute-start(bf16[640,384]{1,0:T(8,128)(2,1)S(1)} %convolution_convert_fusion.9), channel_id=1, source_target_pairs={{0,1},{1,0},{2,3},{3,2},{4,5},{5,4},{6,7},{7,6},{8,9},{9,8},{10,11... | collective-permute-start | bytes 1474568 | tf_op jit(solution)/shard_map/ppermute | solution.py:35
  173.2 14.1 %collective-permute-start.42 = (bf16[640,384]{1,0:T(8,128)(2,1)S(1)}, bf16[640,384]{1,0:T(8,128)(2,1)S(1)}, u32[]{:S(2)}, u32[]{:S(2)}) collective-permute-start(bf16[640,384]{1,0:T(8,128)(2,1)S(1)} %add_convert_fusion.3), channel_id=1, source_target_pairs={{0,2},{1,3},{2,0},{3,1},{4,6},{5,7},{6,4},{7,5},{8,10},{9,11},{10,... | collective-permute-start | bytes 1474568 | tf_op jit(solution)/shard_map/ppermute | solution.py:35
  176.1 24.6 %collective-permute-start.34 = (bf16[640,512]{1,0:T(8,128)(2,1)S(1)}, bf16[640,512]{1,0:T(8,128)(2,1)S(1)}, u32[]{:S(2)}, u32[]{:S(2)}) collective-permute-start(bf16[640,512]{1,0:T(8,128)(2,1)S(1)} %add_convert_fusion.1), channel_id=1, source_target_pairs={{0,2},{1,3},{2,0},{3,1},{4,6},{5,7},{6,4},{7,5},{8,10},{9,11},{10,... | collective-permute-start | bytes 1966088 | tf_op jit(solution)/shard_map/ppermute | solution.py:35
  188.1 15.2 %collective-permute-start.43 = (bf16[512,384]{1,0:T(8,128)(2,1)S(1)}, bf16[512,384]{1,0:T(8,128)(2,1)S(1)}, u32[]{:S(2)}, u32[]{:S(2)}) collective-permute-start(bf16[512,384]{1,0:T(8,128)(2,1)S(1)} %fusion.40), channel_id=1, source_target_pairs={{0,4},{4,0},{8,12},{12,8},{16,20},{20,16},{24,28},{28,24},{1,5},{5... | collective-permute-start | bytes 1179656 | tf_op jit(solution)/shard_map/ppermute | solution.py:119
  201.7 13.4 %collective-permute-start.35 = (bf16[512,512]{1,0:T(8,128)(2,1)S(1)}, bf16[512,512]{1,0:T(8,128)(2,1)S(1)}, u32[]{:S(2)}, u32[]{:S(2)}) collective-permute-start(bf16[512,512]{1,0:T(8,128)(2,1)S(1)} %fusion.32), channel_id=1, source_target_pairs={{0,4},{4,0},{8,12},{12,8},{16,20},{20,16},{24,28},{28,24},{1,5},{5... | collective-permute-start | bytes 1572872 | tf_op jit(solution)/shard_map/ppermute | solution.py:119
  204.0 4.7 %collective-permute-start.44 = (bf16[128,384]{1,0:T(8,128)(2,1)S(1)}, bf16[128,384]{1,0:T(8,128)(2,1)S(1)}, u32[]{:S(2)}, u32[]{:S(2)}) collective-permute-start(bf16[128,384]{1,0:T(8,128)(2,1)S(1)} %get-tuple-element.21), channel_id=1, source_target_pairs={{0,16},{4,20},{8,0},{12,4},{16,24},{20,28},{24,8},{28,12},{1,17},{... | collective-permute-start | bytes 294920 | tf_op jit(solution)/shard_map/ppermute | solution.py:35
  205.6 6.4 %collective-permute-start.46 = (bf16[128,384]{1,0:T(8,128)(2,1)S(1)}, bf16[128,384]{1,0:T(8,128)(2,1)S(1)}, u32[]{:S(2)}, u32[]{:S(2)}) collective-permute-start(bf16[128,384]{1,0:T(8,128)(2,1)S(1)} %get-tuple-element.22), channel_id=1, source_target_pairs={{0,8},{4,12},{8,24},{12,28},{16,0},{20,4},{24,16},{28,20},{1,9},{5... | collective-permute-start | bytes 294920 | tf_op jit(solution)/shard_map/ppermute | solution.py:35
  215.6 16.1 %slice-start = ((s8[4587520]{0:T(1024)(128)(4,1)}), s8[4194304]{0:T(1024)(128)(4,1)S(1)}, s32[]{:S(2)}) async-start(s8[4587520]{0:T(1024)(128)(4,1)} %bitcast.172), calls=%async_computation | async-start | bytes 8388608
  215.6 16.0 %slice-start.1 = ((s8[4587520]{0:T(1024)(128)(4,1)}), s8[393216]{0:T(1024)(128)(4,1)S(1)}, s32[]{:S(2)}) async-start(s8[4587520]{0:T(1024)(128)(4,1)} %bitcast.172), calls=%async_computation.1 | async-start | bytes 786432
  216.2 7.9 %collective-permute-start.36 = (bf16[128,512]{1,0:T(8,128)(2,1)S(1)}, bf16[128,512]{1,0:T(8,128)(2,1)S(1)}, u32[]{:S(2)}, u32[]{:S(2)}) collective-permute-start(bf16[128,512]{1,0:T(8,128)(2,1)S(1)} %get-tuple-element.17), channel_id=1, source_target_pairs={{0,16},{4,20},{8,0},{12,4},{16,24},{20,28},{24,8},{28,12},{1,17},{... | collective-permute-start | bytes 393224 | tf_op jit(solution)/shard_map/ppermute | solution.py:35
  217.8 11.6 %collective-permute-start.38 = (bf16[128,512]{1,0:T(8,128)(2,1)S(1)}, bf16[128,512]{1,0:T(8,128)(2,1)S(1)}, u32[]{:S(2)}, u32[]{:S(2)}) collective-permute-start(bf16[128,512]{1,0:T(8,128)(2,1)S(1)} %get-tuple-element.18), channel_id=1, source_target_pairs={{0,8},{4,12},{8,24},{12,28},{16,0},{20,4},{24,16},{28,20},{1,9},{5... | collective-permute-start | bytes 393224 | tf_op jit(solution)/shard_map/ppermute | solution.py:35
  218.3 18.5 %collective-permute-start.45 = (bf16[256,384]{1,0:T(8,128)(2,1)S(1)}, bf16[256,384]{1,0:T(8,128)(2,1)S(1)}, u32[]{:S(2)}, u32[]{:S(2)}) collective-permute-start(bf16[256,384]{1,0:T(8,128)(2,1)S(1)} %pad_maximum_fusion.4), channel_id=1, source_target_pairs={{0,16},{4,20},{8,0},{12,4},{16,24},{20,28},{24,8},{28,12},{1,17},{... | collective-permute-start | bytes 589832 | tf_op jit(solution)/shard_map/ppermute | solution.py:35
  220.9 18.4 %collective-permute-start.47 = (bf16[256,384]{1,0:T(8,128)(2,1)S(1)}, bf16[256,384]{1,0:T(8,128)(2,1)S(1)}, u32[]{:S(2)}, u32[]{:S(2)}) collective-permute-start(bf16[256,384]{1,0:T(8,128)(2,1)S(1)} %pad_maximum_fusion.5), channel_id=1, source_target_pairs={{0,8},{4,12},{8,24},{12,28},{16,0},{20,4},{24,16},{28,20},{1,9},{5... | collective-permute-start | bytes 589832 | tf_op jit(solution)/shard_map/ppermute | solution.py:35
  229.5 9.8 %collective-permute-start.37 = (bf16[256,512]{1,0:T(8,128)(2,1)S(1)}, bf16[256,512]{1,0:T(8,128)(2,1)S(1)}, u32[]{:S(2)}, u32[]{:S(2)}) collective-permute-start(bf16[256,512]{1,0:T(8,128)(2,1)S(1)} %pad_maximum_fusion.2), channel_id=1, source_target_pairs={{0,16},{4,20},{8,0},{12,4},{16,24},{20,28},{24,8},{28,12},{1,17},{... | collective-permute-start | bytes 786440 | tf_op jit(solution)/shard_map/ppermute | solution.py:35
  229.6 14.9 %collective-permute-start.39 = (bf16[256,512]{1,0:T(8,128)(2,1)S(1)}, bf16[256,512]{1,0:T(8,128)(2,1)S(1)}, u32[]{:S(2)}, u32[]{:S(2)}) collective-permute-start(bf16[256,512]{1,0:T(8,128)(2,1)S(1)} %pad_maximum_fusion.3), channel_id=1, source_target_pairs={{0,8},{4,12},{8,24},{12,28},{16,0},{20,4},{24,16},{28,20},{1,9},{5... | collective-permute-start | bytes 786440 | tf_op jit(solution)/shard_map/ppermute | solution.py:35

commit v2 on v1

v2 whole, which is shorter than its diff:
```python
import math

import jax
import jax.numpy as jnp
from jax import lax
from jax.sharding import PartitionSpec as P

BF = jnp.bfloat16
F32 = jnp.float32
ORDER = "x0 x1 x0 x0 x1 x0 d0 x1 x0 x1 d0 d1 x1 d0 x0 d0 d1 x0 d1 d0 x1 d1 x1 d1 d0 d0 d1 d1"
FETCH = {"x": [384, 512], "d": [512, 384]}
BACK = "g0 g1 g0 g1 g0 g1 g0 g1 g0 g1 g0 g1"


def ring_order(count):
    if count <= 4:
        return list(range(0, count, 2)) + list(range(1, count, 2))[::-1]
    return list(range(count))


def lookup(table, index):
    return sum(jnp.where(index == i, jnp.int32(v), jnp.int32(0)) for i, v in enumerate(table))


class Ring:
    def __init__(self, axis, size, count, stride):
        self.axis, self.count, self.stride = axis, count, stride
        self.order = ring_order(count)
        self.half = count // 2
        spot = {c: i for i, c in enumerate(self.order)}
        self.perms = {}
        for step in (1, -1):
            pairs = []
            for index in range(size):
                c = (index // stride) % count
                there = self.order[(spot[c] + step) % count]
                pairs.append((index, index + (there - c) * stride))
            self.perms[step] = pairs
        self.spot = [spot[c] for c in range(count)]

    def send(self, value, step):
        return lax.ppermute(value, self.axis, self.perms[step])

    def coordinate(self, mine, offset):
        place = lookup(self.spot, mine)
        return lookup(self.order, lax.rem(place + offset + self.count, self.count))

    def offsets(self):
        found = [0]
        for d in range(1, self.half):
            found += [-d, d]
        return found + ([self.half] if self.count > 1 else [])

    def near(self, line, value):
        blocks = {0: value}
        up = down = value
        for d in range(1, self.half):
            up, down = self.send(up, 1), self.send(down, -1)
            yield
            up, down = line.done(up, down)
            blocks[-d], blocks[d] = up, down
        return [blocks[o] for o in self.offsets() if o in blocks]

    def far(self, line, blocks, cut):
        if self.count == 1:
            return []
        if self.count == 2:
            got = self.send(blocks[0], 1)
            yield
            return [line.done(got)]
        up, down = line.go(blocks[-2][:cut], blocks[-1][cut:])
        up, down = self.send(up, 1), self.send(down, -1)
        yield
        return [jnp.concatenate(line.done(up, down), axis=0)]

    def gather(self, line, value, cut):
        blocks = yield from self.near(line, value)
        return blocks + (yield from self.far(line, blocks, cut))

    def reduce(self, line, blocks, cut):
        term = dict(zip(self.offsets(), blocks))
        if self.count == 1:
            return term[0]
        if self.count == 2:
            got = self.send(line.go(term[1].astype(BF)), 1)
            yield
            return term[0] + line.done(got).astype(F32)
        up, down = line.go(term[self.half][:cut].astype(BF), term[self.half][cut:].astype(BF))
        up, down = self.send(up, 1), self.send(down, -1)
        yield
        for d in range(self.half - 1, 0, -1):
            up, down = line.done(up, down)
            up, down = up.astype(F32), down.astype(F32)
            up_sum, down_sum = term[d], term[-d]
            if d == self.half - 1:
                up_sum = jnp.concatenate([up_sum[:cut] + up, up_sum[cut:]], axis=0)
                down_sum = jnp.concatenate([down_sum[:cut], down_sum[cut:] + down], axis=0)
            else:
                up_sum, down_sum = up_sum + up, down_sum + down
            up, down = line.go(up_sum.astype(BF), down_sum.astype(BF))
            up, down = self.send(up, 1), self.send(down, -1)
            yield
        up, down = line.done(up, down)
        return term[0] + up.astype(F32) + down.astype(F32)


class Line:
    def __init__(self):
        self.mark = jnp.zeros((8, 128), F32)

    def go(self, *values):
        out = lax.optimization_barrier((*values, self.mark))
        return out[0] if len(values) == 1 else out[:-1]

    def done(self, *values):
        out = lax.optimization_barrier((*values, self.mark))
        self.mark = out[-1]
        return out[0] if len(values) == 1 else out[:-1]


def run(parts, order):
    results = {}

    def step(name):
        if name not in results:
            try:
                with jax.named_scope(name):
                    next(parts[name])
            except StopIteration as end:
                results[name] = end.value

    for name in order:
        step(name)
    while len(results) < len(parts):
        for name in parts:
            step(name)
    return results


def pick(onehot, rows):
    return jnp.dot(onehot, rows, preferred_element_type=F32).astype(BF)


def unpick(onehot, rows):
    return lax.dot_general(onehot, rows, (((0,), (0,)), ((), ())), preferred_element_type=F32)


def silu_parts(hidden):
    sigma = jax.nn.sigmoid(hidden)
    return (hidden * sigma, sigma * (1.0 + hidden * (1.0 - sigma)))


def per_device(tokens, cotangent, up_weight, down_weight, expert_ids, gate_probs):
    tok, top = expert_ids.shape
    width = tokens.shape[1]
    n_exp, n_tp = lax.axis_size("exp"), lax.axis_size("tp")
    experts = n_exp * up_weight.shape[0]
    slot = min(4 * tok // experts, tok)
    capacity = 5 * tok * n_exp // (2 * experts)
    nx = 2 ** (int(math.log2(n_exp)) // 2)
    nz = n_exp // nx
    nc = 2 if n_tp % 2 == 0 else 1
    ny = n_tp // nc
    zring, yring, cring = (
        Ring("exp", n_exp, nz, nx),
        Ring("tp", n_tp, ny, nc),
        Ring("tp", n_tp, nc, 1),
    )
    e, t = lax.axis_index("exp"), lax.axis_index("tp")
    z, x, y, c = lax.div(e, nx), lax.rem(e, nx), lax.div(t, nc), lax.rem(t, nc)

    def cross(value, dx):
        pairs = [(i, i // nx * nx + (i % nx + dx) % nx) for i in range(n_exp)]
        return lax.ppermute(value, "exp", pairs)

    w_up, w_down = up_weight[0], down_weight[0]
    hid = w_up.shape[1]
    first = min(-(-width // 256) * 128, width)
    edges = [(0, first), (first, width)] if first < width else [(0, width)]

    head = 16
    meta = jnp.concatenate([expert_ids.astype(BF).T, gate_probs.T], axis=0)
    meta = jnp.pad(meta, ((0, head - 2 * top), (0, (FETCH['x'][0] if width > 512 else width) - tok)))

    line = Line()
    shared = {}
    half = capacity // 2

    def ranks(info):
        info = jnp.stack(info, axis=0)
        n = info.shape[0]
        ids, probs = info[:, :top], info[:, top : 2 * top]
        shifts = jnp.arange(nx, dtype=jnp.int32)
        wanted = (z * nx + lax.rem(x + shifts, nx)).astype(BF)
        hit = ids[None] == wanted[:, None, None, None]
        match = jnp.any(hit, axis=2)
        weight = jnp.sum(jnp.where(hit, probs[None], jnp.zeros_like(probs[None])), axis=2)
        spot = jnp.arange(tok)
        below = (spot[:, None] < spot[None, :]).astype(BF)
        local = jnp.dot(
            match.astype(BF).reshape(nx * n, tok), below, preferred_element_type=F32
        ).astype(jnp.int32)
        local = jnp.where(match, local.reshape(nx, n, tok), -1)
        rank_of_slot = jnp.arange(slot, dtype=jnp.int32)[:, None]
        outs = []
        for dx in range(1, nx):
            onehot = local[dx][:, None, :] == rank_of_slot[None]
            scaled = jnp.where(onehot, weight[dx][:, None, :], jnp.zeros((), BF))
            outs.append((onehot.astype(BF), scaled))
        return dict(
            match=match[0], weight=weight[0], local=local[0], outs=outs,
            count=jnp.sum(match.astype(F32), axis=2),
        )

    def places(others):
        zs = zring.coordinate(z, jnp.asarray(zring.offsets(), jnp.int32))
        number = jnp.stack([zs * nx + lax.rem(x - dx + nx, nx) for dx in range(nx)], axis=0)
        counts = jnp.stack(others, axis=0)
        earlier = number.reshape(-1)[None, :] < number.reshape(-1)[:, None]
        base = jnp.sum(jnp.where(earlier, counts.reshape(-1)[None, :], 0.0), axis=1)
        base = base.astype(jnp.int32).reshape(nx, nz)
        counts = counts.astype(jnp.int32)
        place = jnp.arange(capacity, dtype=jnp.int32)[:, None]
        match, local, weight = (
            jnp.concatenate([g[key] for g in groups], axis=0) for key in ("match", "local", "weight")
        )
        rank = jnp.where(match, local + base[0][:, None], -1).reshape(1, nz * tok)
        own = rank == place
        shared["own"] = own.astype(BF)
        shared["own_w"] = jnp.where(own, weight.reshape(1, nz * tok), jnp.zeros((), BF))
        lane = jnp.arange(slot, dtype=jnp.int32)[None, :]
        shared["in"] = []
        for dx in range(1, nx):
            there = jnp.where(lane < counts[dx][:, None], base[dx][:, None] + lane, -1)
            shared["in"].append((there.reshape(1, nz * slot) == place).astype(BF))
        shared["out"] = [
            jnp.concatenate([g["outs"][dx - 1][0] for g in groups], axis=0) for dx in range(1, nx)
        ]

    groups = []

    def leave(group, blocks, tail, lead):
        n = len(blocks)
        rows = jnp.stack(blocks, axis=0)
        backs = []
        for dx in range(1, nx):
            onehot = group["outs"][dx - 1][1 if tail else 0]
            out = lax.dot_general(
                onehot, rows, (((2,), (1,)), ((0,), (0,))), preferred_element_type=F32
            )
            out = out.astype(BF).reshape(n * slot, -1)
            if lead:
                tally = group["count"][dx][None].astype(BF)
                tally = jnp.pad(tally, ((0, head - 1), (0, out.shape[1] - n)))
                out = jnp.concatenate([tally, out], axis=0)
            backs.append(cross(line.go(out), dx))
        return backs

    def fetch(source, lo, hi, tail, lead):
        piece = source[:, lo:hi]
        if lead:
            piece = jnp.concatenate([meta, piece], axis=0)
        piece = line.go(piece)
        top_rows = head if lead else 0
        blocks = yield from zring.near(line, piece)
        far = zring.far(line, blocks, top_rows + tok // 2)
        opposite = []
        try:
            next(far)
        except StopIteration as end:
            opposite = end.value
        yield
        if lead:
            groups.append(ranks([b[:head, :tok] for b in blocks]))
            blocks = [b[head:] for b in blocks]
        backs = [leave(groups[0], blocks, tail, lead)]
        yield
        if nz > 1:
            try:
                next(far)
            except StopIteration as end:
                opposite = end.value
            if lead:
                groups.append(ranks([b[:head, :tok] for b in opposite]))
                opposite = [b[head:] for b in opposite]
            backs.append(leave(groups[1], opposite, tail, lead))
            yield
        backs = [[line.done(g) for g in group] for group in backs]
        if lead:
            tallies = [jnp.concatenate([g["count"][0] for g in groups], axis=0)]
            for dx in range(1, nx):
                parts_ = [
                    b[dx - 1][0, : g["match"].shape[0]].astype(F32) for g, b in zip(groups, backs)
                ]
                tallies.append(jnp.concatenate(parts_, axis=0))
            places(tallies)
            backs = [[g[head:] for g in group] for group in backs]
        rows = jnp.concatenate(blocks + opposite, axis=0)
        part = pick(shared["own" + tail], rows)
        for dx in range(1, nx):
            back = jnp.concatenate([b[dx - 1] for b in backs], axis=0)
            part = part + pick(shared["in"][dx - 1], back)
        part = line.go(part)
        cores = [cring.gather(line, part, half)]
        if nc > 1:
            next(cores[0])
        ys = yring.gather(line, part, half)
        pieces = []
        try:
            next(ys)
            yield
            while True:
                next(ys)
                yield
        except StopIteration as end:
            by_y = end.value
        cores += [cring.gather(line, b, half) for b in by_y[1:]]
        for g in cores[1:]:
            if nc > 1:
                next(g)
        yield
        for oy, g in zip(yring.offsets(), cores):
            try:
                while True:
                    next(g)
            except StopIteration as end:
                for oc, b in zip(cring.offsets(), end.value):
                    index = yring.coordinate(y, oy) * nc + cring.coordinate(c, oc)
                    pieces.append((index * width + lo, b))
        return pieces

    parts = {}
    cuts = FETCH if width > 512 else {"x": [width], "d": [width]}
    for name, source, tail in (("x", tokens, ""), ("d", cotangent, "_w")):
        lo = 0
        for k, w in enumerate(cuts[name]):
            parts[name + str(k)] = fetch(source, lo, lo + w, tail, name + str(k) == "x0")
            lo += w
    order = ORDER.split() if (nz, nx, ny, nc) == (4, 2, 2, 2) else []
    got = run(parts, order)

    full = {}
    for name in ("x", "d"):
        whole = jnp.zeros((capacity, n_tp * width), BF)
        for k in range(len(cuts[name])):
            for column, piece in got[name + str(k)]:
                whole = lax.dynamic_update_slice(whole, piece, (0, column))
        full[name] = whole

    inputs, routed = full["x"], full["d"]
    hidden = jnp.dot(inputs, w_up, preferred_element_type=F32)
    act_full, slope = silu_parts(hidden)
    act = act_full.astype(BF)
    d_act = lax.dot_general(routed, w_down, (((1,), (1,)), ((), ())), preferred_element_type=F32)
    d_hidden = (d_act * slope).astype(BF)
    d_hidden = line.done(d_hidden)

    def give(lo, hi):
        w = hi - lo
        by_y = []
        for oy in yring.offsets():
            by_c = []
            for oc in cring.offsets():
                index = yring.coordinate(y, oy) * nc + cring.coordinate(c, oc)
                part = lax.dynamic_slice(w_up, (index * width + lo, 0), (w, hid))
                by_c.append(
                    lax.dot_general(
                        d_hidden, part, (((1,), (1,)), ((), ())), preferred_element_type=F32
                    )
                )
            by_y.append(by_c)
        stack = [jnp.concatenate([b[i] for b in by_y], axis=0) for i in range(nc)]
        summed = yield from cring.reduce(line, stack, half)
        summed = summed.reshape(ny, capacity, w)
        total = yield from yring.reduce(line, [summed[i] for i in range(ny)], half)
        total = total.astype(BF)
        backs = []
        for dx in range(1, nx):
            out = line.go(unpick(shared["in"][dx - 1], total).astype(BF))
            backs.append(cross(out, -dx))
        mine = unpick(shared["own"], total).reshape(nz, tok, w)
        if backs:
            yield
        for dx, back in enumerate(backs, 1):
            back = line.done(back).reshape(nz, slot, w)
            mine = mine + lax.dot_general(
                shared["out"][dx - 1], back, (((1,), (1,)), ((0,), (0,))), preferred_element_type=F32
            )
        result = yield from zring.reduce(line, [mine[i] for i in range(nz)], tok // 2)
        return result.astype(BF)

    parts = {"g%d" % k: give(lo, hi) for k, (lo, hi) in enumerate(edges)}
    order = BACK.split() if (nz, nx, ny, nc, len(edges)) == (4, 2, 2, 2, 2) else []
    got = run(parts, order)
    results = [got["g%d" % k] for k in range(len(edges))]
    grad_up = unpick(inputs, d_hidden).astype(BF)
    grad_down = unpick(act, routed).astype(BF)
    token_grad = jnp.concatenate(results, axis=1)
    return (token_grad, grad_up[None], grad_down[None])


def solution(mesh):
    placed = (
        P("exp", "tp"),
        P("exp", "tp"),
        P("exp", None, "tp"),
        P("exp", "tp", None),
        P("exp", None),
        P("exp", None),
    )
    return jax.shard_map(
        per_device,
        mesh=mesh,
        in_specs=placed,
        out_specs=(P("exp", "tp"), P("exp", None, "tp"), P("exp", "tp", None)),
        check_vma=False,
    )
```

time: 246 us -> 193 us (0.78)
  waiting for transfers between devices: 115 us -> 88.7 us
  local copies, waits for them, and re-layouts: 24.9 us -> 10.6 us
  matrix products: 49.8 us -> 37.8 us
  other arithmetic: 9.01 us -> 6.34 us
    ppermute x42 -> x40, waiting for transfers between devices: 112 us -> 63 us  [send(): return lax.ppermute(value, self.axis, self.perms[step])]
    ppermute x6 -> x10, waiting for transfers between devices: 3.11 us -> 25.7 us  [cross(): return lax.ppermute(value, 'exp', pairs)]
    dynamic_update_slice x12 -> x16, local copies, waits for them, and re-layouts: 8.3 us -> 1.06 us  [per_device(): whole = lax.dynamic_update_slice(whole, piece, (0, column))]
    ppermute x6 -> x10, starting transfers between devices: 8.2 us -> 12.5 us  [cross(): return lax.ppermute(value, 'exp', pairs)]
    dot_general x8, matrix products: 10.3 us -> 6.43 us  [pick(): return jnp.dot(onehot, rows, preferred_element_type=F32).astype(BF)]
    dot_general x1, matrix products: 6.78 us -> 3.56 us  [per_device(): hidden = jnp.dot(inputs, w_up, preferred_element_type=F32)]
    ppermute x42 -> x40, starting transfers between devices: 37.5 us -> 35.1 us  [send(): return lax.ppermute(value, self.axis, self.perms[step])]
    dot_general x15 -> x20, matrix products: 10.7 us -> 10.2 us  [the longest x8 5.58 us: give(): lax.dot_general(d_hidden, part, (((1,), (1,)), ((), ())), preferred_eleme...]
  transfers between devices with their start and end apart: 48 -> 50, of which waited for: 23 -> 22; matrix products, arithmetic and copies ran while one was open for 25% -> 23% of each run, Pallas kernels for 0% -> 0%
where the time goes in v2:
time: 193 us
  waiting for transfers between devices  88.7 us (46%)
  starting transfers between devices  47.6 us (25%)
  matrix products  37.8 us (20%)
  local copies, waits for them, and re-layouts  10.6 us (5%)
  other arithmetic  6.34 us (3%)
    ppermute x40, waiting for transfers between devices, send(): return lax.ppermute(value, self.axis, self.perms[step])  63 us
    ppermute x40, starting transfers between devices, send(): return lax.ppermute(value, self.axis, self.perms[step])  35.1 us
    ppermute x10, waiting for transfers between devices, cross(): return lax.ppermute(value, 'exp', pairs)  25.7 us
    dot_general x6, matrix products, unpick(): lax.dot_general(onehot, rows, (((0,), (0,)), ((), ())), preferred_element...  13.8 us
    ppermute x10, starting transfers between devices, cross(): return lax.ppermute(value, 'exp', pairs)  12.5 us
    dot_general x8, matrix products, pick(): return jnp.dot(onehot, rows, preferred_element_type=F32).astype(BF)  6.43 us
    dot_general x8, matrix products, give(): lax.dot_general(d_hidden, part, (((1,), (1,)), ((), ())), preferred_eleme...  5.58 us
  transfers between devices with their start and end apart: 50, of which 22 were waited for; matrix products, arithmetic and copies ran while one was open for 23% of the time, Pallas kernels for 0%

profile of v2, /device:TPU:0, one launch (start us, length us, event | category | flops | bytes accessed | tf_op | source)
XLA Modules:
  0.0 192.6 jit_solution(8750109761311196527)
XLA Ops:
  0.6 1.0 slice.260
  3.0 4.1 %collective-permute-start = (bf16[272,384]{1,0:T(8,128)(2,1)S(1)}, bf16[272,384]{1,0:T(8,128)(2,1)S(1)}, u32[]{:S(2)}, u32[]{:S(2)}) collective-permute-start(bf16[272,384]{1,0:T(8,128)(2,1)S(1)} %pad_maximum_fusion.5), channel_id=1, source_target_pairs={{0,16},{4,20},{8,0},{12,4},{16,24},{20,28},{24,8},{28,12},{1,17},{... | collective-permute-start | bytes 626696 | tf_op jit(solution)/shard_map/x0/ppermute | solution.py:42
  7.1 1.0 slice.268
  8.1 3.0 %collective-permute-start.4 = (bf16[256,512]{1,0:T(8,128)(2,1)S(1)}, bf16[256,512]{1,0:T(8,128)(2,1)S(1)}, u32[]{:S(2)}, u32[]{:S(2)}) collective-permute-start(bf16[256,512]{1,0:T(8,128)(2,1)S(1)} %slice.268), channel_id=1, source_target_pairs={{0,16},{4,20},{8,0},{12,4},{16,24},{20,28},{24,8},{28,12},{1,17},{... | collective-permute-start | bytes 786440 | tf_op jit(solution)/shard_map/x1/ppermute | solution.py:42
  11.1 1.0 slice.291
  12.1 1.0 slice.301
  13.0 0.7 constant_dynamic-update-slice_fusion.9
  13.9 5.2 %collective-permute-done.1 = bf16[272,384]{1,0:T(8,128)(2,1)S(1)} collective-permute-done((bf16[272,384]{1,0:T(8,128)(2,1)S(1)}, bf16[272,384]{1,0:T(8,128)(2,1)S(1)}, u32[]{:S(2)}, u32[]{:S(2)}) %collective-permute-start.1) | collective-permute-done | bytes 208928 | tf_op jit(solution)/shard_map/x0/ppermute | solution.py:42
  20.0 1.6 collective-permute-start.3
  22.3 1.6 collective-permute-start.6
  24.1 6.3 %collective-permute-done.5 = bf16[256,512]{1,0:T(8,128)(2,1)S(1)} collective-permute-done((bf16[256,512]{1,0:T(8,128)(2,1)S(1)}, bf16[256,512]{1,0:T(8,128)(2,1)S(1)}, u32[]{:S(2)}, u32[]{:S(2)}) %collective-permute-start.5) | collective-permute-done | bytes 262176 | tf_op jit(solution)/shard_map/x1/ppermute | solution.py:42
  30.9 1.6 collective-permute-start.11
  32.5 0.7 constant_dynamic-update-slice_fusion.8
  33.2 1.3 convolution_convert_fusion.9
  35.6 1.4 collective-permute-start.8
  39.2 1.6 collective-permute-start.7
  41.7 2.2 %collective-permute-done.7 = bf16[144,384]{1,0:T(8,128)(2,1)S(1)} collective-permute-done((bf16[144,384]{1,0:T(8,128)(2,1)S(1)}, bf16[144,384]{1,0:T(8,128)(2,1)S(1)}, u32[]{:S(2)}, u32[]{:S(2)}) %collective-permute-start.7) | collective-permute-done | bytes 110624 | tf_op jit(solution)/shard_map/x0/ppermute | solution.py:174
  44.0 1.5 collective-permute-start.16
  47.3 0.8 fusion.33
  48.7 1.6 collective-permute-start.14
  51.5 2.0 %collective-permute-start.20 = (bf16[256,384]{1,0:T(8,128)(2,1)S(1)}, bf16[256,384]{1,0:T(8,128)(2,1)S(1)}, u32[]{:S(2)}, u32[]{:S(2)}) collective-permute-start(bf16[256,384]{1,0:T(8,128)(2,1)S(1)} %slice.301), channel_id=1, source_target_pairs={{0,16},{4,20},{8,0},{12,4},{16,24},{20,28},{24,8},{28,12},{1,17},{... | collective-permute-start | bytes 589832 | tf_op jit(solution)/shard_map/d1/ppermute | solution.py:42
  54.4 2.6 %collective-permute-done.15 = bf16[128,512]{1,0:T(8,128)(2,1)S(1)} collective-permute-done((bf16[128,512]{1,0:T(8,128)(2,1)S(1)}, bf16[128,512]{1,0:T(8,128)(2,1)S(1)}, u32[]{:S(2)}, u32[]{:S(2)}) %collective-permute-start.15) | collective-permute-done | bytes 131104 | tf_op jit(solution)/shard_map/x1/ppermute | solution.py:174
  56.9 2.0 %collective-permute-start.12 = (bf16[128,512]{1,0:T(8,128)(2,1)S(1)}, bf16[128,512]{1,0:T(8,128)(2,1)S(1)}, u32[]{:S(2)}, u32[]{:S(2)}) collective-permute-start(bf16[128,512]{1,0:T(8,128)(2,1)S(1)} %slice.294), channel_id=1, source_target_pairs={{0,16},{4,20},{8,0},{12,4},{16,24},{20,28},{24,8},{28,12},{1,17},{... | collective-permute-start | bytes 393224 | tf_op jit(solution)/shard_map/d0/ppermute | solution.py:42
  59.0 1.5 convolution_convert_fusion.4
  60.5 0.9 fusion.39
  61.4 4.8 %collective-permute-done.12 = bf16[128,512]{1,0:T(8,128)(2,1)S(1)} collective-permute-done((bf16[128,512]{1,0:T(8,128)(2,1)S(1)}, bf16[128,512]{1,0:T(8,128)(2,1)S(1)}, u32[]{:S(2)}, u32[]{:S(2)}) %collective-permute-start.12) | collective-permute-done | bytes 131104 | tf_op jit(solution)/shard_map/d0/ppermute | solution.py:42
  66.2 0.8 collective-permute-start.27
  67.0 2.4 %collective-permute-done.13 = bf16[128,512]{1,0:T(8,128)(2,1)S(1)} collective-permute-done((bf16[128,512]{1,0:T(8,128)(2,1)S(1)}, bf16[128,512]{1,0:T(8,128)(2,1)S(1)}, u32[]{:S(2)}, u32[]{:S(2)}) %collective-permute-start.13) | collective-permute-done | bytes 131104 | tf_op jit(solution)/shard_map/d0/ppermute | solution.py:42
  69.5 1.5 collective-permute-start.17
  73.5 7.8 %collective-permute-done.17 = bf16[384,512]{1,0:T(8,128)(2,1)S(1)} collective-permute-done((bf16[384,512]{1,0:T(8,128)(2,1)S(1)}, bf16[384,512]{1,0:T(8,128)(2,1)S(1)}, u32[]{:S(2)}, u32[]{:S(2)}) %collective-permute-start.17) | collective-permute-done | bytes 393248 | tf_op jit(solution)/shard_map/d0/ppermute | solution.py:174
  81.4 1.1 collective-permute-start.26
  82.5 1.4 collective-permute-done.22
  84.3 0.8 fusion.42
  85.7 1.2 collective-permute-done.26
  86.9 1.5 collective-permute-start.29
  90.5 5.7 %collective-permute-done.29 = bf16[384,384]{1,0:T(8,128)(2,1)S(1)} collective-permute-done((bf16[384,384]{1,0:T(8,128)(2,1)S(1)}, bf16[384,384]{1,0:T(8,128)(2,1)S(1)}, u32[]{:S(2)}, u32[]{:S(2)}) %collective-permute-start.29) | collective-permute-done | bytes 294944 | tf_op jit(solution)/shard_map/d1/ppermute | solution.py:174
  96.2 1.1 collective-permute-done.28
  97.8 0.8 fusion.45
  98.6 1.6 collective-permute-start.34
  100.3 2.1 %collective-permute-done.24 = bf16[640,512]{1,0:T(8,128)(2,1)S(1)} collective-permute-done((bf16[640,512]{1,0:T(8,128)(2,1)S(1)}, bf16[640,512]{1,0:T(8,128)(2,1)S(1)}, u32[]{:S(2)}, u32[]{:S(2)}) %collective-permute-start.24) | collective-permute-done | bytes 655392 | tf_op jit(solution)/shard_map/d0/ppermute | solution.py:42
  102.6 3.6 %fusion.2 = f32[640,608]{0,1:T(8,128)S(1)} fusion(bf16[640,3584]{1,0:T(8,128)(2,1)S(1)} %constant_dynamic-update-slice_fusion.15, bf16[1,3584,608]{1,2,0:T(8,128)(2,1)S(1)} %bitcast.194), kind=kOutput, calls=%fused_computation.4 | convolution fusion | flops 2789212160 | bytes 10502144 | tf_op jit(solution)/shard_map/dot_general | solution.py:351
  106.2 6.0 %collective-permute-done.34 = bf16[640,384]{1,0:T(8,128)(2,1)S(1)} collective-permute-done((bf16[640,384]{1,0:T(8,128)(2,1)S(1)}, bf16[640,384]{1,0:T(8,128)(2,1)S(1)}, u32[]{:S(2)}, u32[]{:S(2)}) %collective-permute-start.34) | collective-permute-done | bytes 491552 | tf_op jit(solution)/shard_map/d1/ppermute | solution.py:42
  112.5 1.5 collective-permute-done.35
  114.1 3.7 %multiply_convert_fusion.1 = bf16[640,608]{0,1:T(8,128)(2,1)S(1)} fusion(f32[640,608]{0,1:T(8,128)S(1)} %fusion.2, bf16[640,3584]{1,0:T(8,128)(2,1)S(1)} %constant_dynamic-update-slice_fusion.23, bf16[1,608,3584]{2,1,0:T(8,128)(2,1)S(1)} %bitcast.223), kind=kOutput, calls=%fused_computation.20 | convolution fusion | flops 2792714240 | bytes 11280384 | tf_op jit(solution)/shard_map/dot_general | solution.py:354
  125.0 1.0 collective-permute-start.37
  126.2 1.2 collective-permute-start.40
  127.4 5.4 %fusion = bf16[1,608,3584]{2,1,0:T(8,128)(2,1)} fusion(bf16[640,3584]{1,0:T(8,128)(2,1)S(1)} %constant_dynamic-update-slice_fusion.23, f32[640,608]{0,1:T(8,128)S(1)} %fusion.2), kind=kOutput, calls=%fused_computation.2 | convolution fusion | flops 2793336832 | bytes 10502144 | tf_op jit(solution)/shard_map/dot_general | solution.py:145
  132.8 9.8 %collective-permute-done.37 = bf16[640,512]{1,0:T(8,128)(2,1)S(1)} collective-permute-done((bf16[640,512]{1,0:T(8,128)(2,1)S(1)}, bf16[640,512]{1,0:T(8,128)(2,1)S(1)}, u32[]{:S(2)}, u32[]{:S(2)}) %collective-permute-start.37) | collective-permute-done | bytes 655392 | tf_op jit(solution)/shard_map/g0/ppermute | solution.py:42
  143.3 1.6 collective-permute-start.39
  144.8 7.6 %collective-permute-done.40 = bf16[640,384]{1,0:T(8,128)(2,1)S(1)} collective-permute-done((bf16[640,384]{1,0:T(8,128)(2,1)S(1)}, bf16[640,384]{1,0:T(8,128)(2,1)S(1)}, u32[]{:S(2)}, u32[]{:S(2)}) %collective-permute-start.40) | collective-permute-done | bytes 491552 | tf_op jit(solution)/shard_map/g1/ppermute | solution.py:42
  153.0 1.6 collective-permute-start.43
  154.6 1.0 fusion.6
  155.6 1.0 fusion.7
  157.8 1.5 collective-permute-start.42
  159.2 4.9 %collective-permute-done.43 = bf16[512,384]{1,0:T(8,128)(2,1)S(1)} collective-permute-done((bf16[512,384]{1,0:T(8,128)(2,1)S(1)}, bf16[512,384]{1,0:T(8,128)(2,1)S(1)}, u32[]{:S(2)}, u32[]{:S(2)}) %collective-permute-start.43) | collective-permute-done | bytes 393248 | tf_op jit(solution)/shard_map/g1/ppermute | solution.py:174
  165.2 1.5 collective-permute-start.47
  166.8 1.5 collective-permute-start.44
  168.9 2.5 %collective-permute-done.46 = bf16[128,384]{1,0:T(8,128)(2,1)S(1)} collective-permute-done((bf16[128,384]{1,0:T(8,128)(2,1)S(1)}, bf16[128,384]{1,0:T(8,128)(2,1)S(1)}, u32[]{:S(2)}, u32[]{:S(2)}) %collective-permute-start.46) | collective-permute-done | bytes 98336 | tf_op jit(solution)/shard_map/g1/ppermute | solution.py:42
  171.4 6.2 %collective-permute-done.47 = bf16[128,384]{1,0:T(8,128)(2,1)S(1)} collective-permute-done((bf16[128,384]{1,0:T(8,128)(2,1)S(1)}, bf16[128,384]{1,0:T(8,128)(2,1)S(1)}, u32[]{:S(2)}, u32[]{:S(2)}) %collective-permute-start.47) | collective-permute-done | bytes 98336 | tf_op jit(solution)/shard_map/g1/ppermute | solution.py:42
  177.8 2.0 %collective-permute-start.49 = (bf16[256,384]{1,0:T(8,128)(2,1)S(1)}, bf16[256,384]{1,0:T(8,128)(2,1)S(1)}, u32[]{:S(2)}, u32[]{:S(2)}) collective-permute-start(bf16[256,384]{1,0:T(8,128)(2,1)S(1)} %pad_maximum_fusion.8), channel_id=1, source_target_pairs={{0,8},{4,12},{8,24},{12,28},{16,0},{20,4},{24,16},{28,20},{1,9},{5... | collective-permute-start | bytes 589832 | tf_op jit(solution)/shard_map/g1/ppermute | solution.py:42
  179.8 5.1 %fusion.1 = bf16[1,3584,608]{1,2,0:T(8,128)(2,1)} fusion(bf16[640,608]{0,1:T(8,128)(2,1)S(1)} %multiply_convert_fusion.1, bf16[640,3584]{1,0:T(8,128)(2,1)S(1)} %constant_dynamic-update-slice_fusion.15), kind=kOutput, calls=%fused_computation.3 | convolution fusion | flops 2791391232 | bytes 9723904 | tf_op jit(solution)/shard_map/dot_general | solution.py:145
  184.9 2.9 %collective-permute-done.48 = bf16[256,384]{1,0:T(8,128)(2,1)S(1)} collective-permute-done((bf16[256,384]{1,0:T(8,128)(2,1)S(1)}, bf16[256,384]{1,0:T(8,128)(2,1)S(1)}, u32[]{:S(2)}, u32[]{:S(2)}) %collective-permute-start.48) | collective-permute-done | bytes 196640 | tf_op jit(solution)/shard_map/g1/ppermute | solution.py:42
  187.8 3.8 %collective-permute-done.49 = bf16[256,384]{1,0:T(8,128)(2,1)S(1)} collective-permute-done((bf16[256,384]{1,0:T(8,128)(2,1)S(1)}, bf16[256,384]{1,0:T(8,128)(2,1)S(1)}, u32[]{:S(2)}, u32[]{:S(2)}) %collective-permute-start.49) | collective-permute-done | bytes 196640 | tf_op jit(solution)/shard_map/g1/ppermute | solution.py:42
  191.8 0.8 pad_maximum_fusion.2
  (206 shorter events, 30.8 us)
Async XLA Ops:
  0.6 13.1 %copy-start.2 = (s32[4]{0:T(128)S(1)}, s32[4]{0:T(128)}, u32[]{:S(2)}) copy-start(s32[4]{0:T(128)} %constant.97.clone) | copy-start | bytes 52
  3.0 10.9 %collective-permute-start = (bf16[272,384]{1,0:T(8,128)(2,1)S(1)}, bf16[272,384]{1,0:T(8,128)(2,1)S(1)}, u32[]{:S(2)}, u32[]{:S(2)}) collective-permute-start(bf16[272,384]{1,0:T(8,128)(2,1)S(1)} %pad_maximum_fusion.5), channel_id=1, source_target_pairs={{0,16},{4,20},{8,0},{12,4},{16,24},{20,28},{24,8},{28,12},{1,17},{... | collective-permute-start | bytes 626696 | tf_op jit(solution)/shard_map/x0/ppermute | solution.py:42
  7.1 12.0 %collective-permute-start.1 = (bf16[272,384]{1,0:T(8,128)(2,1)S(1)}, bf16[272,384]{1,0:T(8,128)(2,1)S(1)}, u32[]{:S(2)}, u32[]{:S(2)}) collective-permute-start(bf16[272,384]{1,0:T(8,128)(2,1)S(1)} %pad_maximum_fusion.5), channel_id=1, source_target_pairs={{0,8},{4,12},{8,24},{12,28},{16,0},{20,4},{24,16},{28,20},{1,9},{5... | collective-permute-start | bytes 626696 | tf_op jit(solution)/shard_map/x0/ppermute | solution.py:42
  8.1 16.0 %collective-permute-start.4 = (bf16[256,512]{1,0:T(8,128)(2,1)S(1)}, bf16[256,512]{1,0:T(8,128)(2,1)S(1)}, u32[]{:S(2)}, u32[]{:S(2)}) collective-permute-start(bf16[256,512]{1,0:T(8,128)(2,1)S(1)} %slice.268), channel_id=1, source_target_pairs={{0,16},{4,20},{8,0},{12,4},{16,24},{20,28},{24,8},{28,12},{1,17},{... | collective-permute-start | bytes 786440 | tf_op jit(solution)/shard_map/x1/ppermute | solution.py:42
  11.0 19.3 %collective-permute-start.5 = (bf16[256,512]{1,0:T(8,128)(2,1)S(1)}, bf16[256,512]{1,0:T(8,128)(2,1)S(1)}, u32[]{:S(2)}, u32[]{:S(2)}) collective-permute-start(bf16[256,512]{1,0:T(8,128)(2,1)S(1)} %slice.268), channel_id=1, source_target_pairs={{0,8},{4,12},{8,24},{12,28},{16,0},{20,4},{24,16},{28,20},{1,9},{5... | collective-permute-start | bytes 786440 | tf_op jit(solution)/shard_map/x1/ppermute | solution.py:42
  19.5 15.7 %collective-permute-start.2 = (bf16[144,384]{1,0:T(8,128)(2,1)S(1)}, bf16[144,384]{1,0:T(8,128)(2,1)S(1)}, u32[]{:S(2)}, u32[]{:S(2)}) collective-permute-start(bf16[144,384]{1,0:T(8,128)(2,1)S(1)} %slice.266), channel_id=1, source_target_pairs={{0,16},{4,20},{8,0},{12,4},{16,24},{20,28},{24,8},{28,12},{1,17},{... | collective-permute-start | bytes 331784 | tf_op jit(solution)/shard_map/x0/ppermute | solution.py:42
  20.0 15.2 %collective-permute-start.3 = (bf16[128,384]{1,0:T(8,128)(2,1)S(1)}, bf16[128,384]{1,0:T(8,128)(2,1)S(1)}, u32[]{:S(2)}, u32[]{:S(2)}) collective-permute-start(bf16[128,384]{1,0:T(8,128)(2,1)S(1)} %slice.267), channel_id=1, source_target_pairs={{0,8},{4,12},{8,24},{12,28},{16,0},{20,4},{24,16},{28,20},{1,9},{5... | collective-permute-start | bytes 294920 | tf_op jit(solution)/shard_map/x0/ppermute | solution.py:42
  22.3 18.7 %collective-permute-start.6 = (bf16[400,384]{1,0:T(8,128)(2,1)S(1)}, bf16[400,384]{1,0:T(8,128)(2,1)S(1)}, u32[]{:S(2)}, u32[]{:S(2)}) collective-permute-start(bf16[400,384]{1,0:T(8,128)(2,1)S(1)} %fusion.128), channel_id=1, source_target_pairs={{0,4},{4,0},{8,12},{12,8},{16,20},{20,16},{24,28},{28,24},{1,5},{5... | collective-permute-start | bytes 921608 | tf_op jit(solution)/shard_map/x0/ppermute | solution.py:174
  30.4 18.3 %collective-permute-start.10 = (bf16[128,512]{1,0:T(8,128)(2,1)S(1)}, bf16[128,512]{1,0:T(8,128)(2,1)S(1)}, u32[]{:S(2)}, u32[]{:S(2)}) collective-permute-start(bf16[128,512]{1,0:T(8,128)(2,1)S(1)} %slice.292), channel_id=1, source_target_pairs={{0,16},{4,20},{8,0},{12,4},{16,24},{20,28},{24,8},{28,12},{1,17},{... | collective-permute-start | bytes 393224 | tf_op jit(solution)/shard_map/x1/ppermute | solution.py:42
  30.9 19.4 %collective-permute-start.11 = (bf16[128,512]{1,0:T(8,128)(2,1)S(1)}, bf16[128,512]{1,0:T(8,128)(2,1)S(1)}, u32[]{:S(2)}, u32[]{:S(2)}) collective-permute-start(bf16[128,512]{1,0:T(8,128)(2,1)S(1)} %slice.293), channel_id=1, source_target_pairs={{0,8},{4,12},{8,24},{12,28},{16,0},{20,4},{24,16},{28,20},{1,9},{5... | collective-permute-start | bytes 393224 | tf_op jit(solution)/shard_map/x1/ppermute | solution.py:42
  35.6 15.4 %collective-permute-start.8 = (bf16[256,512]{1,0:T(8,128)(2,1)S(1)}, bf16[256,512]{1,0:T(8,128)(2,1)S(1)}, u32[]{:S(2)}, u32[]{:S(2)}) collective-permute-start(bf16[256,512]{1,0:T(8,128)(2,1)S(1)} %slice.291), channel_id=1, source_target_pairs={{0,16},{4,20},{8,0},{12,4},{16,24},{20,28},{24,8},{28,12},{1,17},{... | collective-permute-start | bytes 786440 | tf_op jit(solution)/shard_map/d0/ppermute | solution.py:42
  39.2 4.8 %collective-permute-start.7 = (bf16[144,384]{1,0:T(8,128)(2,1)S(1)}, bf16[144,384]{1,0:T(8,128)(2,1)S(1)}, u32[]{:S(2)}, u32[]{:S(2)}) collective-permute-start(bf16[144,384]{1,0:T(8,128)(2,1)S(1)} %fusion.154), channel_id=1, source_target_pairs={{0,4},{4,0},{8,12},{12,8},{16,20},{20,16},{24,28},{28,24},{1,5},{5... | collective-permute-start | bytes 331784 | tf_op jit(solution)/shard_map/x0/ppermute | solution.py:174
  41.1 10.5 %collective-permute-start.9 = (bf16[256,512]{1,0:T(8,128)(2,1)S(1)}, bf16[256,512]{1,0:T(8,128)(2,1)S(1)}, u32[]{:S(2)}, u32[]{:S(2)}) collective-permute-start(bf16[256,512]{1,0:T(8,128)(2,1)S(1)} %slice.291), channel_id=1, source_target_pairs={{0,8},{4,12},{8,24},{12,28},{16,0},{20,4},{24,16},{28,20},{1,9},{5... | collective-permute-start | bytes 786440 | tf_op jit(solution)/shard_map/d0/ppermute | solution.py:42
  44.0 10.3 %collective-permute-start.16 = (bf16[384,512]{1,0:T(8,128)(2,1)}, bf16[384,512]{1,0:T(8,128)(2,1)}, u32[]{:S(2)}, u32[]{:S(2)}) collective-permute-start(bf16[384,512]{1,0:T(8,128)(2,1)} %bitcast.30), channel_id=1, source_target_pairs={{0,4},{4,0},{8,12},{12,8},{16,20},{20,16},{24,28},{28,24},{1,5},{5... | collective-permute-start | bytes 1179656 | tf_op jit(solution)/shard_map/x1/ppermute | solution.py:174
  48.2 2.3 %copy-start = (bf16[1024,512]{1,0:T(8,128)(2,1)S(1)}, bf16[1024,512]{1,0:T(8,128)(2,1)}, u32[]{:S(2)}) copy-start(bf16[1024,512]{1,0:T(8,128)(2,1)} %constant_dynamic-update-slice_fusion.7) | copy-start | bytes 3145732
  48.7 11.8 %collective-permute-start.14 = (bf16[640,384]{1,0:T(8,128)(2,1)S(1)}, bf16[640,384]{1,0:T(8,128)(2,1)S(1)}, u32[]{:S(2)}, u32[]{:S(2)}) collective-permute-start(bf16[640,384]{1,0:T(8,128)(2,1)S(1)} %fusion.41), channel_id=1, source_target_pairs={{0,2},{1,3},{2,0},{3,1},{4,6},{5,7},{6,4},{7,5},{8,10},{9,11},{10,... | collective-permute-start | bytes 1474568 | tf_op jit(solution)/shard_map/x0/ppermute | solution.py:42
  50.3 20.9 %collective-permute-start.19 = (bf16[640,384]{1,0:T(8,128)(2,1)S(1)}, bf16[640,384]{1,0:T(8,128)(2,1)S(1)}, u32[]{:S(2)}, u32[]{:S(2)}) collective-permute-start(bf16[640,384]{1,0:T(8,128)(2,1)S(1)} %fusion.41), channel_id=1, source_target_pairs={{0,1},{1,0},{2,3},{3,2},{4,5},{5,4},{6,7},{7,6},{8,9},{9,8},{10,11... | collective-permute-start | bytes 1474568 | tf_op jit(solution)/shard_map/x0/ppermute | solution.py:42
  50.8 3.3 %copy-start.1 = (bf16[1024,512]{1,0:T(8,128)(2,1)S(1)}, bf16[1024,512]{1,0:T(8,128)(2,1)}, u32[]{:S(2)}) copy-start(bf16[1024,512]{1,0:T(8,128)(2,1)} %constant_dynamic-update-slice_fusion.4) | copy-start | bytes 3145732
  50.9 6.0 %collective-permute-start.15 = (bf16[128,512]{1,0:T(8,128)(2,1)S(1)}, bf16[128,512]{1,0:T(8,128)(2,1)S(1)}, u32[]{:S(2)}, u32[]{:S(2)}) collective-permute-start(bf16[128,512]{1,0:T(8,128)(2,1)S(1)} %convolution_convert_fusion.13), channel_id=1, source_target_pairs={{0,4},{4,0},{8,12},{12,8},{16,20},{20,16},{24,28},{28,24},{1,5},{5... | collective-permute-start | bytes 393224 | tf_op jit(solution)/shard_map/x1/ppermute | solution.py:174
  51.5 17.9 %collective-permute-start.20 = (bf16[256,384]{1,0:T(8,128)(2,1)S(1)}, bf16[256,384]{1,0:T(8,128)(2,1)S(1)}, u32[]{:S(2)}, u32[]{:S(2)}) collective-permute-start(bf16[256,384]{1,0:T(8,128)(2,1)S(1)} %slice.301), channel_id=1, source_target_pairs={{0,16},{4,20},{8,0},{12,4},{16,24},{20,28},{24,8},{28,12},{1,17},{... | collective-permute-start | bytes 589832 | tf_op jit(solution)/shard_map/d1/ppermute | solution.py:42
  54.3 16.7 %collective-permute-start.21 = (bf16[256,384]{1,0:T(8,128)(2,1)S(1)}, bf16[256,384]{1,0:T(8,128)(2,1)S(1)}, u32[]{:S(2)}, u32[]{:S(2)}) collective-permute-start(bf16[256,384]{1,0:T(8,128)(2,1)S(1)} %slice.301), channel_id=1, source_target_pairs={{0,8},{4,12},{8,24},{12,28},{16,0},{20,4},{24,16},{28,20},{1,9},{5... | collective-permute-start | bytes 589832 | tf_op jit(solution)/shard_map/d1/ppermute | solution.py:42
  56.9 9.3 %collective-permute-start.12 = (bf16[128,512]{1,0:T(8,128)(2,1)S(1)}, bf16[128,512]{1,0:T(8,128)(2,1)S(1)}, u32[]{:S(2)}, u32[]{:S(2)}) collective-permute-start(bf16[128,512]{1,0:T(8,128)(2,1)S(1)} %slice.294), channel_id=1, source_target_pairs={{0,16},{4,20},{8,0},{12,4},{16,24},{20,28},{24,8},{28,12},{1,17},{... | collective-permute-start | bytes 393224 | tf_op jit(solution)/shard_map/d0/ppermute | solution.py:42
  60.5 9.0 %collective-permute-start.13 = (bf16[128,512]{1,0:T(8,128)(2,1)S(1)}, bf16[128,512]{1,0:T(8,128)(2,1)S(1)}, u32[]{:S(2)}, u32[]{:S(2)}) collective-permute-start(bf16[128,512]{1,0:T(8,128)(2,1)S(1)} %slice.295), channel_id=1, source_target_pairs={{0,8},{4,12},{8,24},{12,28},{16,0},{20,4},{24,16},{28,20},{1,9},{5... | collective-permute-start | bytes 393224 | tf_op jit(solution)/shard_map/d0/ppermute | solution.py:42
  66.2 19.5 %collective-permute-start.27 = (bf16[640,512]{1,0:T(8,128)(2,1)S(1)}, bf16[640,512]{1,0:T(8,128)(2,1)S(1)}, u32[]{:S(2)}, u32[]{:S(2)}) collective-permute-start(bf16[640,512]{1,0:T(8,128)(2,1)S(1)} %fusion.39), channel_id=1, source_target_pairs={{0,2},{1,3},{2,0},{3,1},{4,6},{5,7},{6,4},{7,5},{8,10},{9,11},{10,... | collective-permute-start | bytes 1966088 | tf_op jit(solution)/shard_map/x1/ppermute | solution.py:42
  69.5 19.6 %collective-permute-start.31 = (bf16[640,512]{1,0:T(8,128)(2,1)S(1)}, bf16[640,512]{1,0:T(8,128)(2,1)S(1)}, u32[]{:S(2)}, u32[]{:S(2)}) collective-permute-start(bf16[640,512]{1,0:T(8,128)(2,1)S(1)} %fusion.39), channel_id=1, source_target_pairs={{0,1},{1,0},{2,3},{3,2},{4,5},{5,4},{6,7},{7,6},{8,9},{9,8},{10,11... | collective-permute-start | bytes 1966088 | tf_op jit(solution)/shard_map/x1/ppermute | solution.py:42
  69.5 11.9 %collective-permute-start.17 = (bf16[384,512]{1,0:T(8,128)(2,1)S(1)}, bf16[384,512]{1,0:T(8,128)(2,1)S(1)}, u32[]{:S(2)}, u32[]{:S(2)}) collective-permute-start(bf16[384,512]{1,0:T(8,128)(2,1)S(1)} %bitcast.224), channel_id=1, source_target_pairs={{0,4},{4,0},{8,12},{12,8},{16,20},{20,16},{24,28},{28,24},{1,5},{5... | collective-permute-start | bytes 1179656 | tf_op jit(solution)/shard_map/d0/ppermute | solution.py:174
  71.0 1.9 %collective-permute-start.18 = (bf16[640,384]{1,0:T(8,128)(2,1)S(1)}, bf16[640,384]{1,0:T(8,128)(2,1)S(1)}, u32[]{:S(2)}, u32[]{:S(2)}) collective-permute-start(bf16[640,384]{1,0:T(8,128)(2,1)S(1)} %collective-permute-done.14), channel_id=1, source_target_pairs={{0,1},{1,0},{2,3},{3,2},{4,5},{5,4},{6,7},{7,6},{8,9},{9,8},{10,11... | collective-permute-start | bytes 1474568 | tf_op jit(solution)/shard_map/x0/ppermute | solution.py:42
  71.4 12.4 %collective-permute-start.22 = (bf16[128,512]{1,0:T(8,128)(2,1)S(1)}, bf16[128,512]{1,0:T(8,128)(2,1)S(1)}, u32[]{:S(2)}, u32[]{:S(2)}) collective-permute-start(bf16[128,512]{1,0:T(8,128)(2,1)S(1)} %convolution_convert_fusion.12), channel_id=1, source_target_pairs={{0,4},{4,0},{8,12},{12,8},{16,20},{20,16},{24,28},{28,24},{1,5},{5... | collective-permute-start | bytes 393224 | tf_op jit(solution)/shard_map/d0/ppermute | solution.py:174
  72.9 12.8 %collective-permute-start.25 = (bf16[128,384]{1,0:T(8,128)(2,1)S(1)}, bf16[128,384]{1,0:T(8,128)(2,1)S(1)}, u32[]{:S(2)}, u32[]{:S(2)}) collective-permute-start(bf16[128,384]{1,0:T(8,128)(2,1)S(1)} %slice.303), channel_id=1, source_target_pairs={{0,16},{4,20},{8,0},{12,4},{16,24},{20,28},{24,8},{28,12},{1,17},{... | collective-permute-start | bytes 294920 | tf_op jit(solution)/shard_map/d1/ppermute | solution.py:42
  81.4 5.5 %collective-permute-start.26 = (bf16[128,384]{1,0:T(8,128)(2,1)S(1)}, bf16[128,384]{1,0:T(8,128)(2,1)S(1)}, u32[]{:S(2)}, u32[]{:S(2)}) collective-permute-start(bf16[128,384]{1,0:T(8,128)(2,1)S(1)} %slice.304), channel_id=1, source_target_pairs={{0,8},{4,12},{8,24},{12,28},{16,0},{20,4},{24,16},{28,20},{1,9},{5... | collective-permute-start | bytes 294920 | tf_op jit(solution)/shard_map/d1/ppermute | solution.py:42
  85.2 17.2 %collective-permute-start.24 = (bf16[640,512]{1,0:T(8,128)(2,1)S(1)}, bf16[640,512]{1,0:T(8,128)(2,1)S(1)}, u32[]{:S(2)}, u32[]{:S(2)}) collective-permute-start(bf16[640,512]{1,0:T(8,128)(2,1)S(1)} %fusion.42), channel_id=1, source_target_pairs={{0,2},{1,3},{2,0},{3,1},{4,6},{5,7},{6,4},{7,5},{8,10},{9,11},{10,... | collective-permute-start | bytes 1966088 | tf_op jit(solution)/shard_map/d0/ppermute | solution.py:42
  85.7 16.6 %collective-permute-start.23 = (bf16[640,512]{1,0:T(8,128)(2,1)S(1)}, bf16[640,512]{1,0:T(8,128)(2,1)S(1)}, u32[]{:S(2)}, u32[]{:S(2)}) collective-permute-start(bf16[640,512]{1,0:T(8,128)(2,1)S(1)} %fusion.42), channel_id=1, source_target_pairs={{0,1},{1,0},{2,3},{3,2},{4,5},{5,4},{6,7},{7,6},{8,9},{9,8},{10,11... | collective-permute-start | bytes 1966088 | tf_op jit(solution)/shard_map/d0/ppermute | solution.py:42
  86.9 9.3 %collective-permute-start.29 = (bf16[384,384]{1,0:T(8,128)(2,1)S(1)}, bf16[384,384]{1,0:T(8,128)(2,1)S(1)}, u32[]{:S(2)}, u32[]{:S(2)}) collective-permute-start(bf16[384,384]{1,0:T(8,128)(2,1)S(1)} %bitcast.225), channel_id=1, source_target_pairs={{0,4},{4,0},{8,12},{12,8},{16,20},{20,16},{24,28},{28,24},{1,5},{5... | collective-permute-start | bytes 884744 | tf_op jit(solution)/shard_map/d1/ppermute | solution.py:174
  88.4 2.1 %collective-permute-start.30 = (bf16[640,512]{1,0:T(8,128)(2,1)S(1)}, bf16[640,512]{1,0:T(8,128)(2,1)S(1)}, u32[]{:S(2)}, u32[]{:S(2)}) collective-permute-start(bf16[640,512]{1,0:T(8,128)(2,1)S(1)} %collective-permute-done.27), channel_id=1, source_target_pairs={{0,1},{1,0},{2,3},{3,2},{4,5},{5,4},{6,7},{7,6},{8,9},{9,8},{10,11... | collective-permute-start | bytes 1966088 | tf_op jit(solution)/shard_map/x1/ppermute | solution.py:42
  89.1 8.2 %collective-permute-start.28 = (bf16[128,384]{1,0:T(8,128)(2,1)S(1)}, bf16[128,384]{1,0:T(8,128)(2,1)S(1)}, u32[]{:S(2)}, u32[]{:S(2)}) collective-permute-start(bf16[128,384]{1,0:T(8,128)(2,1)S(1)} %convolution_convert_fusion.14), channel_id=1, source_target_pairs={{0,4},{4,0},{8,12},{12,8},{16,20},{20,16},{24,28},{28,24},{1,5},{5... | collective-permute-start | bytes 294920 | tf_op jit(solution)/shard_map/d1/ppermute | solution.py:174
  97.3 5.3 %slice-start = ((s8[4358144]{0:T(1024)(128)(4,1)}), s8[4194304]{0:T(1024)(128)(4,1)S(1)}, s32[]{:S(2)}) async-start(s8[4358144]{0:T(1024)(128)(4,1)} %bitcast.193), calls=%async_computation | async-start | bytes 8388608
  97.8 4.8 %slice-start.1 = ((s8[4358144]{0:T(1024)(128)(4,1)}), s8[163840]{0:T(1024)(128)(4,1)S(1)}, s32[]{:S(2)}) async-start(s8[4358144]{0:T(1024)(128)(4,1)} %bitcast.193), calls=%async_computation.1 | async-start | bytes 327680
  98.6 13.5 %collective-permute-start.34 = (bf16[640,384]{1,0:T(8,128)(2,1)S(1)}, bf16[640,384]{1,0:T(8,128)(2,1)S(1)}, u32[]{:S(2)}, u32[]{:S(2)}) collective-permute-start(bf16[640,384]{1,0:T(8,128)(2,1)S(1)} %fusion.45), channel_id=1, source_target_pairs={{0,2},{1,3},{2,0},{3,1},{4,6},{5,7},{6,4},{7,5},{8,10},{9,11},{10,... | collective-permute-start | bytes 1474568 | tf_op jit(solution)/shard_map/d1/ppermute | solution.py:42
  100.3 11.9 %collective-permute-start.33 = (bf16[640,384]{1,0:T(8,128)(2,1)S(1)}, bf16[640,384]{1,0:T(8,128)(2,1)S(1)}, u32[]{:S(2)}, u32[]{:S(2)}) collective-permute-start(bf16[640,384]{1,0:T(8,128)(2,1)S(1)} %fusion.45), channel_id=1, source_target_pairs={{0,1},{1,0},{2,3},{3,2},{4,5},{5,4},{6,7},{7,6},{8,9},{9,8},{10,11... | collective-permute-start | bytes 1474568 | tf_op jit(solution)/shard_map/d1/ppermute | solution.py:42
  102.4 3.8 %collective-permute-start.32 = (bf16[640,512]{1,0:T(8,128)(2,1)S(1)}, bf16[640,512]{1,0:T(8,128)(2,1)S(1)}, u32[]{:S(2)}, u32[]{:S(2)}) collective-permute-start(bf16[640,512]{1,0:T(8,128)(2,1)S(1)} %collective-permute-done.24), channel_id=1, source_target_pairs={{0,1},{1,0},{2,3},{3,2},{4,5},{5,4},{6,7},{7,6},{8,9},{9,8},{10,11... | collective-permute-start | bytes 1966088 | tf_op jit(solution)/shard_map/d0/ppermute | solution.py:42
  102.5 11.6 %slice-start.2 = ((s8[4358144]{0:T(1024)(128)(4,1)}), s8[4194304]{0:T(1024)(128)(4,1)S(1)}, s32[]{:S(2)}) async-start(s8[4358144]{0:T(1024)(128)(4,1)} %bitcast.222), calls=%async_computation.2 | async-start | bytes 8388608
  102.6 11.5 %slice-start.3 = ((s8[4358144]{0:T(1024)(128)(4,1)}), s8[163840]{0:T(1024)(128)(4,1)S(1)}, s32[]{:S(2)}) async-start(s8[4358144]{0:T(1024)(128)(4,1)} %bitcast.222), calls=%async_computation.3 | async-start | bytes 327680
  112.1 1.9 collective-permute-start.35
  120.7 3.6 %collective-permute-start.36 = (bf16[1280,512]{1,0:T(8,128)(2,1)S(1)}, bf16[1280,512]{1,0:T(8,128)(2,1)S(1)}, u32[]{:S(2)}, u32[]{:S(2)}) collective-permute-start(bf16[1280,512]{1,0:T(8,128)(2,1)S(1)} %pad_maximum_fusion), channel_id=1, source_target_pairs={{0,1},{1,0},{2,3},{3,2},{4,5},{5,4},{6,7},{7,6},{8,9},{9,8},{10,11... | collective-permute-start | bytes 3932168 | tf_op jit(solution)/shard_map/g0/ppermute | solution.py:42
  121.0 5.0 %collective-permute-start.38 = (bf16[1280,384]{1,0:T(8,128)(2,1)S(1)}, bf16[1280,384]{1,0:T(8,128)(2,1)S(1)}, u32[]{:S(2)}, u32[]{:S(2)}) collective-permute-start(bf16[1280,384]{1,0:T(8,128)(2,1)S(1)} %pad_maximum_fusion.1), channel_id=1, source_target_pairs={{0,1},{1,0},{2,3},{3,2},{4,5},{5,4},{6,7},{7,6},{8,9},{9,8},{10,11... | collective-permute-start | bytes 2949128 | tf_op jit(solution)/shard_map/g1/ppermute | solution.py:42
  125.0 17.6 %collective-permute-start.37 = (bf16[640,512]{1,0:T(8,128)(2,1)S(1)}, bf16[640,512]{1,0:T(8,128)(2,1)S(1)}, u32[]{:S(2)}, u32[]{:S(2)}) collective-permute-start(bf16[640,512]{1,0:T(8,128)(2,1)S(1)} %slice.433), channel_id=1, source_target_pairs={{0,2},{1,3},{2,0},{3,1},{4,6},{5,7},{6,4},{7,5},{8,10},{9,11},{10,... | collective-permute-start | bytes 1966088 | tf_op jit(solution)/shard_map/g0/ppermute | solution.py:42
  126.2 26.2 %collective-permute-start.40 = (bf16[640,384]{1,0:T(8,128)(2,1)S(1)}, bf16[640,384]{1,0:T(8,128)(2,1)S(1)}, u32[]{:S(2)}, u32[]{:S(2)}) collective-permute-start(bf16[640,384]{1,0:T(8,128)(2,1)S(1)} %slice.434), channel_id=1, source_target_pairs={{0,2},{1,3},{2,0},{3,1},{4,6},{5,7},{6,4},{7,5},{8,10},{9,11},{10,... | collective-permute-start | bytes 1474568 | tf_op jit(solution)/shard_map/g1/ppermute | solution.py:42
  143.3 13.4 %collective-permute-start.39 = (bf16[512,512]{1,0:T(8,128)(2,1)S(1)}, bf16[512,512]{1,0:T(8,128)(2,1)S(1)}, u32[]{:S(2)}, u32[]{:S(2)}) collective-permute-start(bf16[512,512]{1,0:T(8,128)(2,1)S(1)} %fusion.32), channel_id=1, source_target_pairs={{0,4},{4,0},{8,12},{12,8},{16,20},{20,16},{24,28},{28,24},{1,5},{5... | collective-permute-start | bytes 1572872 | tf_op jit(solution)/shard_map/g0/ppermute | solution.py:174
  153.0 11.1 %collective-permute-start.43 = (bf16[512,384]{1,0:T(8,128)(2,1)S(1)}, bf16[512,384]{1,0:T(8,128)(2,1)S(1)}, u32[]{:S(2)}, u32[]{:S(2)}) collective-permute-start(bf16[512,384]{1,0:T(8,128)(2,1)S(1)} %fusion.40), channel_id=1, source_target_pairs={{0,4},{4,0},{8,12},{12,8},{16,20},{20,16},{24,28},{28,24},{1,5},{5... | collective-permute-start | bytes 1179656 | tf_op jit(solution)/shard_map/g1/ppermute | solution.py:174
  157.2 9.5 %collective-permute-start.41 = (bf16[128,512]{1,0:T(8,128)(2,1)S(1)}, bf16[128,512]{1,0:T(8,128)(2,1)S(1)}, u32[]{:S(2)}, u32[]{:S(2)}) collective-permute-start(bf16[128,512]{1,0:T(8,128)(2,1)S(1)} %get-tuple-element.233), channel_id=1, source_target_pairs={{0,16},{4,20},{8,0},{12,4},{16,24},{20,28},{24,8},{28,12},{1,17},{... | collective-permute-start | bytes 393224 | tf_op jit(solution)/shard_map/g0/ppermute | solution.py:42
  157.8 8.9 %collective-permute-start.42 = (bf16[128,512]{1,0:T(8,128)(2,1)S(1)}, bf16[128,512]{1,0:T(8,128)(2,1)S(1)}, u32[]{:S(2)}, u32[]{:S(2)}) collective-permute-start(bf16[128,512]{1,0:T(8,128)(2,1)S(1)} %get-tuple-element.234), channel_id=1, source_target_pairs={{0,8},{4,12},{8,24},{12,28},{16,0},{20,4},{24,16},{28,20},{1,9},{5... | collective-permute-start | bytes 393224 | tf_op jit(solution)/shard_map/g0/ppermute | solution.py:42
  164.6 6.8 %collective-permute-start.46 = (bf16[128,384]{1,0:T(8,128)(2,1)S(1)}, bf16[128,384]{1,0:T(8,128)(2,1)S(1)}, u32[]{:S(2)}, u32[]{:S(2)}) collective-permute-start(bf16[128,384]{1,0:T(8,128)(2,1)S(1)} %get-tuple-element.244), channel_id=1, source_target_pairs={{0,16},{4,20},{8,0},{12,4},{16,24},{20,28},{24,8},{28,12},{1,17},{... | collective-permute-start | bytes 294920 | tf_op jit(solution)/shard_map/g1/ppermute | solution.py:42
  165.2 12.4 %collective-permute-start.47 = (bf16[128,384]{1,0:T(8,128)(2,1)S(1)}, bf16[128,384]{1,0:T(8,128)(2,1)S(1)}, u32[]{:S(2)}, u32[]{:S(2)}) collective-permute-start(bf16[128,384]{1,0:T(8,128)(2,1)S(1)} %get-tuple-element.245), channel_id=1, source_target_pairs={{0,8},{4,12},{8,24},{12,28},{16,0},{20,4},{24,16},{28,20},{1,9},{5... | collective-permute-start | bytes 294920 | tf_op jit(solution)/shard_map/g1/ppermute | solution.py:42
  166.8 24.9 %collective-permute-start.44 = (bf16[256,512]{1,0:T(8,128)(2,1)S(1)}, bf16[256,512]{1,0:T(8,128)(2,1)S(1)}, u32[]{:S(2)}, u32[]{:S(2)}) collective-permute-start(bf16[256,512]{1,0:T(8,128)(2,1)S(1)} %pad_maximum_fusion.3), channel_id=1, source_target_pairs={{0,16},{4,20},{8,0},{12,4},{16,24},{20,28},{24,8},{28,12},{1,17},{... | collective-permute-start | bytes 786440 | tf_op jit(solution)/shard_map/g0/ppermute | solution.py:42
  168.3 23.4 %collective-permute-start.45 = (bf16[256,512]{1,0:T(8,128)(2,1)S(1)}, bf16[256,512]{1,0:T(8,128)(2,1)S(1)}, u32[]{:S(2)}, u32[]{:S(2)}) collective-permute-start(bf16[256,512]{1,0:T(8,128)(2,1)S(1)} %pad_maximum_fusion.4), channel_id=1, source_target_pairs={{0,8},{4,12},{8,24},{12,28},{16,0},{20,4},{24,16},{28,20},{1,9},{5... | collective-permute-start | bytes 786440 | tf_op jit(solution)/shard_map/g0/ppermute | solution.py:42
  177.7 10.1 %collective-permute-start.48 = (bf16[256,384]{1,0:T(8,128)(2,1)S(1)}, bf16[256,384]{1,0:T(8,128)(2,1)S(1)}, u32[]{:S(2)}, u32[]{:S(2)}) collective-permute-start(bf16[256,384]{1,0:T(8,128)(2,1)S(1)} %pad_maximum_fusion.7), channel_id=1, source_target_pairs={{0,16},{4,20},{8,0},{12,4},{16,24},{20,28},{24,8},{28,12},{1,17},{... | collective-permute-start | bytes 589832 | tf_op jit(solution)/shard_map/g1/ppermute | solution.py:42
  177.8 13.9 %collective-permute-start.49 = (bf16[256,384]{1,0:T(8,128)(2,1)S(1)}, bf16[256,384]{1,0:T(8,128)(2,1)S(1)}, u32[]{:S(2)}, u32[]{:S(2)}) collective-permute-start(bf16[256,384]{1,0:T(8,128)(2,1)S(1)} %pad_maximum_fusion.8), channel_id=1, source_target_pairs={{0,8},{4,12},{8,24},{12,28},{16,0},{20,4},{24,16},{28,20},{1,9},{5... | collective-permute-start | bytes 589832 | tf_op jit(solution)/shard_map/g1/ppermute | solution.py:42

commit v3 on v2

v3 whole, which is shorter than its diff:
```python
import functools
import math

import jax
import jax.numpy as jnp
from jax import lax
from jax.experimental import pallas as pl
from jax.experimental.pallas import tpu as pltpu
from jax.sharding import PartitionSpec as P

BF = jnp.bfloat16
F32 = jnp.float32
ORDER = [
    "x0", "x1", "x0", "x0", "x1", "x0", "d0", "x1", "x1", "x0", "d0", "d0", "d1", "x1", "d0", "x0",
    "d1", "x0", "d0", "d1", "d1", "x1", "d1", "x1", "d0", "d0", "h", "d1", "d1",
]
HEAD = 16
COST = {"leave": 300, "places": 300, "pick": 60, "slots": 300, "terms": 300}
BACK = [
    "g0", "g1", "g0", "g2", "g1", "g2", "w", "w", "u", "u", "g0", "g0", "g0", "g1", "g2", "g1",
    "g0", "g1", "g2", "g2", "g0", "g1", "g2", "g2", "g1",
]
PINS = [
    "d0A", "d1A", "g1B", "g2C",
]


def ring_order(count):
    if count <= 4:
        return list(range(0, count, 2)) + list(range(1, count, 2))[::-1]
    return list(range(count))


def lookup(table, index):
    return sum(jnp.where(index == i, jnp.int32(v), jnp.int32(0)) for i, v in enumerate(table))


class Ring:
    def __init__(self, axis, size, count, stride):
        self.axis, self.count, self.stride = axis, count, stride
        self.order = ring_order(count)
        self.half = count // 2
        spot = {c: i for i, c in enumerate(self.order)}
        self.perms = {}
        for step in (1, -1):
            pairs = []
            for index in range(size):
                c = (index // stride) % count
                there = self.order[(spot[c] + step) % count]
                pairs.append((index, index + (there - c) * stride))
            self.perms[step] = pairs
        self.spot = [spot[c] for c in range(count)]

    def send(self, value, step):
        return lax.ppermute(value, self.axis, self.perms[step])

    def coordinate(self, mine, offset):
        place = lookup(self.spot, mine)
        return lookup(self.order, lax.rem(place + offset + self.count, self.count))

    def offsets(self):
        found = [0]
        for d in range(1, self.half):
            found += [-d, d]
        return found + ([self.half] if self.count > 1 else [])

    def near(self, line, value):
        blocks = {0: value}
        up = down = value
        for d in range(1, self.half):
            up, down = self.send(up, 1), self.send(down, -1)
            yield
            up, down = line.done(up, down)
            blocks[-d], blocks[d] = up, down
        return [blocks[o] for o in self.offsets() if o in blocks]

    def far(self, line, blocks, cut):
        if self.count == 1:
            return []
        if self.count == 2:
            got = self.send(blocks[0], 1)
            yield
            return [line.done(got)]
        up, down = line.go(blocks[-2][:cut], blocks[-1][cut:])
        up, down = self.send(up, 1), self.send(down, -1)
        yield
        return list(line.done(up, down))

    def gather(self, line, value, cut):
        blocks = yield from self.near(line, value)
        far = yield from self.far(line, blocks, cut)
        return blocks + ([jnp.concatenate(far, axis=0)] if len(far) > 1 else far)

    def reduce(self, line, far, near):
        if self.count == 1:
            return near()[0]
        if self.count == 2:
            got = self.send(line.go(*far()), 1)
            yield
            return near()[0] + line.done(got).astype(F32)
        up, down = line.go(*far())
        cut = up.shape[0]
        up, down = self.send(up, 1), self.send(down, -1)
        yield
        term = near()
        for d in range(self.half - 1, 0, -1):
            up, down = line.done(up, down)
            up, down = up.astype(F32), down.astype(F32)
            up_sum, down_sum = term[d], term[-d]
            if d == self.half - 1:
                up_sum = jnp.concatenate([up_sum[:cut] + up, up_sum[cut:]], axis=0)
                down_sum = jnp.concatenate([down_sum[:cut], down_sum[cut:] + down], axis=0)
            else:
                up_sum, down_sum = up_sum + up, down_sum + down
            up, down = line.go(up_sum.astype(BF), down_sum.astype(BF))
            up, down = self.send(up, 1), self.send(down, -1)
            yield
        up, down = line.done(up, down)
        return term[0] + up.astype(F32) + down.astype(F32)

    def halves(self, term, cut):
        return [term] if self.count == 2 else [term[:cut], term[cut:]]


class Line:
    def __init__(self):
        self.mark = jnp.zeros((8, 128), F32)

    def go(self, *values):
        out = lax.optimization_barrier((*values, self.mark))
        return out[0] if len(values) == 1 else out[:-1]

    def pin(self, value, label):
        return self.done(value) if label in PINS else self.go(value)

    def done(self, *values):
        out = lax.optimization_barrier((*values, self.mark))
        self.mark = out[-1]
        return out[0] if len(values) == 1 else out[:-1]


def run(parts, order, results):
    def step(name):
        if name not in results:
            try:
                with jax.named_scope(name):
                    next(parts[name])
            except StopIteration as end:
                results[name] = end.value

    for name in order:
        step(name)
    while len(results) < len(parts):
        for name in parts:
            step(name)


def kernel_call(kind, body, outs, scalars, *arrays):
    vmem, smem = pl.BlockSpec(memory_space=pltpu.VMEM), pl.BlockSpec(memory_space=pltpu.SMEM)
    many = isinstance(outs, (list, tuple))
    return pl.pallas_call(
        body,
        out_shape=outs,
        in_specs=[smem] * len(scalars) + [vmem] * len(arrays),
        out_specs=[vmem] * len(outs) if many else vmem,
        compiler_params=pltpu.CompilerParams(vmem_limit_bytes=32 * 2**20),
        cost_estimate=pl.CostEstimate(
            flops=COST[kind] * 10**8, bytes_accessed=COST[kind] * 10**5, transcendentals=0
        ),
    )(*scalars, *arrays)


def shape(rows, columns, dtype=BF):
    return jax.ShapeDtypeStruct((rows, columns), dtype)


class Blocks:
    def __init__(self):
        self.arrays, self.parts = [], []

    def add(self, pieces, skip):
        found = []
        for k, piece in enumerate(pieces):
            lead = skip if k == 0 else 0
            found.append((len(self.arrays), lead, piece.shape[0] - lead))
            self.arrays.append(piece)
        self.parts.append(found)

    def joined(self, other):
        both = Blocks()
        both.arrays = self.arrays + other.arrays
        both.parts = self.parts + [
            [(a + len(self.arrays), r, n) for a, r, n in found] for found in other.parts
        ]
        return both


def rows_dot(onehot, refs, parts):
    total, at = 0.0, 0
    for number, first, count in parts:
        total += jnp.dot(
            onehot[:, at : at + count],
            refs[number][first : first + count, :],
            preferred_element_type=F32,
        )
        at += count
    return total


def matches(lines, expert, top):
    hit = weight = 0.0
    for k in range(top):
        same = lines[k : k + 1] == expert
        hit += jnp.where(same, 1.0, 0.0)
        weight += jnp.where(same, lines[top + k : top + k + 1], 0.0)
    return hit, weight


def stack_rows(rows, height):
    index = lax.broadcasted_iota(jnp.int32, (height, rows[0].shape[1]), 0)
    total = 0.0
    for i, row in enumerate(rows):
        total += jnp.where(index == i, jnp.broadcast_to(row, index.shape), 0.0)
    return total


def ranks_in_group(hits):
    tok = hits.shape[1]
    before = lax.broadcasted_iota(jnp.int32, (tok, tok), 0)
    after = lax.broadcasted_iota(jnp.int32, (tok, tok), 1)
    below = jnp.where(before < after, 1.0, 0.0).astype(BF)
    return jnp.dot(hits.astype(BF), below, preferred_element_type=F32)


def leave_kernel(blocks, metas, tok, top, slot, scaled, expert_ref, *refs):
    refs, out = refs[:-1], refs[-1]
    expert = expert_ref[0].astype(F32)
    found = []
    for number, first in metas:
        lines = refs[number][first : first + HEAD, :tok].astype(F32)
        found.append(matches(lines, expert, top))
    local = ranks_in_group(stack_rows([h for h, _ in found], HEAD))
    place = lax.broadcasted_iota(jnp.int32, (slot, tok), 0).astype(F32)
    for i, parts in enumerate(blocks.parts):
        hit, weight = found[i]
        rank = jnp.where(hit > 0.0, local[i : i + 1], -1.0)
        value = weight if scaled else hit
        onehot = jnp.where(place == rank, value, 0.0).astype(BF)
        out[i * slot : (i + 1) * slot, :] = rows_dot(onehot, refs, parts).astype(BF)


def places_kernel(spots, tok, top, slot, own, nx, *refs):
    experts, earlier_ref = refs[:nx], refs[nx]
    refs, (rank_ref, weight_ref, in_ref, out_ref) = refs[nx + 1 : -4], refs[-4:]
    expert = experts[0][0].astype(F32)
    height = earlier_ref.shape[0]
    found = []
    for number, first in spots:
        lines = refs[number][first : first + 2 * top, :tok].astype(F32)
        found.append(matches(lines, expert, top))
    hits = stack_rows([h for h, _ in found], height)
    local = ranks_in_group(hits)
    count = jnp.broadcast_to(jnp.sum(hits, axis=1, keepdims=True), (height, 128))
    base = jnp.dot(earlier_ref[...], count.astype(BF), preferred_element_type=F32)
    lane = lax.broadcasted_iota(jnp.int32, (1, slot), 1).astype(F32)
    for i, (hit, weight) in enumerate(found):
        start = base[i : i + 1, :1]
        if i < own:
            rank_ref[i : i + 1, :] = jnp.where(hit > 0.0, local[i : i + 1] + start, -1.0)
            weight_ref[i : i + 1, :] = weight
        else:
            there = jnp.where(lane < count[i : i + 1, :1], start + lane, -1.0)
            in_ref[i - own : i - own + 1, :] = there
    for dx in range(1, nx):
        rows = []
        for number, first in spots[:own]:
            lines = refs[number][first : first + 2 * top, :tok].astype(F32)
            rows.append(matches(lines, experts[dx][0].astype(F32), top)[0])
        hits = stack_rows(rows, height)
        local = jnp.where(hits > 0.0, ranks_in_group(hits), -1.0)
        out_ref[(dx - 1) * own : dx * own, :] = local[:own]


def pick_kernel(blocks, backs, tok, slot, tile, scaled, rank_ref, weight_ref, in_ref, *refs):
    refs, out = refs[:-1], refs[-1]

    def step(number, carry):
        first = pl.multiple_of(number * tile, tile)

        def onehot(ranks, value, columns):
            place = lax.broadcasted_iota(jnp.int32, (tile, columns), 0) + first
            return jnp.where(place.astype(F32) == ranks, value, 0.0).astype(BF)

        total = 0.0
        for i, parts in enumerate(blocks.parts):
            value = weight_ref[i : i + 1, :] if scaled else 1.0
            total += rows_dot(onehot(rank_ref[i : i + 1, :], value, tok), refs, parts)
        for i, parts in enumerate(backs.parts):
            total += rows_dot(onehot(in_ref[i : i + 1, :], 1.0, slot), refs, parts)
        out[pl.ds(first, tile), :] = total.astype(BF)
        return carry

    lax.fori_loop(0, out.shape[0] // tile, step, 0)


def chosen(ranks, height):
    place = lax.broadcasted_iota(jnp.int32, (height, ranks.shape[1]), 0).astype(F32)
    return jnp.where(place == ranks, 1.0, 0.0).astype(BF)


def turned_dot(onehot, rows):
    return lax.dot_general(onehot, rows, (((0,), (0,)), ((), ())), preferred_element_type=F32)


def slots_kernel(first, slot, in_ref, total_ref, out_ref):
    total = total_ref[...]
    for i in range(out_ref.shape[0] // slot):
        onehot = chosen(in_ref[first + i : first + i + 1, :], total.shape[0])
        out_ref[i * slot : (i + 1) * slot, :] = turned_dot(onehot, total).astype(BF)


def terms_kernel(first, nz, slot, backs, rank_ref, slots_ref, total_ref, *refs):
    back_refs, outs = refs[:backs], refs[backs:]
    total = total_ref[...]
    for i, out in enumerate(outs):
        sum_ = turned_dot(chosen(rank_ref[first + i : first + i + 1, :], total.shape[0]), total)
        for k, back in enumerate(back_refs):
            line = k * nz + first + i
            rows = back[i * slot : (i + 1) * slot, :]
            sum_ += turned_dot(chosen(slots_ref[line : line + 1, :], slot), rows)
        out[...] = sum_.astype(out.dtype)


def unpick(onehot, rows):
    return lax.dot_general(onehot, rows, (((0,), (0,)), ((), ())), preferred_element_type=F32)


def silu_parts(hidden):
    sigma = jax.nn.sigmoid(hidden)
    return (hidden * sigma, sigma * (1.0 + hidden * (1.0 - sigma)))


def per_device(tokens, cotangent, up_weight, down_weight, expert_ids, gate_probs):
    tok, top = expert_ids.shape
    width = tokens.shape[1]
    n_exp, n_tp = lax.axis_size("exp"), lax.axis_size("tp")
    experts = n_exp * up_weight.shape[0]
    slot = min(4 * tok // experts, tok)
    capacity = 5 * tok * n_exp // (2 * experts)
    nx = 2 ** (int(math.log2(n_exp)) // 2)
    nz = n_exp // nx
    nc = 2 if n_tp % 2 == 0 else 1
    ny = n_tp // nc
    zring, yring, cring = (
        Ring("exp", n_exp, nz, nx),
        Ring("tp", n_tp, ny, nc),
        Ring("tp", n_tp, nc, 1),
    )
    e, t = lax.axis_index("exp"), lax.axis_index("tp")
    z, x, y, c = lax.div(e, nx), lax.rem(e, nx), lax.div(t, nc), lax.rem(t, nc)

    def cross(value, dx):
        pairs = [(i, i // nx * nx + (i % nx + dx) % nx) for i in range(n_exp)]
        return lax.ppermute(value, "exp", pairs)

    w_up, w_down = up_weight[0], down_weight[0]
    hid = w_up.shape[1]

    lanes = width // 128
    if width % 128 == 0 and lanes >= 4:
        small = lanes * 3 // 7 * 128
        cuts = {"x": [width - small, small], "d": [width - small, small]}
    else:
        cuts = {"x": [width], "d": [width]}

    meta = jnp.concatenate([expert_ids.astype(BF).T, gate_probs.T], axis=0)
    lines = 2 * top
    swaps = [cross(meta, dx) for dx in range(1, nx)]

    def headed(rows, piece):
        rows = jnp.pad(rows, ((0, HEAD - rows.shape[0]), (0, piece.shape[1] - tok)))
        return jnp.concatenate([rows, piece], axis=0)

    line = Line()
    shared = {}
    half = capacity // 2
    tile = math.gcd(capacity, 128)
    zs = [zring.coordinate(z, o) for o in zring.offsets()]
    columns = [lax.rem(x - dx + nx, nx) for dx in range(nx)]
    number = jnp.stack([zc * nx + xc for xc in columns for zc in zs])
    high = -(-n_exp // 16) * 16
    earlier = (number[None, :] < number[:, None]).astype(BF)
    earlier = jnp.pad(earlier, ((0, high - n_exp), (0, high - n_exp)))
    me = jnp.reshape(e, (1,)).astype(jnp.int32)
    over = [jnp.reshape(z * nx + lax.rem(x + dx, nx), (1,)).astype(jnp.int32) for dx in range(1, nx)]

    def leave(blocks, metas, scaled, label):
        arrays = blocks.arrays + [m for m, _ in metas]
        spots = [(len(blocks.arrays) + k, first) for k, (_, first) in enumerate(metas)]
        backs = []
        for dx in range(1, nx):
            body = functools.partial(leave_kernel, blocks, spots, tok, top, slot, scaled)
            out = shape(len(blocks.parts) * slot, blocks.arrays[0].shape[1])
            sent = kernel_call("leave", body, out, [over[dx - 1]], *arrays)
            backs.append(cross(line.pin(sent, label), dx))
        return backs

    def places():
        arrays = shared["own"] + shared["others"]
        spots = [(i, 0) for i in range(nz)]
        for dx in range(1, nx):
            spots += [(nz + i, (dx - 1) * lines) for i in range(nz)]
        body = functools.partial(places_kernel, spots, tok, top, slot, nz, nx)
        many = max(1, nx - 1) * nz
        outs = [shape(nz, tok, F32), shape(nz, tok, F32), shape(many, slot, F32), shape(many, tok, F32)]
        *shared["places"], shared["slots"] = kernel_call("places", body, outs, [me] + over, earlier, *arrays)

    def fetch(source, lo, hi, scaled, number, label):
        skip = HEAD if number < 2 else 0
        piece = source[:, lo:hi]
        if number == 0:
            piece = headed(meta, piece)
        if number == 1:
            others = [line.done(g) for g in swaps]
            piece = headed(jnp.concatenate(others, axis=0) if others else meta, piece)
        piece = line.go(piece)
        near = yield from zring.near(line, piece)
        far = zring.far(line, near, skip + tok // 2)
        opposite = []
        try:
            next(far)
        except StopIteration as end:
            opposite = end.value
        yield
        blocks = Blocks()
        for b in near:
            blocks.add([b], skip)
        if number == 0:
            shared["own"] = list(near)
        if number == 1:
            shared["others"] = list(near)
        metas = [(m, 0) for m in shared["own"][: len(near)]]
        backs = [leave(blocks, metas, scaled, label + "A")]
        yield
        if nz > 1:
            try:
                next(far)
            except StopIteration as end:
                opposite = end.value
            if number == 0:
                shared["own"].append(opposite[0])
            if number == 1:
                shared["others"].append(opposite[0])
            last = Blocks()
            last.add(opposite, skip)
            backs.append(leave(last, [(shared["own"][-1], 0)], scaled, label + "B"))
            blocks = blocks.joined(last)
            yield
        backs = [[line.done(g) for g in group] for group in backs]
        if "places" not in shared:
            places()
        arrived = Blocks()
        for dx in range(1, nx):
            for group in backs:
                at = len(arrived.arrays)
                arrived.arrays.append(group[dx - 1])
                for r in range(0, group[dx - 1].shape[0], slot):
                    arrived.parts.append([(at, r, slot)])
        shifted = blocks.joined(arrived)
        arrived.parts = shifted.parts[len(blocks.parts) :]
        body = functools.partial(pick_kernel, blocks, arrived, tok, slot, tile, scaled)
        part = kernel_call("pick", body, shape(capacity, hi - lo), [], *shared["places"], *shifted.arrays)
        part = line.pin(part, label + "P")
        cores = [cring.gather(line, part, half)]
        if nc > 1:
            next(cores[0])
        ys = yring.gather(line, part, half)
        pieces = []
        try:
            next(ys)
            yield
            while True:
                next(ys)
                yield
        except StopIteration as end:
            by_y = end.value
        cores += [cring.gather(line, b, half) for b in by_y[1:]]
        for g in cores[1:]:
            if nc > 1:
                next(g)
        yield
        for oy, g in zip(yring.offsets(), cores):
            try:
                while True:
                    next(g)
            except StopIteration as end:
                for oc, b in zip(cring.offsets(), end.value):
                    index = yring.coordinate(y, oy) * nc + cring.coordinate(c, oc)
                    pieces.append((index * width + lo, b))
        return pieces

    parts = {}
    for name, source in (("x", tokens), ("d", cotangent)):
        lo = 0
        for k, w in enumerate(cuts[name]):
            parts[name + str(k)] = fetch(
                source, lo, lo + w, name == "d", len(parts), name + str(k)
            )
            lo += w
    def assembled(names):
        whole = jnp.zeros((capacity, n_tp * width), BF)
        for name in names:
            for column, piece in done[name]:
                whole = lax.dynamic_update_slice(whole, piece, (0, column))
        return whole

    def first_half():
        names = [name for name in parts if name[0] == "x"]
        while any(name not in done for name in names):
            yield
        inputs = assembled(names)
        hidden = jnp.dot(inputs, w_up, preferred_element_type=F32)
        return inputs, line.done(hidden)

    done = {}
    parts["h"] = first_half()
    order = ORDER if (nz, nx, ny, nc, len(parts)) == (4, 2, 2, 2, 5) else []
    run(parts, order, done)

    inputs, hidden = done["h"]
    routed = assembled([name for name in parts if name[0] == "d"])
    act_full, slope = silu_parts(hidden)
    act = act_full.astype(BF)
    d_act = lax.dot_general(routed, w_down, (((1,), (1,)), ((), ())), preferred_element_type=F32)
    d_hidden = (d_act * slope).astype(BF)
    d_hidden = line.done(d_hidden)

    rank, weight, there = shared["places"]
    taken = shared["slots"]

    def give(lo, hi, label):
        w = hi - lo

        def term(oy, oc):
            index = yring.coordinate(y, oy) * nc + cring.coordinate(c, oc)
            part = lax.dynamic_slice(w_up, (index * width + lo, 0), (w, hid))
            return lax.dot_general(
                line.go(d_hidden), part, (((1,), (1,)), ((), ())), preferred_element_type=F32
            )

        def of_core(oc):
            return jnp.concatenate([term(oy, oc) for oy in yring.offsets()], axis=0)

        if nc > 1:
            other = cring.send(line.pin(of_core(1).astype(BF), label + "C"), 1)
            yield
            summed = of_core(0) + line.done(other).astype(F32)
        else:
            summed = of_core(0)
        summed = summed.reshape(ny, capacity, w)
        by_y = dict(zip(yring.offsets(), [summed[i] for i in range(ny)]))
        total = yield from yring.reduce(
            line, lambda: [p.astype(BF) for p in yring.halves(by_y[yring.half], half)], lambda: by_y
        )
        total = total.astype(BF)

        def across(first, groups):
            backs = []
            for dx in range(1, nx):
                body = functools.partial(slots_kernel, (dx - 1) * nz + first, slot)
                out = kernel_call("slots", body, shape(groups * slot, w), [], there, total)
                backs.append(cross(line.pin(out, label + "AB"[first > 0]), -dx))
            return backs

        def terms(first, groups, backs, kind):
            backs = [line.done(b) for b in backs]
            body = functools.partial(terms_kernel, first, nz, slot, len(backs))
            outs = [shape(tok, w, kind)] * groups
            return kernel_call("terms", body, outs, [], rank, taken, total, *backs)

        far_backs = across(nz - 1, 1) if nz > 1 else []
        if far_backs:
            yield
        near_backs = across(0, max(1, nz - 1))
        if near_backs:
            yield

        def far():
            return zring.halves(terms(nz - 1, 1, far_backs, BF)[0], tok // 2)

        def near():
            found = terms(0, max(1, nz - 1), near_backs, F32)
            return dict(zip(zring.offsets(), found))

        result = yield from zring.reduce(line, far, near)
        return result.astype(BF)

    if width % 128 == 0 and lanes >= 6:
        third = lanes // 3 * 128
        back_cuts = [width - 2 * third, third, third]
    else:
        back_cuts = [width]
    parts, lo = {}, 0
    for k, w in enumerate(back_cuts):
        parts["g%d" % k] = give(lo, lo + w, "g%d" % k)
        lo += w
    def weights(left, right):
        yield
        return line.done(unpick(line.go(left), right).astype(BF))

    parts["u"], parts["w"] = weights(d_hidden, inputs), weights(act, routed)
    order = BACK if (nz, nx, ny, nc, len(parts)) == (4, 2, 2, 2, 5) else []
    got = {}
    run(parts, order, got)
    results = [got["g%d" % k] for k in range(len(back_cuts))]
    grad_up, grad_down = got["u"].T, got["w"]
    token_grad = jnp.concatenate(results, axis=1)
    return (token_grad, grad_up[None], grad_down[None])


def solution(mesh):
    placed = (
        P("exp", "tp"),
        P("exp", "tp"),
        P("exp", None, "tp"),
        P("exp", "tp", None),
        P("exp", None),
        P("exp", None),
    )
    return jax.shard_map(
        per_device,
        mesh=mesh,
        in_specs=placed,
        out_specs=(P("exp", "tp"), P("exp", None, "tp"), P("exp", "tp", None)),
        check_vma=False,
    )
```

time: 193 us -> 183 us (0.948)
  waiting for transfers between devices: 88.7 us -> 62.8 us
  Pallas kernels: 0 us -> 19.6 us
  starting transfers between devices: 47.6 us -> 63.4 us
  matrix products: 37.8 us -> 24.2 us
  local copies, waits for them, and re-layouts: 10.6 us -> 6.92 us
  other arithmetic: 6.34 us -> 3.98 us
    pallas_call x0 -> x25, Pallas kernels: none -> 19.6 us  [kernel_call(): pl.pallas_call(body, out_shape=outs, in_specs=[smem] * len(scalars) + [vm...]
    ppermute x40 -> x46, waiting for transfers between devices: 63 us -> 45.7 us  [send(): return lax.ppermute(value, self.axis, self.perms[step])]
    ppermute x40 -> x46, starting transfers between devices: 35.1 us -> 45.3 us  [send(): return lax.ppermute(value, self.axis, self.perms[step])]
    dot_general x29 -> x13, matrix products: 20.2 us -> 10.1 us  [the longest x12 6.5 us: term(): lax.dot_general(line.go(d_hidden), part, (((1,), (1,)), ((), ())), prefer...]
    ppermute x10 -> x15, waiting for transfers between devices: 25.7 us -> 17.1 us  [cross(): return lax.ppermute(value, 'exp', pairs)]
    ppermute x10 -> x15, starting transfers between devices: 12.5 us -> 18.1 us  [cross(): return lax.ppermute(value, 'exp', pairs)]
    dot_general x6 -> x2, matrix products: 13.8 us -> 10.5 us  [unpick(): lax.dot_general(onehot, rows, (((0,), (0,)), ((), ())), preferred_element...]
    unnamed x28 -> x14, local copies, waits for them, and re-layouts: 3.11 us -> 0.35 us
  transfers between devices with their start and end apart: 50 -> 61, of which waited for: 22 -> 26; matrix products, arithmetic and copies ran while one was open for 23% -> 14% of each run, Pallas kernels for 0% -> 11%
where the time goes in v3:
time: 183 us
  starting transfers between devices  63.4 us (35%)
  waiting for transfers between devices  62.8 us (34%)
  matrix products  24.2 us (13%)
  Pallas kernels  19.6 us (11%)
  local copies, waits for them, and re-layouts  6.92 us (4%)
  other arithmetic  3.98 us (2%)
    ppermute x46, waiting for transfers between devices, send(): return lax.ppermute(value, self.axis, self.perms[step])  45.7 us
    ppermute x46, starting transfers between devices, send(): return lax.ppermute(value, self.axis, self.perms[step])  45.3 us
    pallas_call x25, Pallas kernels, kernel_call(): pl.pallas_call(body, out_shape=outs, in_specs=[smem] * len(scalars) + [vm...  19.6 us
    ppermute x15, starting transfers between devices, cross(): return lax.ppermute(value, 'exp', pairs)  18.1 us
    ppermute x15, waiting for transfers between devices, cross(): return lax.ppermute(value, 'exp', pairs)  17.1 us
    dot_general x2, matrix products, unpick(): lax.dot_general(onehot, rows, (((0,), (0,)), ((), ())), preferred_element...  10.5 us
    dot_general x12, matrix products, term(): lax.dot_general(line.go(d_hidden), part, (((1,), (1,)), ((), ())), prefer...  6.5 us
    slice x4, local copies, waits for them, and re-layouts, fetch(): piece = source[:, lo:hi]  4.51 us
  transfers between devices with their start and end apart: 61, of which 26 were waited for; matrix products, arithmetic and copies ran while one was open for 14% of the time, Pallas kernels for 11%

profile of v3, /device:TPU:0, one launch (start us, length us, event | category | flops | bytes accessed | tf_op | source)
XLA Modules:
  0.0 182.7 jit_solution(1191685959160133213)
XLA Ops:
  1.3 1.0 slice.123
  3.0 4.1 %collective-permute-start = (bf16[272,512]{1,0:T(8,128)(2,1)S(1)}, bf16[272,512]{1,0:T(8,128)(2,1)S(1)}, u32[]{:S(2)}, u32[]{:S(2)}) collective-permute-start(bf16[272,512]{1,0:T(8,128)(2,1)S(1)} %fusion.41.refs_3_.refs_0_), channel_id=1, source_target_pairs={{0,16},{4,20},{8,0},{12,4},{16,24},{20,28},{24,8},{28,12},{1,17},{... | collective-permute-start | bytes 835592 | tf_op jit(solution)/shard_map/x0/ppermute | solution.py:55
  7.1 1.5 collective-permute-start.2
  8.6 0.9 slice.126
  9.7 1.0 collective-permute-done.2
  10.7 3.0 %collective-permute-start.5 = (bf16[272,384]{1,0:T(8,128)(2,1)S(1)}, bf16[272,384]{1,0:T(8,128)(2,1)S(1)}, u32[]{:S(2)}, u32[]{:S(2)}) collective-permute-start(bf16[272,384]{1,0:T(8,128)(2,1)S(1)} %fusion.42.refs_7_.refs_0_), channel_id=1, source_target_pairs={{0,16},{4,20},{8,0},{12,4},{16,24},{20,28},{24,8},{28,12},{1,17},{... | collective-permute-start | bytes 626696 | tf_op jit(solution)/shard_map/x1/ppermute | solution.py:55
  13.8 1.0 slice.129.refs_0_
  14.7 1.6 slice.132.refs_0_
  16.4 5.7 %collective-permute-done.1.refs_5_.refs_2_ = bf16[272,512]{1,0:T(8,128)(2,1)S(1)} collective-permute-done((bf16[272,512]{1,0:T(8,128)(2,1)S(1)}, bf16[272,512]{1,0:T(8,128)(2,1)S(1)}, u32[]{:S(2)}, u32[]{:S(2)}) %collective-permute-start.1) | collective-permute-done | bytes 278560 | tf_op jit(solution)/shard_map/x0/ppermute | solution.py:55
  22.6 1.6 collective-permute-start.4
  24.7 6.4 %collective-permute-done.6.refs_9_.refs_2_ = bf16[272,384]{1,0:T(8,128)(2,1)S(1)} collective-permute-done((bf16[272,384]{1,0:T(8,128)(2,1)S(1)}, bf16[272,384]{1,0:T(8,128)(2,1)S(1)}, u32[]{:S(2)}, u32[]{:S(2)}) %collective-permute-start.6) | collective-permute-done | bytes 208928 | tf_op jit(solution)/shard_map/x1/ppermute | solution.py:55
  32.4 1.6 collective-permute-start.8
  34.0 1.5 collective-permute-start.12
  35.5 1.0 collective-permute-done.4.refs_1_.refs_4_
  36.5 1.1 collective-permute-start.10
  37.6 1.8 collective-permute-start.9
  40.4 1.5 collective-permute-start.11
  43.1 2.6 %collective-permute-done.12.refs_5_ = bf16[384,512]{1,0:T(8,128)(2,1)S(1)} collective-permute-done((bf16[384,512]{1,0:T(8,128)(2,1)S(1)}, bf16[384,512]{1,0:T(8,128)(2,1)S(1)}, u32[]{:S(2)}, u32[]{:S(2)}) %collective-permute-start.12) | collective-permute-done | bytes 393248 | tf_op jit(solution)/shard_map/x0/ppermute | solution.py:364
  45.7 1.5 collective-permute-start.15
  47.2 1.3 collective-permute-done.11.refs_6_
  48.5 2.4 %x0.7 = bf16[640,512]{1,0:T(8,128)(2,1)S(1)} custom-call(f32[4,256]{1,0:T(4,128)S(1)} %get-tuple-element.205.rank_ref, f32[4,256]{1,0:T(4,128)S(1)} %get-tuple-element.207.weight_ref, f32[4,128]{1,0:T(4,128)S(1)} %get-tuple-element.208.in_ref, bf16[272,512]{1,0:T(8,128)(2,1)S(1)} %fusion.41.refs_3_.refs_0_, ...), custom_call_target="tpu_custom_call" | custom-call | flops 6000000000 | bytes 6000000 | tf_op jit(solution)/shard_map/x0/pallas_call | solution.py:161
  50.9 1.6 collective-permute-start.18
  53.4 1.8 collective-permute-start.13
  55.8 2.3 %collective-permute-start.21 = (bf16[256,384]{1,0:T(8,128)(2,1)S(1)}, bf16[256,384]{1,0:T(8,128)(2,1)S(1)}, u32[]{:S(2)}, u32[]{:S(2)}) collective-permute-start(bf16[256,384]{1,0:T(8,128)(2,1)S(1)} %copy-done), channel_id=1, source_target_pairs={{0,16},{4,20},{8,0},{12,4},{16,24},{20,28},{24,8},{28,12},{1,17},{... | collective-permute-start | bytes 589832 | tf_op jit(solution)/shard_map/d1/ppermute | solution.py:55
  58.1 2.2 %x1.5 = bf16[640,384]{1,0:T(8,128)(2,1)S(1)} custom-call(f32[4,256]{1,0:T(4,128)S(1)} %get-tuple-element.205.rank_ref, f32[4,256]{1,0:T(4,128)S(1)} %get-tuple-element.207.weight_ref, f32[4,128]{1,0:T(4,128)S(1)} %get-tuple-element.208.in_ref, bf16[272,384]{1,0:T(8,128)(2,1)S(1)} %fusion.42.refs_7_.refs_0_, ...), custom_call_target="tpu_custom_call" | custom-call | flops 6000000000 | bytes 6000000 | tf_op jit(solution)/shard_map/x1/pallas_call | solution.py:161
  60.4 2.2 %collective-permute-start.22 = (bf16[256,384]{1,0:T(8,128)(2,1)S(1)}, bf16[256,384]{1,0:T(8,128)(2,1)S(1)}, u32[]{:S(2)}, u32[]{:S(2)}) collective-permute-start(bf16[256,384]{1,0:T(8,128)(2,1)S(1)} %copy-done), channel_id=1, source_target_pairs={{0,8},{4,12},{8,24},{12,28},{16,0},{20,4},{24,16},{28,20},{1,9},{5... | collective-permute-start | bytes 589832 | tf_op jit(solution)/shard_map/d1/ppermute | solution.py:55
  62.6 2.3 %collective-permute-done.14.refs_1_.refs_4_ = bf16[128,512]{1,0:T(8,128)(2,1)S(1)} collective-permute-done((bf16[128,512]{1,0:T(8,128)(2,1)S(1)}, bf16[128,512]{1,0:T(8,128)(2,1)S(1)}, u32[]{:S(2)}, u32[]{:S(2)}) %collective-permute-start.14) | collective-permute-done | bytes 131104 | tf_op jit(solution)/shard_map/d0/ppermute | solution.py:55
  64.9 1.5 collective-permute-start.17
  67.4 5.5 %collective-permute-done.22.refs_2_ = bf16[256,384]{1,0:T(8,128)(2,1)S(1)} collective-permute-done((bf16[256,384]{1,0:T(8,128)(2,1)S(1)}, bf16[256,384]{1,0:T(8,128)(2,1)S(1)}, u32[]{:S(2)}, u32[]{:S(2)}) %collective-permute-start.22) | collective-permute-done | bytes 196640 | tf_op jit(solution)/shard_map/d1/ppermute | solution.py:55
  73.2 1.6 collective-permute-start.23
  75.8 1.2 collective-permute-start.28
  77.0 2.2 %collective-permute-done.23.refs_6_ = bf16[128,512]{1,0:T(8,128)(2,1)S(1)} collective-permute-done((bf16[128,512]{1,0:T(8,128)(2,1)S(1)}, bf16[128,512]{1,0:T(8,128)(2,1)S(1)}, u32[]{:S(2)}, u32[]{:S(2)}) %collective-permute-start.23) | collective-permute-done | bytes 131104 | tf_op jit(solution)/shard_map/d0/ppermute | solution.py:364
  79.2 2.4 %d0.5 = bf16[640,512]{1,0:T(8,128)(2,1)S(1)} custom-call(f32[4,256]{1,0:T(4,128)S(1)} %get-tuple-element.205.rank_ref, f32[4,256]{1,0:T(4,128)S(1)} %get-tuple-element.207.weight_ref, f32[4,128]{1,0:T(4,128)S(1)} %get-tuple-element.208.in_ref, bf16[256,512]{1,0:T(8,128)(2,1)S(1)} %slice.129.refs_0_, bf16[256,512]{1,0:T(8,128)(2,1)S(1)} %collective-permute-done.9.refs_1_, ...), custom_call_target="tpu_custom_call" | custom-call | flops 6000000000 | bytes 6000000 | tf_op jit(solution)/shard_map/d0/pallas_call | solution.py:161
  82.2 1.5 collective-permute-start.32
  85.3 6.8 %collective-permute-done.32.refs_5_ = bf16[384,384]{1,0:T(8,128)(2,1)S(1)} collective-permute-done((bf16[384,384]{1,0:T(8,128)(2,1)S(1)}, bf16[384,384]{1,0:T(8,128)(2,1)S(1)}, u32[]{:S(2)}, u32[]{:S(2)}) %collective-permute-start.32) | collective-permute-done | bytes 294944 | tf_op jit(solution)/shard_map/d1/ppermute | solution.py:364
  92.1 1.6 collective-permute-done.31.refs_6_
  93.8 2.3 %d1.5 = bf16[640,384]{1,0:T(8,128)(2,1)S(1)} custom-call(f32[4,256]{1,0:T(4,128)S(1)} %get-tuple-element.205.rank_ref, f32[4,256]{1,0:T(4,128)S(1)} %get-tuple-element.207.weight_ref, f32[4,128]{1,0:T(4,128)S(1)} %get-tuple-element.208.in_ref, bf16[256,384]{1,0:T(8,128)(2,1)S(1)} %copy-done, bf16[256,384]{1,0:T(8,128)(2,1)S(1)} %collective-permute-done.21.refs_1_, ...), custom_call_target="tpu_custom_call" | custom-call | flops 6000000000 | bytes 6000000 | tf_op jit(solution)/shard_map/d1/pallas_call | solution.py:161
  96.1 1.5 collective-permute-start.35
  98.6 3.6 %fusion.2 = f32[640,608]{0,1:T(8,128)S(1)} fusion(bf16[640,3584]{1,0:T(8,128)(2,1)S(1)} %constant_dynamic-update-slice_fusion.3, bf16[1,3584,608]{1,2,0:T(8,128)(2,1)S(1)} %bitcast.80), kind=kOutput, calls=%fused_computation.4 | convolution fusion | flops 2789212160 | bytes 10502144 | tf_op jit(solution)/shard_map/h/dot_general | solution.py:522
  102.3 6.7 %collective-permute-done.35 = bf16[640,384]{1,0:T(8,128)(2,1)S(1)} collective-permute-done((bf16[640,384]{1,0:T(8,128)(2,1)S(1)}, bf16[640,384]{1,0:T(8,128)(2,1)S(1)}, u32[]{:S(2)}, u32[]{:S(2)}) %collective-permute-start.35) | collective-permute-done | bytes 491552 | tf_op jit(solution)/shard_map/d1/ppermute | solution.py:55
  109.7 1.1 collective-permute-done.36
  110.9 3.7 %multiply_convert_fusion.1 = bf16[640,608]{0,1:T(8,128)(2,1)S(1)} fusion(f32[640,608]{0,1:T(8,128)S(1)} %fusion.2, bf16[640,3584]{1,0:T(8,128)(2,1)S(1)} %constant_dynamic-update-slice_fusion, bf16[1,608,3584]{2,1,0:T(8,128)(2,1)S(1)} %bitcast.83), kind=kOutput, calls=%fused_computation.8 | convolution fusion | flops 2792714240 | bytes 11280384 | tf_op jit(solution)/shard_map/dot_general | solution.py:534
  120.6 1.6 collective-permute-start.38
  124.9 5.4 %convolution_convert_fusion.1 = bf16[608,3584]{1,0:T(8,128)(2,1)} fusion(bf16[640,608]{0,1:T(8,128)(2,1)S(1)} %multiply_convert_fusion, bf16[640,3584]{1,0:T(8,128)(2,1)S(1)} %constant_dynamic-update-slice_fusion), kind=kOutput, calls=%fused_computation.1 | convolution fusion | flops 2791391232 | bytes 9723904 | tf_op jit(solution)/shard_map/w/dot_general | solution.py:335
  130.2 5.1 %convolution_convert_fusion = bf16[608,3584]{1,0:T(8,128)(2,1)} fusion(bf16[640,608]{0,1:T(8,128)(2,1)S(1)} %multiply_convert_fusion.1, bf16[640,3584]{1,0:T(8,128)(2,1)S(1)} %constant_dynamic-update-slice_fusion.3), kind=kOutput, calls=%fused_computation | convolution fusion | flops 2791391232 | bytes 9723904 | tf_op jit(solution)/shard_map/u/dot_general | solution.py:335
  135.8 1.2 g0.4
  137.0 1.5 collective-permute-start.44
  138.7 1.6 collective-permute-start.42
  143.8 1.4 collective-permute-start.46
  145.2 1.8 collective-permute-start.50
  147.0 1.2 collective-permute-done.42
  148.9 1.5 collective-permute-start.49
  150.5 1.9 %g0.6 = (f32[256,384]{1,0:T(8,128)S(1)}, f32[256,384]{1,0:T(8,128)S(1)}, f32[256,384]{1,0:T(8,128)S(1)}) custom-call(f32[4,256]{1,0:T(4,128)S(1)} %copy-done.2, f32[4,256]{1,0:T(4,128)S(1)} %get-tuple-element.206.slots_ref, bf16[640,384]{1,0:T(8,128)(2,1)S(1)} %fusion.6.total_ref, bf16[384,384]{1,0:T(8,128)(2,1)} %collective-permute-done.41.refs_0_), custom_call_target="tpu_custom_call" | custom-call | flops 30000001024 | bytes 30000000 | tf_op jit(solution)/shard_map/g0/pallas_call | solution.py:161
  153.2 1.4 collective-permute-start.48
  155.8 2.5 %collective-permute-start.52 = (bf16[128,256]{1,0:T(8,128)(2,1)S(1)}, bf16[128,256]{1,0:T(8,128)(2,1)S(1)}, u32[]{:S(2)}, u32[]{:S(2)}) collective-permute-start(bf16[128,256]{1,0:T(8,128)(2,1)S(1)} %get-tuple-element.343), channel_id=1, source_target_pairs={{0,16},{4,20},{8,0},{12,4},{16,24},{20,28},{24,8},{28,12},{1,17},{... | collective-permute-start | bytes 196616 | tf_op jit(solution)/shard_map/g1/ppermute | solution.py:55
  158.6 5.9 %collective-permute-done.47 = bf16[256,384]{1,0:T(8,128)(2,1)S(1)} collective-permute-done((bf16[256,384]{1,0:T(8,128)(2,1)S(1)}, bf16[256,384]{1,0:T(8,128)(2,1)S(1)}, u32[]{:S(2)}, u32[]{:S(2)}) %collective-permute-start.47) | collective-permute-done | bytes 196640 | tf_op jit(solution)/shard_map/g0/ppermute | solution.py:55
  164.8 2.0 %collective-permute-start.58 = (bf16[128,256]{1,0:T(8,128)(2,1)S(1)}, bf16[128,256]{1,0:T(8,128)(2,1)S(1)}, u32[]{:S(2)}, u32[]{:S(2)}) collective-permute-start(bf16[128,256]{1,0:T(8,128)(2,1)S(1)} %get-tuple-element.360), channel_id=1, source_target_pairs={{0,8},{4,12},{8,24},{12,28},{16,0},{20,4},{24,16},{28,20},{1,9},{5... | collective-permute-start | bytes 196616 | tf_op jit(solution)/shard_map/g2/ppermute | solution.py:55
  167.6 1.0 collective-permute-start.54
  168.6 1.1 collective-permute-start.55
  170.2 2.1 %collective-permute-done.58 = bf16[128,256]{1,0:T(8,128)(2,1)S(1)} collective-permute-done((bf16[128,256]{1,0:T(8,128)(2,1)S(1)}, bf16[128,256]{1,0:T(8,128)(2,1)S(1)}, u32[]{:S(2)}, u32[]{:S(2)}) %collective-permute-start.58) | collective-permute-done | bytes 65568 | tf_op jit(solution)/shard_map/g2/ppermute | solution.py:55
  173.0 2.0 %collective-permute-start.60 = (bf16[256,256]{1,0:T(8,128)(2,1)S(1)}, bf16[256,256]{1,0:T(8,128)(2,1)S(1)}, u32[]{:S(2)}, u32[]{:S(2)}) collective-permute-start(bf16[256,256]{1,0:T(8,128)(2,1)S(1)} %pad_maximum_fusion.9), channel_id=1, source_target_pairs={{0,8},{4,12},{8,24},{12,28},{16,0},{20,4},{24,16},{28,20},{1,9},{5... | collective-permute-start | bytes 393224 | tf_op jit(solution)/shard_map/g2/ppermute | solution.py:55
  175.2 3.7 %collective-permute-done.55 = bf16[256,256]{1,0:T(8,128)(2,1)S(1)} collective-permute-done((bf16[256,256]{1,0:T(8,128)(2,1)S(1)}, bf16[256,256]{1,0:T(8,128)(2,1)S(1)}, u32[]{:S(2)}, u32[]{:S(2)}) %collective-permute-start.55) | collective-permute-done | bytes 131104 | tf_op jit(solution)/shard_map/g1/ppermute | solution.py:55
  178.9 1.5 collective-permute-done.59
  180.4 1.4 collective-permute-done.60
  (189 shorter events, 32.6 us)
Async XLA Ops:
  3.0 13.4 %collective-permute-start = (bf16[272,512]{1,0:T(8,128)(2,1)S(1)}, bf16[272,512]{1,0:T(8,128)(2,1)S(1)}, u32[]{:S(2)}, u32[]{:S(2)}) collective-permute-start(bf16[272,512]{1,0:T(8,128)(2,1)S(1)} %fusion.41.refs_3_.refs_0_), channel_id=1, source_target_pairs={{0,16},{4,20},{8,0},{12,4},{16,24},{20,28},{24,8},{28,12},{1,17},{... | collective-permute-start | bytes 835592 | tf_op jit(solution)/shard_map/x0/ppermute | solution.py:55
  7.1 15.0 %collective-permute-start.1 = (bf16[272,512]{1,0:T(8,128)(2,1)S(1)}, bf16[272,512]{1,0:T(8,128)(2,1)S(1)}, u32[]{:S(2)}, u32[]{:S(2)}) collective-permute-start(bf16[272,512]{1,0:T(8,128)(2,1)S(1)} %fusion.41.refs_3_.refs_0_), channel_id=1, source_target_pairs={{0,8},{4,12},{8,24},{12,28},{16,0},{20,4},{24,16},{28,20},{1,9},{5... | collective-permute-start | bytes 835592 | tf_op jit(solution)/shard_map/x0/ppermute | solution.py:55
  7.1 3.6 %collective-permute-start.2 = (bf16[4,256]{1,0:T(4,128)(2,1)S(1)}, bf16[4,256]{1,0:T(4,128)(2,1)S(1)}, u32[]{:S(2)}, u32[]{:S(2)}) collective-permute-start(bf16[4,256]{1,0:T(4,128)(2,1)S(1)} %pad_maximum_fusion.10), channel_id=1, source_target_pairs={{0,4},{4,0},{8,12},{12,8},{16,20},{20,16},{24,28},{28,24},{1,5},{5... | collective-permute-start | bytes 6152 | tf_op jit(solution)/shard_map/ppermute | solution.py:364
  10.7 14.0 %collective-permute-start.5 = (bf16[272,384]{1,0:T(8,128)(2,1)S(1)}, bf16[272,384]{1,0:T(8,128)(2,1)S(1)}, u32[]{:S(2)}, u32[]{:S(2)}) collective-permute-start(bf16[272,384]{1,0:T(8,128)(2,1)S(1)} %fusion.42.refs_7_.refs_0_), channel_id=1, source_target_pairs={{0,16},{4,20},{8,0},{12,4},{16,24},{20,28},{24,8},{28,12},{1,17},{... | collective-permute-start | bytes 626696 | tf_op jit(solution)/shard_map/x1/ppermute | solution.py:55
  13.7 17.4 %collective-permute-start.6 = (bf16[272,384]{1,0:T(8,128)(2,1)S(1)}, bf16[272,384]{1,0:T(8,128)(2,1)S(1)}, u32[]{:S(2)}, u32[]{:S(2)}) collective-permute-start(bf16[272,384]{1,0:T(8,128)(2,1)S(1)} %fusion.42.refs_7_.refs_0_), channel_id=1, source_target_pairs={{0,8},{4,12},{8,24},{12,28},{16,0},{20,4},{24,16},{28,20},{1,9},{5... | collective-permute-start | bytes 626696 | tf_op jit(solution)/shard_map/x1/ppermute | solution.py:55
  22.1 14.4 %collective-permute-start.3 = (bf16[144,512]{1,0:T(8,128)(2,1)S(1)}, bf16[144,512]{1,0:T(8,128)(2,1)S(1)}, u32[]{:S(2)}, u32[]{:S(2)}) collective-permute-start(bf16[144,512]{1,0:T(8,128)(2,1)S(1)} %slice.124), channel_id=1, source_target_pairs={{0,16},{4,20},{8,0},{12,4},{16,24},{20,28},{24,8},{28,12},{1,17},{... | collective-permute-start | bytes 442376 | tf_op jit(solution)/shard_map/x0/ppermute | solution.py:55
  22.6 13.9 %collective-permute-start.4 = (bf16[128,512]{1,0:T(8,128)(2,1)S(1)}, bf16[128,512]{1,0:T(8,128)(2,1)S(1)}, u32[]{:S(2)}, u32[]{:S(2)}) collective-permute-start(bf16[128,512]{1,0:T(8,128)(2,1)S(1)} %slice.125), channel_id=1, source_target_pairs={{0,8},{4,12},{8,24},{12,28},{16,0},{20,4},{24,16},{28,20},{1,9},{5... | collective-permute-start | bytes 393224 | tf_op jit(solution)/shard_map/x0/ppermute | solution.py:55
  31.9 10.0 %collective-permute-start.7 = (bf16[144,384]{1,0:T(8,128)(2,1)S(1)}, bf16[144,384]{1,0:T(8,128)(2,1)S(1)}, u32[]{:S(2)}, u32[]{:S(2)}) collective-permute-start(bf16[144,384]{1,0:T(8,128)(2,1)S(1)} %slice.127), channel_id=1, source_target_pairs={{0,16},{4,20},{8,0},{12,4},{16,24},{20,28},{24,8},{28,12},{1,17},{... | collective-permute-start | bytes 331784 | tf_op jit(solution)/shard_map/x1/ppermute | solution.py:55
  32.4 8.0 %collective-permute-start.8 = (bf16[128,384]{1,0:T(8,128)(2,1)S(1)}, bf16[128,384]{1,0:T(8,128)(2,1)S(1)}, u32[]{:S(2)}, u32[]{:S(2)}) collective-permute-start(bf16[128,384]{1,0:T(8,128)(2,1)S(1)} %slice.128), channel_id=1, source_target_pairs={{0,8},{4,12},{8,24},{12,28},{16,0},{20,4},{24,16},{28,20},{1,9},{5... | collective-permute-start | bytes 294920 | tf_op jit(solution)/shard_map/x1/ppermute | solution.py:55
  34.0 11.7 %collective-permute-start.12 = (bf16[384,512]{1,0:T(8,128)(2,1)S(1)}, bf16[384,512]{1,0:T(8,128)(2,1)S(1)}, u32[]{:S(2)}, u32[]{:S(2)}) collective-permute-start(bf16[384,512]{1,0:T(8,128)(2,1)S(1)} %x0.6), channel_id=1, source_target_pairs={{0,4},{4,0},{8,12},{12,8},{16,20},{20,16},{24,28},{28,24},{1,5},{5... | collective-permute-start | bytes 1179656 | tf_op jit(solution)/shard_map/x0/ppermute | solution.py:364
  36.5 16.4 %collective-permute-start.10 = (bf16[256,512]{1,0:T(8,128)(2,1)S(1)}, bf16[256,512]{1,0:T(8,128)(2,1)S(1)}, u32[]{:S(2)}, u32[]{:S(2)}) collective-permute-start(bf16[256,512]{1,0:T(8,128)(2,1)S(1)} %slice.129.refs_0_), channel_id=1, source_target_pairs={{0,8},{4,12},{8,24},{12,28},{16,0},{20,4},{24,16},{28,20},{1,9},{5... | collective-permute-start | bytes 786440 | tf_op jit(solution)/shard_map/d0/ppermute | solution.py:55
  37.6 15.3 %collective-permute-start.9 = (bf16[256,512]{1,0:T(8,128)(2,1)S(1)}, bf16[256,512]{1,0:T(8,128)(2,1)S(1)}, u32[]{:S(2)}, u32[]{:S(2)}) collective-permute-start(bf16[256,512]{1,0:T(8,128)(2,1)S(1)} %slice.129.refs_0_), channel_id=1, source_target_pairs={{0,16},{4,20},{8,0},{12,4},{16,24},{20,28},{24,8},{28,12},{1,17},{... | collective-permute-start | bytes 786440 | tf_op jit(solution)/shard_map/d0/ppermute | solution.py:55
  40.4 8.1 %collective-permute-start.11 = (bf16[128,512]{1,0:T(8,128)(2,1)S(1)}, bf16[128,512]{1,0:T(8,128)(2,1)S(1)}, u32[]{:S(2)}, u32[]{:S(2)}) collective-permute-start(bf16[128,512]{1,0:T(8,128)(2,1)S(1)} %x0.5), channel_id=1, source_target_pairs={{0,4},{4,0},{8,12},{12,8},{16,20},{20,16},{24,28},{28,24},{1,5},{5... | collective-permute-start | bytes 393224 | tf_op jit(solution)/shard_map/x0/ppermute | solution.py:364
  41.9 13.3 %collective-permute-start.16 = (bf16[384,384]{1,0:T(8,128)(2,1)S(1)}, bf16[384,384]{1,0:T(8,128)(2,1)S(1)}, u32[]{:S(2)}, u32[]{:S(2)}) collective-permute-start(bf16[384,384]{1,0:T(8,128)(2,1)S(1)} %x1.4), channel_id=1, source_target_pairs={{0,4},{4,0},{8,12},{12,8},{16,20},{20,16},{24,28},{28,24},{1,5},{5... | collective-permute-start | bytes 884744 | tf_op jit(solution)/shard_map/x1/ppermute | solution.py:364
  43.1 50.7 %copy-start.1 = (f32[4,256]{1,0:T(4,128)}, f32[4,256]{1,0:T(4,128)S(1)}, u32[]{:S(2)}) copy-start(f32[4,256]{1,0:T(4,128)S(1)} %get-tuple-element.205.rank_ref) | copy-start | bytes 12292
  45.7 10.1 %collective-permute-start.15 = (bf16[128,384]{1,0:T(8,128)(2,1)S(1)}, bf16[128,384]{1,0:T(8,128)(2,1)S(1)}, u32[]{:S(2)}, u32[]{:S(2)}) collective-permute-start(bf16[128,384]{1,0:T(8,128)(2,1)S(1)} %x1.3), channel_id=1, source_target_pairs={{0,4},{4,0},{8,12},{12,8},{16,20},{20,16},{24,28},{28,24},{1,5},{5... | collective-permute-start | bytes 294920 | tf_op jit(solution)/shard_map/x1/ppermute | solution.py:364
  50.9 15.8 %collective-permute-start.18 = (bf16[640,512]{1,0:T(8,128)(2,1)S(1)}, bf16[640,512]{1,0:T(8,128)(2,1)S(1)}, u32[]{:S(2)}, u32[]{:S(2)}) collective-permute-start(bf16[640,512]{1,0:T(8,128)(2,1)S(1)} %x0.7), channel_id=1, source_target_pairs={{0,2},{1,3},{2,0},{3,1},{4,6},{5,7},{6,4},{7,5},{8,10},{9,11},{10,... | collective-permute-start | bytes 1966088 | tf_op jit(solution)/shard_map/x0/ppermute | solution.py:55
  52.9 20.3 %collective-permute-start.20 = (bf16[640,512]{1,0:T(8,128)(2,1)S(1)}, bf16[640,512]{1,0:T(8,128)(2,1)S(1)}, u32[]{:S(2)}, u32[]{:S(2)}) collective-permute-start(bf16[640,512]{1,0:T(8,128)(2,1)S(1)} %x0.7), channel_id=1, source_target_pairs={{0,1},{1,0},{2,3},{3,2},{4,5},{5,4},{6,7},{7,6},{8,9},{9,8},{10,11... | collective-permute-start | bytes 1966088 | tf_op jit(solution)/shard_map/x0/ppermute | solution.py:55
  53.4 6.9 %collective-permute-start.13 = (bf16[128,512]{1,0:T(8,128)(2,1)S(1)}, bf16[128,512]{1,0:T(8,128)(2,1)S(1)}, u32[]{:S(2)}, u32[]{:S(2)}) collective-permute-start(bf16[128,512]{1,0:T(8,128)(2,1)S(1)} %slice.130), channel_id=1, source_target_pairs={{0,16},{4,20},{8,0},{12,4},{16,24},{20,28},{24,8},{28,12},{1,17},{... | collective-permute-start | bytes 393224 | tf_op jit(solution)/shard_map/d0/ppermute | solution.py:55
  55.2 9.7 %collective-permute-start.14 = (bf16[128,512]{1,0:T(8,128)(2,1)S(1)}, bf16[128,512]{1,0:T(8,128)(2,1)S(1)}, u32[]{:S(2)}, u32[]{:S(2)}) collective-permute-start(bf16[128,512]{1,0:T(8,128)(2,1)S(1)} %slice.131), channel_id=1, source_target_pairs={{0,8},{4,12},{8,24},{12,28},{16,0},{20,4},{24,16},{28,20},{1,9},{5... | collective-permute-start | bytes 393224 | tf_op jit(solution)/shard_map/d0/ppermute | solution.py:55
  55.8 11.5 %collective-permute-start.21 = (bf16[256,384]{1,0:T(8,128)(2,1)S(1)}, bf16[256,384]{1,0:T(8,128)(2,1)S(1)}, u32[]{:S(2)}, u32[]{:S(2)}) collective-permute-start(bf16[256,384]{1,0:T(8,128)(2,1)S(1)} %copy-done), channel_id=1, source_target_pairs={{0,16},{4,20},{8,0},{12,4},{16,24},{20,28},{24,8},{28,12},{1,17},{... | collective-permute-start | bytes 589832 | tf_op jit(solution)/shard_map/d1/ppermute | solution.py:55
  60.4 12.4 %collective-permute-start.22 = (bf16[256,384]{1,0:T(8,128)(2,1)S(1)}, bf16[256,384]{1,0:T(8,128)(2,1)S(1)}, u32[]{:S(2)}, u32[]{:S(2)}) collective-permute-start(bf16[256,384]{1,0:T(8,128)(2,1)S(1)} %copy-done), channel_id=1, source_target_pairs={{0,8},{4,12},{8,24},{12,28},{16,0},{20,4},{24,16},{28,20},{1,9},{5... | collective-permute-start | bytes 589832 | tf_op jit(solution)/shard_map/d1/ppermute | solution.py:55
  64.9 10.9 %collective-permute-start.17 = (bf16[384,512]{1,0:T(8,128)(2,1)S(1)}, bf16[384,512]{1,0:T(8,128)(2,1)S(1)}, u32[]{:S(2)}, u32[]{:S(2)}) collective-permute-start(bf16[384,512]{1,0:T(8,128)(2,1)S(1)} %d0.3), channel_id=1, source_target_pairs={{0,4},{4,0},{8,12},{12,8},{16,20},{20,16},{24,28},{28,24},{1,5},{5... | collective-permute-start | bytes 1179656 | tf_op jit(solution)/shard_map/d0/ppermute | solution.py:364
  66.8 17.7 %collective-permute-start.26 = (bf16[640,384]{1,0:T(8,128)(2,1)S(1)}, bf16[640,384]{1,0:T(8,128)(2,1)S(1)}, u32[]{:S(2)}, u32[]{:S(2)}) collective-permute-start(bf16[640,384]{1,0:T(8,128)(2,1)S(1)} %x1.5), channel_id=1, source_target_pairs={{0,2},{1,3},{2,0},{3,1},{4,6},{5,7},{6,4},{7,5},{8,10},{9,11},{10,... | collective-permute-start | bytes 1474568 | tf_op jit(solution)/shard_map/x1/ppermute | solution.py:55
  67.4 30.3 %collective-permute-start.30 = (bf16[640,384]{1,0:T(8,128)(2,1)S(1)}, bf16[640,384]{1,0:T(8,128)(2,1)S(1)}, u32[]{:S(2)}, u32[]{:S(2)}) collective-permute-start(bf16[640,384]{1,0:T(8,128)(2,1)S(1)} %x1.5), channel_id=1, source_target_pairs={{0,1},{1,0},{2,3},{3,2},{4,5},{5,4},{6,7},{7,6},{8,9},{9,8},{10,11... | collective-permute-start | bytes 1474568 | tf_op jit(solution)/shard_map/x1/ppermute | solution.py:55
  72.8 2.1 %collective-permute-start.19 = (bf16[640,512]{1,0:T(8,128)(2,1)S(1)}, bf16[640,512]{1,0:T(8,128)(2,1)S(1)}, u32[]{:S(2)}, u32[]{:S(2)}) collective-permute-start(bf16[640,512]{1,0:T(8,128)(2,1)S(1)} %collective-permute-done.18), channel_id=1, source_target_pairs={{0,1},{1,0},{2,3},{3,2},{4,5},{5,4},{6,7},{7,6},{8,9},{9,8},{10,11... | collective-permute-start | bytes 1966088 | tf_op jit(solution)/shard_map/x0/ppermute | solution.py:55
  73.2 6.0 %collective-permute-start.23 = (bf16[128,512]{1,0:T(8,128)(2,1)S(1)}, bf16[128,512]{1,0:T(8,128)(2,1)S(1)}, u32[]{:S(2)}, u32[]{:S(2)}) collective-permute-start(bf16[128,512]{1,0:T(8,128)(2,1)S(1)} %d0.4), channel_id=1, source_target_pairs={{0,4},{4,0},{8,12},{12,8},{16,20},{20,16},{24,28},{28,24},{1,5},{5... | collective-permute-start | bytes 393224 | tf_op jit(solution)/shard_map/d0/ppermute | solution.py:364
  75.0 7.3 %collective-permute-start.27 = (bf16[128,384]{1,0:T(8,128)(2,1)S(1)}, bf16[128,384]{1,0:T(8,128)(2,1)S(1)}, u32[]{:S(2)}, u32[]{:S(2)}) collective-permute-start(bf16[128,384]{1,0:T(8,128)(2,1)S(1)} %slice.133), channel_id=1, source_target_pairs={{0,16},{4,20},{8,0},{12,4},{16,24},{20,28},{24,8},{28,12},{1,17},{... | collective-permute-start | bytes 294920 | tf_op jit(solution)/shard_map/d1/ppermute | solution.py:55
  75.8 6.4 %collective-permute-start.28 = (bf16[128,384]{1,0:T(8,128)(2,1)S(1)}, bf16[128,384]{1,0:T(8,128)(2,1)S(1)}, u32[]{:S(2)}, u32[]{:S(2)}) collective-permute-start(bf16[128,384]{1,0:T(8,128)(2,1)S(1)} %slice.134), channel_id=1, source_target_pairs={{0,8},{4,12},{8,24},{12,28},{16,0},{20,4},{24,16},{28,20},{1,9},{5... | collective-permute-start | bytes 294920 | tf_op jit(solution)/shard_map/d1/ppermute | solution.py:55
  81.6 16.4 %collective-permute-start.25 = (bf16[640,512]{1,0:T(8,128)(2,1)S(1)}, bf16[640,512]{1,0:T(8,128)(2,1)S(1)}, u32[]{:S(2)}, u32[]{:S(2)}) collective-permute-start(bf16[640,512]{1,0:T(8,128)(2,1)S(1)} %d0.5), channel_id=1, source_target_pairs={{0,2},{1,3},{2,0},{3,1},{4,6},{5,7},{6,4},{7,5},{8,10},{9,11},{10,... | collective-permute-start | bytes 1966088 | tf_op jit(solution)/shard_map/d0/ppermute | solution.py:55
  82.2 19.9 %collective-permute-start.24 = (bf16[640,512]{1,0:T(8,128)(2,1)S(1)}, bf16[640,512]{1,0:T(8,128)(2,1)S(1)}, u32[]{:S(2)}, u32[]{:S(2)}) collective-permute-start(bf16[640,512]{1,0:T(8,128)(2,1)S(1)} %d0.5), channel_id=1, source_target_pairs={{0,1},{1,0},{2,3},{3,2},{4,5},{5,4},{6,7},{7,6},{8,9},{9,8},{10,11... | collective-permute-start | bytes 1966088 | tf_op jit(solution)/shard_map/d0/ppermute | solution.py:55
  82.2 9.9 %collective-permute-start.32 = (bf16[384,384]{1,0:T(8,128)(2,1)S(1)}, bf16[384,384]{1,0:T(8,128)(2,1)S(1)}, u32[]{:S(2)}, u32[]{:S(2)}) collective-permute-start(bf16[384,384]{1,0:T(8,128)(2,1)S(1)} %d1.3), channel_id=1, source_target_pairs={{0,4},{4,0},{8,12},{12,8},{16,20},{20,16},{24,28},{28,24},{1,5},{5... | collective-permute-start | bytes 884744 | tf_op jit(solution)/shard_map/d1/ppermute | solution.py:364
  84.5 9.3 %collective-permute-start.31 = (bf16[128,384]{1,0:T(8,128)(2,1)S(1)}, bf16[128,384]{1,0:T(8,128)(2,1)S(1)}, u32[]{:S(2)}, u32[]{:S(2)}) collective-permute-start(bf16[128,384]{1,0:T(8,128)(2,1)S(1)} %d1.4), channel_id=1, source_target_pairs={{0,4},{4,0},{8,12},{12,8},{16,20},{20,16},{24,28},{28,24},{1,5},{5... | collective-permute-start | bytes 294920 | tf_op jit(solution)/shard_map/d1/ppermute | solution.py:364
  85.2 13.4 %slice-start = ((s8[4358144]{0:T(1024)(128)(4,1)}), s8[4194304]{0:T(1024)(128)(4,1)S(1)}, s32[]{:S(2)}) async-start(s8[4358144]{0:T(1024)(128)(4,1)} %bitcast.79), calls=%async_computation | async-start | bytes 8388608
  85.3 13.3 %slice-start.1 = ((s8[4358144]{0:T(1024)(128)(4,1)}), s8[163840]{0:T(1024)(128)(4,1)S(1)}, s32[]{:S(2)}) async-start(s8[4358144]{0:T(1024)(128)(4,1)} %bitcast.79), calls=%async_computation.1 | async-start | bytes 327680
  92.1 5.7 %collective-permute-start.29 = (bf16[640,384]{1,0:T(8,128)(2,1)S(1)}, bf16[640,384]{1,0:T(8,128)(2,1)S(1)}, u32[]{:S(2)}, u32[]{:S(2)}) collective-permute-start(bf16[640,384]{1,0:T(8,128)(2,1)S(1)} %collective-permute-done.26), channel_id=1, source_target_pairs={{0,1},{1,0},{2,3},{3,2},{4,5},{5,4},{6,7},{7,6},{8,9},{9,8},{10,11... | collective-permute-start | bytes 1474568 | tf_op jit(solution)/shard_map/x1/ppermute | solution.py:55
  96.1 12.8 %collective-permute-start.35 = (bf16[640,384]{1,0:T(8,128)(2,1)S(1)}, bf16[640,384]{1,0:T(8,128)(2,1)S(1)}, u32[]{:S(2)}, u32[]{:S(2)}) collective-permute-start(bf16[640,384]{1,0:T(8,128)(2,1)S(1)} %d1.5), channel_id=1, source_target_pairs={{0,2},{1,3},{2,0},{3,1},{4,6},{5,7},{6,4},{7,5},{8,10},{9,11},{10,... | collective-permute-start | bytes 1474568 | tf_op jit(solution)/shard_map/d1/ppermute | solution.py:55
  97.7 11.3 %collective-permute-start.34 = (bf16[640,384]{1,0:T(8,128)(2,1)S(1)}, bf16[640,384]{1,0:T(8,128)(2,1)S(1)}, u32[]{:S(2)}, u32[]{:S(2)}) collective-permute-start(bf16[640,384]{1,0:T(8,128)(2,1)S(1)} %d1.5), channel_id=1, source_target_pairs={{0,1},{1,0},{2,3},{3,2},{4,5},{5,4},{6,7},{7,6},{8,9},{9,8},{10,11... | collective-permute-start | bytes 1474568 | tf_op jit(solution)/shard_map/d1/ppermute | solution.py:55
  98.0 4.2 %collective-permute-start.33 = (bf16[640,512]{1,0:T(8,128)(2,1)S(1)}, bf16[640,512]{1,0:T(8,128)(2,1)S(1)}, u32[]{:S(2)}, u32[]{:S(2)}) collective-permute-start(bf16[640,512]{1,0:T(8,128)(2,1)S(1)} %collective-permute-done.25), channel_id=1, source_target_pairs={{0,1},{1,0},{2,3},{3,2},{4,5},{5,4},{6,7},{7,6},{8,9},{9,8},{10,11... | collective-permute-start | bytes 1966088 | tf_op jit(solution)/shard_map/d0/ppermute | solution.py:55
  109.0 1.9 %collective-permute-start.36 = (bf16[640,384]{1,0:T(8,128)(2,1)S(1)}, bf16[640,384]{1,0:T(8,128)(2,1)S(1)}, u32[]{:S(2)}, u32[]{:S(2)}) collective-permute-start(bf16[640,384]{1,0:T(8,128)(2,1)S(1)} %collective-permute-done.35), channel_id=1, source_target_pairs={{0,1},{1,0},{2,3},{3,2},{4,5},{5,4},{6,7},{7,6},{8,9},{9,8},{10,11... | collective-permute-start | bytes 1474568 | tf_op jit(solution)/shard_map/d1/ppermute | solution.py:55
  116.1 3.0 %collective-permute-start.37 = (bf16[1280,384]{1,0:T(8,128)(2,1)S(1)}, bf16[1280,384]{1,0:T(8,128)(2,1)S(1)}, u32[]{:S(2)}, u32[]{:S(2)}) collective-permute-start(bf16[1280,384]{1,0:T(8,128)(2,1)S(1)} %pad_maximum_fusion), channel_id=1, source_target_pairs={{0,1},{1,0},{2,3},{3,2},{4,5},{5,4},{6,7},{7,6},{8,9},{9,8},{10,11... | collective-permute-start | bytes 2949128 | tf_op jit(solution)/shard_map/g0/ppermute | solution.py:55
  117.3 3.1 %collective-permute-start.40 = (bf16[1280,256]{1,0:T(8,128)(2,1)S(1)}, bf16[1280,256]{1,0:T(8,128)(2,1)S(1)}, u32[]{:S(2)}, u32[]{:S(2)}) collective-permute-start(bf16[1280,256]{1,0:T(8,128)(2,1)S(1)} %pad_maximum_fusion.2), channel_id=1, source_target_pairs={{0,1},{1,0},{2,3},{3,2},{4,5},{5,4},{6,7},{7,6},{8,9},{9,8},{10,11... | collective-permute-start | bytes 1966088 | tf_op jit(solution)/shard_map/g1/ppermute | solution.py:55
  120.2 4.7 %collective-permute-start.39 = (bf16[1280,256]{1,0:T(8,128)(2,1)S(1)}, bf16[1280,256]{1,0:T(8,128)(2,1)S(1)}, u32[]{:S(2)}, u32[]{:S(2)}) collective-permute-start(bf16[1280,256]{1,0:T(8,128)(2,1)S(1)} %pad_maximum_fusion.1), channel_id=1, source_target_pairs={{0,1},{1,0},{2,3},{3,2},{4,5},{5,4},{6,7},{7,6},{8,9},{9,8},{10,11... | collective-permute-start | bytes 1966088 | tf_op jit(solution)/shard_map/g2/ppermute | solution.py:55
  120.6 14.7 %collective-permute-start.38 = (bf16[640,384]{1,0:T(8,128)(2,1)S(1)}, bf16[640,384]{1,0:T(8,128)(2,1)S(1)}, u32[]{:S(2)}, u32[]{:S(2)}) collective-permute-start(bf16[640,384]{1,0:T(8,128)(2,1)S(1)} %slice.201), channel_id=1, source_target_pairs={{0,2},{1,3},{2,0},{3,1},{4,6},{5,7},{6,4},{7,5},{8,10},{9,11},{10,... | collective-permute-start | bytes 1474568 | tf_op jit(solution)/shard_map/g0/ppermute | solution.py:55
  123.3 18.3 %collective-permute-start.43 = (bf16[640,256]{1,0:T(8,128)(2,1)S(1)}, bf16[640,256]{1,0:T(8,128)(2,1)S(1)}, u32[]{:S(2)}, u32[]{:S(2)}) collective-permute-start(bf16[640,256]{1,0:T(8,128)(2,1)S(1)} %slice.202), channel_id=1, source_target_pairs={{0,2},{1,3},{2,0},{3,1},{4,6},{5,7},{6,4},{7,5},{8,10},{9,11},{10,... | collective-permute-start | bytes 983048 | tf_op jit(solution)/shard_map/g1/ppermute | solution.py:55
  137.0 4.6 %collective-permute-start.44 = (bf16[128,384]{1,0:T(8,128)(2,1)S(1)}, bf16[128,384]{1,0:T(8,128)(2,1)S(1)}, u32[]{:S(2)}, u32[]{:S(2)}) collective-permute-start(bf16[128,384]{1,0:T(8,128)(2,1)S(1)} %g0.5), channel_id=1, source_target_pairs={{0,4},{4,0},{8,12},{12,8},{16,20},{20,16},{24,28},{28,24},{1,5},{5... | collective-permute-start | bytes 294920 | tf_op jit(solution)/shard_map/g0/ppermute | solution.py:364
  138.7 9.5 %collective-permute-start.42 = (bf16[640,256]{1,0:T(8,128)(2,1)S(1)}, bf16[640,256]{1,0:T(8,128)(2,1)S(1)}, u32[]{:S(2)}, u32[]{:S(2)}) collective-permute-start(bf16[640,256]{1,0:T(8,128)(2,1)S(1)} %slice.203), channel_id=1, source_target_pairs={{0,2},{1,3},{2,0},{3,1},{4,6},{5,7},{6,4},{7,5},{8,10},{9,11},{10,... | collective-permute-start | bytes 983048 | tf_op jit(solution)/shard_map/g2/ppermute | solution.py:55
  140.3 10.2 %collective-permute-start.41 = (bf16[384,384]{1,0:T(8,128)(2,1)}, bf16[384,384]{1,0:T(8,128)(2,1)}, u32[]{:S(2)}, u32[]{:S(2)}) collective-permute-start(bf16[384,384]{1,0:T(8,128)(2,1)} %g0.4), channel_id=1, source_target_pairs={{0,4},{4,0},{8,12},{12,8},{16,20},{20,16},{24,28},{28,24},{1,5},{5... | collective-permute-start | bytes 884744 | tf_op jit(solution)/shard_map/g0/ppermute | solution.py:364
  143.2 7.3 %collective-permute-start.45 = (bf16[128,384]{1,0:T(8,128)(2,1)S(1)}, bf16[128,384]{1,0:T(8,128)(2,1)S(1)}, u32[]{:S(2)}, u32[]{:S(2)}) collective-permute-start(bf16[128,384]{1,0:T(8,128)(2,1)S(1)} %get-tuple-element.321), channel_id=1, source_target_pairs={{0,16},{4,20},{8,0},{12,4},{16,24},{20,28},{24,8},{28,12},{1,17},{... | collective-permute-start | bytes 294920 | tf_op jit(solution)/shard_map/g0/ppermute | solution.py:55
  143.8 6.7 %collective-permute-start.46 = (bf16[128,384]{1,0:T(8,128)(2,1)S(1)}, bf16[128,384]{1,0:T(8,128)(2,1)S(1)}, u32[]{:S(2)}, u32[]{:S(2)}) collective-permute-start(bf16[128,384]{1,0:T(8,128)(2,1)S(1)} %get-tuple-element.322), channel_id=1, source_target_pairs={{0,8},{4,12},{8,24},{12,28},{16,0},{20,4},{24,16},{28,20},{1,9},{5... | collective-permute-start | bytes 294920 | tf_op jit(solution)/shard_map/g0/ppermute | solution.py:55
  145.2 5.2 %collective-permute-start.50 = (bf16[128,256]{1,0:T(8,128)(2,1)S(1)}, bf16[128,256]{1,0:T(8,128)(2,1)S(1)}, u32[]{:S(2)}, u32[]{:S(2)}) collective-permute-start(bf16[128,256]{1,0:T(8,128)(2,1)S(1)} %g1.4), channel_id=1, source_target_pairs={{0,4},{4,0},{8,12},{12,8},{16,20},{20,16},{24,28},{28,24},{1,5},{5... | collective-permute-start | bytes 196616 | tf_op jit(solution)/shard_map/g1/ppermute | solution.py:364
  148.9 9.3 %collective-permute-start.49 = (bf16[128,256]{1,0:T(8,128)(2,1)S(1)}, bf16[128,256]{1,0:T(8,128)(2,1)S(1)}, u32[]{:S(2)}, u32[]{:S(2)}) collective-permute-start(bf16[128,256]{1,0:T(8,128)(2,1)S(1)} %g2.4), channel_id=1, source_target_pairs={{0,4},{4,0},{8,12},{12,8},{16,20},{20,16},{24,28},{28,24},{1,5},{5... | collective-permute-start | bytes 196616 | tf_op jit(solution)/shard_map/g2/ppermute | solution.py:364
  152.5 11.9 %collective-permute-start.47 = (bf16[256,384]{1,0:T(8,128)(2,1)S(1)}, bf16[256,384]{1,0:T(8,128)(2,1)S(1)}, u32[]{:S(2)}, u32[]{:S(2)}) collective-permute-start(bf16[256,384]{1,0:T(8,128)(2,1)S(1)} %pad_maximum_fusion.4), channel_id=1, source_target_pairs={{0,16},{4,20},{8,0},{12,4},{16,24},{20,28},{24,8},{28,12},{1,17},{... | collective-permute-start | bytes 589832 | tf_op jit(solution)/shard_map/g0/ppermute | solution.py:55
  153.2 11.6 %collective-permute-start.48 = (bf16[256,384]{1,0:T(8,128)(2,1)S(1)}, bf16[256,384]{1,0:T(8,128)(2,1)S(1)}, u32[]{:S(2)}, u32[]{:S(2)}) collective-permute-start(bf16[256,384]{1,0:T(8,128)(2,1)S(1)} %pad_maximum_fusion.5), channel_id=1, source_target_pairs={{0,8},{4,12},{8,24},{12,28},{16,0},{20,4},{24,16},{28,20},{1,9},{5... | collective-permute-start | bytes 589832 | tf_op jit(solution)/shard_map/g0/ppermute | solution.py:55
  154.6 10.2 %collective-permute-start.51 = (bf16[384,256]{1,0:T(8,128)(2,1)S(1)}, bf16[384,256]{1,0:T(8,128)(2,1)S(1)}, u32[]{:S(2)}, u32[]{:S(2)}) collective-permute-start(bf16[384,256]{1,0:T(8,128)(2,1)S(1)} %g1.5), channel_id=1, source_target_pairs={{0,4},{4,0},{8,12},{12,8},{16,20},{20,16},{24,28},{28,24},{1,5},{5... | collective-permute-start | bytes 589832 | tf_op jit(solution)/shard_map/g1/ppermute | solution.py:364
  155.8 11.7 %collective-permute-start.52 = (bf16[128,256]{1,0:T(8,128)(2,1)S(1)}, bf16[128,256]{1,0:T(8,128)(2,1)S(1)}, u32[]{:S(2)}, u32[]{:S(2)}) collective-permute-start(bf16[128,256]{1,0:T(8,128)(2,1)S(1)} %get-tuple-element.343), channel_id=1, source_target_pairs={{0,16},{4,20},{8,0},{12,4},{16,24},{20,28},{24,8},{28,12},{1,17},{... | collective-permute-start | bytes 196616 | tf_op jit(solution)/shard_map/g1/ppermute | solution.py:55
  158.2 9.2 %collective-permute-start.53 = (bf16[128,256]{1,0:T(8,128)(2,1)S(1)}, bf16[128,256]{1,0:T(8,128)(2,1)S(1)}, u32[]{:S(2)}, u32[]{:S(2)}) collective-permute-start(bf16[128,256]{1,0:T(8,128)(2,1)S(1)} %get-tuple-element.344), channel_id=1, source_target_pairs={{0,8},{4,12},{8,24},{12,28},{16,0},{20,4},{24,16},{28,20},{1,9},{5... | collective-permute-start | bytes 196616 | tf_op jit(solution)/shard_map/g1/ppermute | solution.py:55
  164.5 5.7 %collective-permute-start.56 = (bf16[384,256]{1,0:T(8,128)(2,1)S(1)}, bf16[384,256]{1,0:T(8,128)(2,1)S(1)}, u32[]{:S(2)}, u32[]{:S(2)}) collective-permute-start(bf16[384,256]{1,0:T(8,128)(2,1)S(1)} %g2.5), channel_id=1, source_target_pairs={{0,4},{4,0},{8,12},{12,8},{16,20},{20,16},{24,28},{28,24},{1,5},{5... | collective-permute-start | bytes 589832 | tf_op jit(solution)/shard_map/g2/ppermute | solution.py:364
  164.8 5.4 %collective-permute-start.57 = (bf16[128,256]{1,0:T(8,128)(2,1)S(1)}, bf16[128,256]{1,0:T(8,128)(2,1)S(1)}, u32[]{:S(2)}, u32[]{:S(2)}) collective-permute-start(bf16[128,256]{1,0:T(8,128)(2,1)S(1)} %get-tuple-element.359), channel_id=1, source_target_pairs={{0,16},{4,20},{8,0},{12,4},{16,24},{20,28},{24,8},{28,12},{1,17},{... | collective-permute-start | bytes 196616 | tf_op jit(solution)/shard_map/g2/ppermute | solution.py:55
  164.8 7.4 %collective-permute-start.58 = (bf16[128,256]{1,0:T(8,128)(2,1)S(1)}, bf16[128,256]{1,0:T(8,128)(2,1)S(1)}, u32[]{:S(2)}, u32[]{:S(2)}) collective-permute-start(bf16[128,256]{1,0:T(8,128)(2,1)S(1)} %get-tuple-element.360), channel_id=1, source_target_pairs={{0,8},{4,12},{8,24},{12,28},{16,0},{20,4},{24,16},{28,20},{1,9},{5... | collective-permute-start | bytes 196616 | tf_op jit(solution)/shard_map/g2/ppermute | solution.py:55
  167.6 7.6 %collective-permute-start.54 = (bf16[256,256]{1,0:T(8,128)(2,1)S(1)}, bf16[256,256]{1,0:T(8,128)(2,1)S(1)}, u32[]{:S(2)}, u32[]{:S(2)}) collective-permute-start(bf16[256,256]{1,0:T(8,128)(2,1)S(1)} %pad_maximum_fusion.6), channel_id=1, source_target_pairs={{0,16},{4,20},{8,0},{12,4},{16,24},{20,28},{24,8},{28,12},{1,17},{... | collective-permute-start | bytes 393224 | tf_op jit(solution)/shard_map/g1/ppermute | solution.py:55
  168.6 10.3 %collective-permute-start.55 = (bf16[256,256]{1,0:T(8,128)(2,1)S(1)}, bf16[256,256]{1,0:T(8,128)(2,1)S(1)}, u32[]{:S(2)}, u32[]{:S(2)}) collective-permute-start(bf16[256,256]{1,0:T(8,128)(2,1)S(1)} %pad_maximum_fusion.7), channel_id=1, source_target_pairs={{0,8},{4,12},{8,24},{12,28},{16,0},{20,4},{24,16},{28,20},{1,9},{5... | collective-permute-start | bytes 393224 | tf_op jit(solution)/shard_map/g1/ppermute | solution.py:55
  173.0 7.4 %collective-permute-start.59 = (bf16[256,256]{1,0:T(8,128)(2,1)S(1)}, bf16[256,256]{1,0:T(8,128)(2,1)S(1)}, u32[]{:S(2)}, u32[]{:S(2)}) collective-permute-start(bf16[256,256]{1,0:T(8,128)(2,1)S(1)} %pad_maximum_fusion.8), channel_id=1, source_target_pairs={{0,16},{4,20},{8,0},{12,4},{16,24},{20,28},{24,8},{28,12},{1,17},{... | collective-permute-start | bytes 393224 | tf_op jit(solution)/shard_map/g2/ppermute | solution.py:55
  173.0 8.7 %collective-permute-start.60 = (bf16[256,256]{1,0:T(8,128)(2,1)S(1)}, bf16[256,256]{1,0:T(8,128)(2,1)S(1)}, u32[]{:S(2)}, u32[]{:S(2)}) collective-permute-start(bf16[256,256]{1,0:T(8,128)(2,1)S(1)} %pad_maximum_fusion.9), channel_id=1, source_target_pairs={{0,8},{4,12},{8,24},{12,28},{16,0},{20,4},{24,16},{28,20},{1,9},{5... | collective-permute-start | bytes 393224 | tf_op jit(solution)/shard_map/g2/ppermute | solution.py:55
  (4 other events, 29.7 us)

commit v4 on v3

--- a/solution.py
+++ b/solution.py
@@ -373,9 +373,9 @@
     else:
         cuts = {"x": [width], "d": [width]}
 
-    meta = jnp.concatenate([expert_ids.astype(BF).T, gate_probs.T], axis=0)
+    meta = jnp.concatenate([expert_ids.T.astype(BF), gate_probs.T, jnp.zeros((HEAD - 2 * top, tok), BF)], axis=0)
     lines = 2 * top
-    swaps = [cross(meta, dx) for dx in range(1, nx)]
+    swaps = [cross(meta[: 2 * top], dx) for dx in range(1, nx)]
 
     def headed(rows, piece):
         rows = jnp.pad(rows, ((0, HEAD - rows.shape[0]), (0, piece.shape[1] - tok)))

time: 183 us -> 183 us (level)
  transfers between devices with their start and end apart: 61 -> 61, of which waited for: 26 -> 25; matrix products, arithmetic and copies ran while one was open for 14% -> 15% of each run, Pallas kernels for 11% -> 11%
where the time goes in v4:
time: 183 us
  starting transfers between devices  63.5 us (35%)
  waiting for transfers between devices  62 us (34%)
  matrix products  24.2 us (13%)
  Pallas kernels  19.7 us (11%)
  local copies, waits for them, and re-layouts  7 us (4%)
  other arithmetic  4.73 us (3%)
    ppermute x46, starting transfers between devices, send(): return lax.ppermute(value, self.axis, self.perms[step])  45.3 us
    ppermute x46, waiting for transfers between devices, send(): return lax.ppermute(value, self.axis, self.perms[step])  45 us
    pallas_call x25, Pallas kernels, kernel_call(): pl.pallas_call(body, out_shape=outs, in_specs=[smem] * len(scalars) + [vm...  19.7 us
    ppermute x15, starting transfers between devices, cross(): return lax.ppermute(value, 'exp', pairs)  18.3 us
    ppermute x15, waiting for transfers between devices, cross(): return lax.ppermute(value, 'exp', pairs)  17 us
    dot_general x2, matrix products, unpick(): lax.dot_general(onehot, rows, (((0,), (0,)), ((), ())), preferred_element...  10.5 us
    dot_general x12, matrix products, term(): lax.dot_general(line.go(d_hidden), part, (((1,), (1,)), ((), ())), prefer...  6.51 us
    slice x4, local copies, waits for them, and re-layouts, fetch(): piece = source[:, lo:hi]  4.51 us
  transfers between devices with their start and end apart: 61, of which 25 were waited for; matrix products, arithmetic and copies ran while one was open for 15% of the time, Pallas kernels for 11%

profile of v4, /device:TPU:0, one launch (start us, length us, event | category | flops | bytes accessed | tf_op | source)
XLA Modules:
  0.0 182.9 jit_solution(17247707376358196842)
XLA Ops:
  1.3 1.0 slice.125
  3.2 4.1 %collective-permute-start = (bf16[272,512]{1,0:T(8,128)(2,1)S(1)}, bf16[272,512]{1,0:T(8,128)(2,1)S(1)}, u32[]{:S(2)}, u32[]{:S(2)}) collective-permute-start(bf16[272,512]{1,0:T(8,128)(2,1)S(1)} %fusion.41.refs_3_.refs_0_), channel_id=1, source_target_pairs={{0,16},{4,20},{8,0},{12,4},{16,24},{20,28},{24,8},{28,12},{1,17},{... | collective-permute-start | bytes 835592 | tf_op jit(solution)/shard_map/x0/ppermute | solution.py:55
  7.9 1.5 collective-permute-start.2
  9.4 0.9 slice.128
  10.5 1.0 collective-permute-done.2
  11.5 3.0 %collective-permute-start.5 = (bf16[272,384]{1,0:T(8,128)(2,1)S(1)}, bf16[272,384]{1,0:T(8,128)(2,1)S(1)}, u32[]{:S(2)}, u32[]{:S(2)}) collective-permute-start(bf16[272,384]{1,0:T(8,128)(2,1)S(1)} %fusion.42.refs_7_.refs_0_), channel_id=1, source_target_pairs={{0,16},{4,20},{8,0},{12,4},{16,24},{20,28},{24,8},{28,12},{1,17},{... | collective-permute-start | bytes 626696 | tf_op jit(solution)/shard_map/x1/ppermute | solution.py:55
  14.6 1.0 slice.131.refs_0_
  15.6 1.6 slice.134.refs_0_
  17.2 5.0 %collective-permute-done.1.refs_5_.refs_2_ = bf16[272,512]{1,0:T(8,128)(2,1)S(1)} collective-permute-done((bf16[272,512]{1,0:T(8,128)(2,1)S(1)}, bf16[272,512]{1,0:T(8,128)(2,1)S(1)}, u32[]{:S(2)}, u32[]{:S(2)}) %collective-permute-start.1) | collective-permute-done | bytes 278560 | tf_op jit(solution)/shard_map/x0/ppermute | solution.py:55
  22.8 1.6 collective-permute-start.4
  24.8 6.4 %collective-permute-done.6.refs_9_.refs_2_ = bf16[272,384]{1,0:T(8,128)(2,1)S(1)} collective-permute-done((bf16[272,384]{1,0:T(8,128)(2,1)S(1)}, bf16[272,384]{1,0:T(8,128)(2,1)S(1)}, u32[]{:S(2)}, u32[]{:S(2)}) %collective-permute-start.6) | collective-permute-done | bytes 208928 | tf_op jit(solution)/shard_map/x1/ppermute | solution.py:55
  32.6 1.6 collective-permute-start.8
  34.2 1.5 collective-permute-start.12
  35.7 1.0 collective-permute-done.4.refs_1_.refs_4_
  36.6 1.1 collective-permute-start.10
  37.8 1.8 collective-permute-start.9
  40.6 1.5 collective-permute-start.11
  43.3 2.6 %collective-permute-done.12.refs_5_ = bf16[384,512]{1,0:T(8,128)(2,1)S(1)} collective-permute-done((bf16[384,512]{1,0:T(8,128)(2,1)S(1)}, bf16[384,512]{1,0:T(8,128)(2,1)S(1)}, u32[]{:S(2)}, u32[]{:S(2)}) %collective-permute-start.12) | collective-permute-done | bytes 393248 | tf_op jit(solution)/shard_map/x0/ppermute | solution.py:364
  45.9 1.5 collective-permute-start.15
  47.3 1.3 collective-permute-done.11.refs_6_
  48.7 2.4 %x0.7 = bf16[640,512]{1,0:T(8,128)(2,1)S(1)} custom-call(f32[4,256]{1,0:T(4,128)S(1)} %get-tuple-element.205.rank_ref, f32[4,256]{1,0:T(4,128)S(1)} %get-tuple-element.207.weight_ref, f32[4,128]{1,0:T(4,128)S(1)} %get-tuple-element.208.in_ref, bf16[272,512]{1,0:T(8,128)(2,1)S(1)} %fusion.41.refs_3_.refs_0_, ...), custom_call_target="tpu_custom_call" | custom-call | flops 6000000000 | bytes 6000000 | tf_op jit(solution)/shard_map/x0/pallas_call | solution.py:161
  51.1 1.6 collective-permute-start.18
  53.6 1.8 collective-permute-start.13
  56.0 2.3 %collective-permute-start.21 = (bf16[256,384]{1,0:T(8,128)(2,1)S(1)}, bf16[256,384]{1,0:T(8,128)(2,1)S(1)}, u32[]{:S(2)}, u32[]{:S(2)}) collective-permute-start(bf16[256,384]{1,0:T(8,128)(2,1)S(1)} %copy-done), channel_id=1, source_target_pairs={{0,16},{4,20},{8,0},{12,4},{16,24},{20,28},{24,8},{28,12},{1,17},{... | collective-permute-start | bytes 589832 | tf_op jit(solution)/shard_map/d1/ppermute | solution.py:55
  58.3 2.2 %x1.5 = bf16[640,384]{1,0:T(8,128)(2,1)S(1)} custom-call(f32[4,256]{1,0:T(4,128)S(1)} %get-tuple-element.205.rank_ref, f32[4,256]{1,0:T(4,128)S(1)} %get-tuple-element.207.weight_ref, f32[4,128]{1,0:T(4,128)S(1)} %get-tuple-element.208.in_ref, bf16[272,384]{1,0:T(8,128)(2,1)S(1)} %fusion.42.refs_7_.refs_0_, ...), custom_call_target="tpu_custom_call" | custom-call | flops 6000000000 | bytes 6000000 | tf_op jit(solution)/shard_map/x1/pallas_call | solution.py:161
  60.5 2.2 %collective-permute-start.22 = (bf16[256,384]{1,0:T(8,128)(2,1)S(1)}, bf16[256,384]{1,0:T(8,128)(2,1)S(1)}, u32[]{:S(2)}, u32[]{:S(2)}) collective-permute-start(bf16[256,384]{1,0:T(8,128)(2,1)S(1)} %copy-done), channel_id=1, source_target_pairs={{0,8},{4,12},{8,24},{12,28},{16,0},{20,4},{24,16},{28,20},{1,9},{5... | collective-permute-start | bytes 589832 | tf_op jit(solution)/shard_map/d1/ppermute | solution.py:55
  62.7 2.3 %collective-permute-done.14.refs_1_.refs_4_ = bf16[128,512]{1,0:T(8,128)(2,1)S(1)} collective-permute-done((bf16[128,512]{1,0:T(8,128)(2,1)S(1)}, bf16[128,512]{1,0:T(8,128)(2,1)S(1)}, u32[]{:S(2)}, u32[]{:S(2)}) %collective-permute-start.14) | collective-permute-done | bytes 131104 | tf_op jit(solution)/shard_map/d0/ppermute | solution.py:55
  65.0 1.5 collective-permute-start.17
  67.5 5.5 %collective-permute-done.22.refs_2_ = bf16[256,384]{1,0:T(8,128)(2,1)S(1)} collective-permute-done((bf16[256,384]{1,0:T(8,128)(2,1)S(1)}, bf16[256,384]{1,0:T(8,128)(2,1)S(1)}, u32[]{:S(2)}, u32[]{:S(2)}) %collective-permute-start.22) | collective-permute-done | bytes 196640 | tf_op jit(solution)/shard_map/d1/ppermute | solution.py:55
  73.4 1.6 collective-permute-start.23
  75.9 1.3 collective-permute-start.28
  77.2 2.1 %collective-permute-done.23.refs_6_ = bf16[128,512]{1,0:T(8,128)(2,1)S(1)} collective-permute-done((bf16[128,512]{1,0:T(8,128)(2,1)S(1)}, bf16[128,512]{1,0:T(8,128)(2,1)S(1)}, u32[]{:S(2)}, u32[]{:S(2)}) %collective-permute-start.23) | collective-permute-done | bytes 131104 | tf_op jit(solution)/shard_map/d0/ppermute | solution.py:364
  79.4 2.4 %d0.5 = bf16[640,512]{1,0:T(8,128)(2,1)S(1)} custom-call(f32[4,256]{1,0:T(4,128)S(1)} %get-tuple-element.205.rank_ref, f32[4,256]{1,0:T(4,128)S(1)} %get-tuple-element.207.weight_ref, f32[4,128]{1,0:T(4,128)S(1)} %get-tuple-element.208.in_ref, bf16[256,512]{1,0:T(8,128)(2,1)S(1)} %slice.131.refs_0_, bf16[256,512]{1,0:T(8,128)(2,1)S(1)} %collective-permute-done.9.refs_1_, ...), custom_call_target="tpu_custom_call" | custom-call | flops 6000000000 | bytes 6000000 | tf_op jit(solution)/shard_map/d0/pallas_call | solution.py:161
  82.4 1.6 collective-permute-start.32
  85.4 6.8 %collective-permute-done.32.refs_5_ = bf16[384,384]{1,0:T(8,128)(2,1)S(1)} collective-permute-done((bf16[384,384]{1,0:T(8,128)(2,1)S(1)}, bf16[384,384]{1,0:T(8,128)(2,1)S(1)}, u32[]{:S(2)}, u32[]{:S(2)}) %collective-permute-start.32) | collective-permute-done | bytes 294944 | tf_op jit(solution)/shard_map/d1/ppermute | solution.py:364
  92.3 1.6 collective-permute-done.31.refs_6_
  93.9 2.3 %d1.5 = bf16[640,384]{1,0:T(8,128)(2,1)S(1)} custom-call(f32[4,256]{1,0:T(4,128)S(1)} %get-tuple-element.205.rank_ref, f32[4,256]{1,0:T(4,128)S(1)} %get-tuple-element.207.weight_ref, f32[4,128]{1,0:T(4,128)S(1)} %get-tuple-element.208.in_ref, bf16[256,384]{1,0:T(8,128)(2,1)S(1)} %copy-done, bf16[256,384]{1,0:T(8,128)(2,1)S(1)} %collective-permute-done.21.refs_1_, ...), custom_call_target="tpu_custom_call" | custom-call | flops 6000000000 | bytes 6000000 | tf_op jit(solution)/shard_map/d1/pallas_call | solution.py:161
  96.2 1.6 collective-permute-start.35
  98.7 3.6 %fusion.2 = f32[640,608]{0,1:T(8,128)S(1)} fusion(bf16[640,3584]{1,0:T(8,128)(2,1)S(1)} %constant_dynamic-update-slice_fusion.3, bf16[1,3584,608]{1,2,0:T(8,128)(2,1)S(1)} %bitcast.80), kind=kOutput, calls=%fused_computation.4 | convolution fusion | flops 2789212160 | bytes 10502144 | tf_op jit(solution)/shard_map/h/dot_general | solution.py:522
  102.4 6.7 %collective-permute-done.35 = bf16[640,384]{1,0:T(8,128)(2,1)S(1)} collective-permute-done((bf16[640,384]{1,0:T(8,128)(2,1)S(1)}, bf16[640,384]{1,0:T(8,128)(2,1)S(1)}, u32[]{:S(2)}, u32[]{:S(2)}) %collective-permute-start.35) | collective-permute-done | bytes 491552 | tf_op jit(solution)/shard_map/d1/ppermute | solution.py:55
  109.8 1.1 collective-permute-done.36
  111.1 3.7 %multiply_convert_fusion.1 = bf16[640,608]{0,1:T(8,128)(2,1)S(1)} fusion(f32[640,608]{0,1:T(8,128)S(1)} %fusion.2, bf16[640,3584]{1,0:T(8,128)(2,1)S(1)} %constant_dynamic-update-slice_fusion, bf16[1,608,3584]{2,1,0:T(8,128)(2,1)S(1)} %bitcast.84), kind=kOutput, calls=%fused_computation.8 | convolution fusion | flops 2792714240 | bytes 11280384 | tf_op jit(solution)/shard_map/dot_general | solution.py:534
  120.8 1.6 collective-permute-start.38
  125.0 5.4 %convolution_convert_fusion.1 = bf16[608,3584]{1,0:T(8,128)(2,1)} fusion(bf16[640,608]{0,1:T(8,128)(2,1)S(1)} %multiply_convert_fusion, bf16[640,3584]{1,0:T(8,128)(2,1)S(1)} %constant_dynamic-update-slice_fusion), kind=kOutput, calls=%fused_computation.1 | convolution fusion | flops 2791391232 | bytes 9723904 | tf_op jit(solution)/shard_map/w/dot_general | solution.py:335
  130.4 5.1 %convolution_convert_fusion = bf16[608,3584]{1,0:T(8,128)(2,1)} fusion(bf16[640,608]{0,1:T(8,128)(2,1)S(1)} %multiply_convert_fusion.1, bf16[640,3584]{1,0:T(8,128)(2,1)S(1)} %constant_dynamic-update-slice_fusion.3), kind=kOutput, calls=%fused_computation | convolution fusion | flops 2791391232 | bytes 9723904 | tf_op jit(solution)/shard_map/u/dot_general | solution.py:335
  135.9 1.2 g0.4
  137.2 1.5 collective-permute-start.44
  138.9 1.6 collective-permute-start.42
  144.0 1.4 collective-permute-start.46
  145.4 1.8 collective-permute-start.50
  147.2 1.2 collective-permute-done.42
  149.1 1.6 collective-permute-start.49
  150.7 1.9 %g0.6 = (f32[256,384]{1,0:T(8,128)S(1)}, f32[256,384]{1,0:T(8,128)S(1)}, f32[256,384]{1,0:T(8,128)S(1)}) custom-call(f32[4,256]{1,0:T(4,128)S(1)} %copy-done.2, f32[4,256]{1,0:T(4,128)S(1)} %get-tuple-element.206.slots_ref, bf16[640,384]{1,0:T(8,128)(2,1)S(1)} %fusion.6.total_ref, bf16[384,384]{1,0:T(8,128)(2,1)} %collective-permute-done.41.refs_0_), custom_call_target="tpu_custom_call" | custom-call | flops 30000001024 | bytes 30000000 | tf_op jit(solution)/shard_map/g0/pallas_call | solution.py:161
  153.3 1.4 collective-permute-start.48
  155.9 2.4 %collective-permute-start.52 = (bf16[128,256]{1,0:T(8,128)(2,1)S(1)}, bf16[128,256]{1,0:T(8,128)(2,1)S(1)}, u32[]{:S(2)}, u32[]{:S(2)}) collective-permute-start(bf16[128,256]{1,0:T(8,128)(2,1)S(1)} %get-tuple-element.343), channel_id=1, source_target_pairs={{0,16},{4,20},{8,0},{12,4},{16,24},{20,28},{24,8},{28,12},{1,17},{... | collective-permute-start | bytes 196616 | tf_op jit(solution)/shard_map/g1/ppermute | solution.py:55
  158.7 5.9 %collective-permute-done.47 = bf16[256,384]{1,0:T(8,128)(2,1)S(1)} collective-permute-done((bf16[256,384]{1,0:T(8,128)(2,1)S(1)}, bf16[256,384]{1,0:T(8,128)(2,1)S(1)}, u32[]{:S(2)}, u32[]{:S(2)}) %collective-permute-start.47) | collective-permute-done | bytes 196640 | tf_op jit(solution)/shard_map/g0/ppermute | solution.py:55
  165.0 2.0 %collective-permute-start.58 = (bf16[128,256]{1,0:T(8,128)(2,1)S(1)}, bf16[128,256]{1,0:T(8,128)(2,1)S(1)}, u32[]{:S(2)}, u32[]{:S(2)}) collective-permute-start(bf16[128,256]{1,0:T(8,128)(2,1)S(1)} %get-tuple-element.360), channel_id=1, source_target_pairs={{0,8},{4,12},{8,24},{12,28},{16,0},{20,4},{24,16},{28,20},{1,9},{5... | collective-permute-start | bytes 196616 | tf_op jit(solution)/shard_map/g2/ppermute | solution.py:55
  167.8 1.0 collective-permute-start.54
  168.8 1.1 collective-permute-start.55
  170.3 2.1 %collective-permute-done.58 = bf16[128,256]{1,0:T(8,128)(2,1)S(1)} collective-permute-done((bf16[128,256]{1,0:T(8,128)(2,1)S(1)}, bf16[128,256]{1,0:T(8,128)(2,1)S(1)}, u32[]{:S(2)}, u32[]{:S(2)}) %collective-permute-start.58) | collective-permute-done | bytes 65568 | tf_op jit(solution)/shard_map/g2/ppermute | solution.py:55
  173.2 2.0 %collective-permute-start.60 = (bf16[256,256]{1,0:T(8,128)(2,1)S(1)}, bf16[256,256]{1,0:T(8,128)(2,1)S(1)}, u32[]{:S(2)}, u32[]{:S(2)}) collective-permute-start(bf16[256,256]{1,0:T(8,128)(2,1)S(1)} %pad_maximum_fusion.9), channel_id=1, source_target_pairs={{0,8},{4,12},{8,24},{12,28},{16,0},{20,4},{24,16},{28,20},{1,9},{5... | collective-permute-start | bytes 393224 | tf_op jit(solution)/shard_map/g2/ppermute | solution.py:55
  175.4 3.6 %collective-permute-done.55 = bf16[256,256]{1,0:T(8,128)(2,1)S(1)} collective-permute-done((bf16[256,256]{1,0:T(8,128)(2,1)S(1)}, bf16[256,256]{1,0:T(8,128)(2,1)S(1)}, u32[]{:S(2)}, u32[]{:S(2)}) %collective-permute-start.55) | collective-permute-done | bytes 131104 | tf_op jit(solution)/shard_map/g1/ppermute | solution.py:55
  179.0 1.5 collective-permute-done.59
  180.5 1.4 collective-permute-done.60
  (192 shorter events, 33.4 us)
Async XLA Ops:
  3.2 14.1 %collective-permute-start = (bf16[272,512]{1,0:T(8,128)(2,1)S(1)}, bf16[272,512]{1,0:T(8,128)(2,1)S(1)}, u32[]{:S(2)}, u32[]{:S(2)}) collective-permute-start(bf16[272,512]{1,0:T(8,128)(2,1)S(1)} %fusion.41.refs_3_.refs_0_), channel_id=1, source_target_pairs={{0,16},{4,20},{8,0},{12,4},{16,24},{20,28},{24,8},{28,12},{1,17},{... | collective-permute-start | bytes 835592 | tf_op jit(solution)/shard_map/x0/ppermute | solution.py:55
  7.2 15.0 %collective-permute-start.1 = (bf16[272,512]{1,0:T(8,128)(2,1)S(1)}, bf16[272,512]{1,0:T(8,128)(2,1)S(1)}, u32[]{:S(2)}, u32[]{:S(2)}) collective-permute-start(bf16[272,512]{1,0:T(8,128)(2,1)S(1)} %fusion.41.refs_3_.refs_0_), channel_id=1, source_target_pairs={{0,8},{4,12},{8,24},{12,28},{16,0},{20,4},{24,16},{28,20},{1,9},{5... | collective-permute-start | bytes 835592 | tf_op jit(solution)/shard_map/x0/ppermute | solution.py:55
  7.9 3.6 %collective-permute-start.2 = (bf16[4,256]{1,0:T(4,128)(2,1)S(1)}, bf16[4,256]{1,0:T(4,128)(2,1)S(1)}, u32[]{:S(2)}, u32[]{:S(2)}) collective-permute-start(bf16[4,256]{1,0:T(4,128)(2,1)S(1)} %pad_maximum_fusion.10), channel_id=1, source_target_pairs={{0,4},{4,0},{8,12},{12,8},{16,20},{20,16},{24,28},{28,24},{1,5},{5... | collective-permute-start | bytes 6152 | tf_op jit(solution)/shard_map/ppermute | solution.py:364
  11.5 13.3 %collective-permute-start.5 = (bf16[272,384]{1,0:T(8,128)(2,1)S(1)}, bf16[272,384]{1,0:T(8,128)(2,1)S(1)}, u32[]{:S(2)}, u32[]{:S(2)}) collective-permute-start(bf16[272,384]{1,0:T(8,128)(2,1)S(1)} %fusion.42.refs_7_.refs_0_), channel_id=1, source_target_pairs={{0,16},{4,20},{8,0},{12,4},{16,24},{20,28},{24,8},{28,12},{1,17},{... | collective-permute-start | bytes 626696 | tf_op jit(solution)/shard_map/x1/ppermute | solution.py:55
  14.5 16.7 %collective-permute-start.6 = (bf16[272,384]{1,0:T(8,128)(2,1)S(1)}, bf16[272,384]{1,0:T(8,128)(2,1)S(1)}, u32[]{:S(2)}, u32[]{:S(2)}) collective-permute-start(bf16[272,384]{1,0:T(8,128)(2,1)S(1)} %fusion.42.refs_7_.refs_0_), channel_id=1, source_target_pairs={{0,8},{4,12},{8,24},{12,28},{16,0},{20,4},{24,16},{28,20},{1,9},{5... | collective-permute-start | bytes 626696 | tf_op jit(solution)/shard_map/x1/ppermute | solution.py:55
  22.3 14.4 %collective-permute-start.3 = (bf16[144,512]{1,0:T(8,128)(2,1)S(1)}, bf16[144,512]{1,0:T(8,128)(2,1)S(1)}, u32[]{:S(2)}, u32[]{:S(2)}) collective-permute-start(bf16[144,512]{1,0:T(8,128)(2,1)S(1)} %slice.126), channel_id=1, source_target_pairs={{0,16},{4,20},{8,0},{12,4},{16,24},{20,28},{24,8},{28,12},{1,17},{... | collective-permute-start | bytes 442376 | tf_op jit(solution)/shard_map/x0/ppermute | solution.py:55
  22.8 13.9 %collective-permute-start.4 = (bf16[128,512]{1,0:T(8,128)(2,1)S(1)}, bf16[128,512]{1,0:T(8,128)(2,1)S(1)}, u32[]{:S(2)}, u32[]{:S(2)}) collective-permute-start(bf16[128,512]{1,0:T(8,128)(2,1)S(1)} %slice.127), channel_id=1, source_target_pairs={{0,8},{4,12},{8,24},{12,28},{16,0},{20,4},{24,16},{28,20},{1,9},{5... | collective-permute-start | bytes 393224 | tf_op jit(solution)/shard_map/x0/ppermute | solution.py:55
  32.1 10.0 %collective-permute-start.7 = (bf16[144,384]{1,0:T(8,128)(2,1)S(1)}, bf16[144,384]{1,0:T(8,128)(2,1)S(1)}, u32[]{:S(2)}, u32[]{:S(2)}) collective-permute-start(bf16[144,384]{1,0:T(8,128)(2,1)S(1)} %slice.129), channel_id=1, source_target_pairs={{0,16},{4,20},{8,0},{12,4},{16,24},{20,28},{24,8},{28,12},{1,17},{... | collective-permute-start | bytes 331784 | tf_op jit(solution)/shard_map/x1/ppermute | solution.py:55
  32.6 8.0 %collective-permute-start.8 = (bf16[128,384]{1,0:T(8,128)(2,1)S(1)}, bf16[128,384]{1,0:T(8,128)(2,1)S(1)}, u32[]{:S(2)}, u32[]{:S(2)}) collective-permute-start(bf16[128,384]{1,0:T(8,128)(2,1)S(1)} %slice.130), channel_id=1, source_target_pairs={{0,8},{4,12},{8,24},{12,28},{16,0},{20,4},{24,16},{28,20},{1,9},{5... | collective-permute-start | bytes 294920 | tf_op jit(solution)/shard_map/x1/ppermute | solution.py:55
  34.2 11.7 %collective-permute-start.12 = (bf16[384,512]{1,0:T(8,128)(2,1)S(1)}, bf16[384,512]{1,0:T(8,128)(2,1)S(1)}, u32[]{:S(2)}, u32[]{:S(2)}) collective-permute-start(bf16[384,512]{1,0:T(8,128)(2,1)S(1)} %x0.6), channel_id=1, source_target_pairs={{0,4},{4,0},{8,12},{12,8},{16,20},{20,16},{24,28},{28,24},{1,5},{5... | collective-permute-start | bytes 1179656 | tf_op jit(solution)/shard_map/x0/ppermute | solution.py:364
  36.6 16.4 %collective-permute-start.10 = (bf16[256,512]{1,0:T(8,128)(2,1)S(1)}, bf16[256,512]{1,0:T(8,128)(2,1)S(1)}, u32[]{:S(2)}, u32[]{:S(2)}) collective-permute-start(bf16[256,512]{1,0:T(8,128)(2,1)S(1)} %slice.131.refs_0_), channel_id=1, source_target_pairs={{0,8},{4,12},{8,24},{12,28},{16,0},{20,4},{24,16},{28,20},{1,9},{5... | collective-permute-start | bytes 786440 | tf_op jit(solution)/shard_map/d0/ppermute | solution.py:55
  37.8 15.3 %collective-permute-start.9 = (bf16[256,512]{1,0:T(8,128)(2,1)S(1)}, bf16[256,512]{1,0:T(8,128)(2,1)S(1)}, u32[]{:S(2)}, u32[]{:S(2)}) collective-permute-start(bf16[256,512]{1,0:T(8,128)(2,1)S(1)} %slice.131.refs_0_), channel_id=1, source_target_pairs={{0,16},{4,20},{8,0},{12,4},{16,24},{20,28},{24,8},{28,12},{1,17},{... | collective-permute-start | bytes 786440 | tf_op jit(solution)/shard_map/d0/ppermute | solution.py:55
  40.6 8.1 %collective-permute-start.11 = (bf16[128,512]{1,0:T(8,128)(2,1)S(1)}, bf16[128,512]{1,0:T(8,128)(2,1)S(1)}, u32[]{:S(2)}, u32[]{:S(2)}) collective-permute-start(bf16[128,512]{1,0:T(8,128)(2,1)S(1)} %x0.5), channel_id=1, source_target_pairs={{0,4},{4,0},{8,12},{12,8},{16,20},{20,16},{24,28},{28,24},{1,5},{5... | collective-permute-start | bytes 393224 | tf_op jit(solution)/shard_map/x0/ppermute | solution.py:364
  42.1 13.3 %collective-permute-start.16 = (bf16[384,384]{1,0:T(8,128)(2,1)S(1)}, bf16[384,384]{1,0:T(8,128)(2,1)S(1)}, u32[]{:S(2)}, u32[]{:S(2)}) collective-permute-start(bf16[384,384]{1,0:T(8,128)(2,1)S(1)} %x1.4), channel_id=1, source_target_pairs={{0,4},{4,0},{8,12},{12,8},{16,20},{20,16},{24,28},{28,24},{1,5},{5... | collective-permute-start | bytes 884744 | tf_op jit(solution)/shard_map/x1/ppermute | solution.py:364
  43.2 50.7 %copy-start.1 = (f32[4,256]{1,0:T(4,128)}, f32[4,256]{1,0:T(4,128)S(1)}, u32[]{:S(2)}) copy-start(f32[4,256]{1,0:T(4,128)S(1)} %get-tuple-element.205.rank_ref) | copy-start | bytes 12292
  45.9 10.1 %collective-permute-start.15 = (bf16[128,384]{1,0:T(8,128)(2,1)S(1)}, bf16[128,384]{1,0:T(8,128)(2,1)S(1)}, u32[]{:S(2)}, u32[]{:S(2)}) collective-permute-start(bf16[128,384]{1,0:T(8,128)(2,1)S(1)} %x1.3), channel_id=1, source_target_pairs={{0,4},{4,0},{8,12},{12,8},{16,20},{20,16},{24,28},{28,24},{1,5},{5... | collective-permute-start | bytes 294920 | tf_op jit(solution)/shard_map/x1/ppermute | solution.py:364
  51.1 15.8 %collective-permute-start.18 = (bf16[640,512]{1,0:T(8,128)(2,1)S(1)}, bf16[640,512]{1,0:T(8,128)(2,1)S(1)}, u32[]{:S(2)}, u32[]{:S(2)}) collective-permute-start(bf16[640,512]{1,0:T(8,128)(2,1)S(1)} %x0.7), channel_id=1, source_target_pairs={{0,2},{1,3},{2,0},{3,1},{4,6},{5,7},{6,4},{7,5},{8,10},{9,11},{10,... | collective-permute-start | bytes 1966088 | tf_op jit(solution)/shard_map/x0/ppermute | solution.py:55
  53.0 20.4 %collective-permute-start.20 = (bf16[640,512]{1,0:T(8,128)(2,1)S(1)}, bf16[640,512]{1,0:T(8,128)(2,1)S(1)}, u32[]{:S(2)}, u32[]{:S(2)}) collective-permute-start(bf16[640,512]{1,0:T(8,128)(2,1)S(1)} %x0.7), channel_id=1, source_target_pairs={{0,1},{1,0},{2,3},{3,2},{4,5},{5,4},{6,7},{7,6},{8,9},{9,8},{10,11... | collective-permute-start | bytes 1966088 | tf_op jit(solution)/shard_map/x0/ppermute | solution.py:55
  53.6 6.9 %collective-permute-start.13 = (bf16[128,512]{1,0:T(8,128)(2,1)S(1)}, bf16[128,512]{1,0:T(8,128)(2,1)S(1)}, u32[]{:S(2)}, u32[]{:S(2)}) collective-permute-start(bf16[128,512]{1,0:T(8,128)(2,1)S(1)} %slice.132), channel_id=1, source_target_pairs={{0,16},{4,20},{8,0},{12,4},{16,24},{20,28},{24,8},{28,12},{1,17},{... | collective-permute-start | bytes 393224 | tf_op jit(solution)/shard_map/d0/ppermute | solution.py:55
  55.4 9.7 %collective-permute-start.14 = (bf16[128,512]{1,0:T(8,128)(2,1)S(1)}, bf16[128,512]{1,0:T(8,128)(2,1)S(1)}, u32[]{:S(2)}, u32[]{:S(2)}) collective-permute-start(bf16[128,512]{1,0:T(8,128)(2,1)S(1)} %slice.133), channel_id=1, source_target_pairs={{0,8},{4,12},{8,24},{12,28},{16,0},{20,4},{24,16},{28,20},{1,9},{5... | collective-permute-start | bytes 393224 | tf_op jit(solution)/shard_map/d0/ppermute | solution.py:55
  56.0 11.5 %collective-permute-start.21 = (bf16[256,384]{1,0:T(8,128)(2,1)S(1)}, bf16[256,384]{1,0:T(8,128)(2,1)S(1)}, u32[]{:S(2)}, u32[]{:S(2)}) collective-permute-start(bf16[256,384]{1,0:T(8,128)(2,1)S(1)} %copy-done), channel_id=1, source_target_pairs={{0,16},{4,20},{8,0},{12,4},{16,24},{20,28},{24,8},{28,12},{1,17},{... | collective-permute-start | bytes 589832 | tf_op jit(solution)/shard_map/d1/ppermute | solution.py:55
  60.5 12.5 %collective-permute-start.22 = (bf16[256,384]{1,0:T(8,128)(2,1)S(1)}, bf16[256,384]{1,0:T(8,128)(2,1)S(1)}, u32[]{:S(2)}, u32[]{:S(2)}) collective-permute-start(bf16[256,384]{1,0:T(8,128)(2,1)S(1)} %copy-done), channel_id=1, source_target_pairs={{0,8},{4,12},{8,24},{12,28},{16,0},{20,4},{24,16},{28,20},{1,9},{5... | collective-permute-start | bytes 589832 | tf_op jit(solution)/shard_map/d1/ppermute | solution.py:55
  65.0 10.9 %collective-permute-start.17 = (bf16[384,512]{1,0:T(8,128)(2,1)S(1)}, bf16[384,512]{1,0:T(8,128)(2,1)S(1)}, u32[]{:S(2)}, u32[]{:S(2)}) collective-permute-start(bf16[384,512]{1,0:T(8,128)(2,1)S(1)} %d0.3), channel_id=1, source_target_pairs={{0,4},{4,0},{8,12},{12,8},{16,20},{20,16},{24,28},{28,24},{1,5},{5... | collective-permute-start | bytes 1179656 | tf_op jit(solution)/shard_map/d0/ppermute | solution.py:364
  66.9 17.7 %collective-permute-start.26 = (bf16[640,384]{1,0:T(8,128)(2,1)S(1)}, bf16[640,384]{1,0:T(8,128)(2,1)S(1)}, u32[]{:S(2)}, u32[]{:S(2)}) collective-permute-start(bf16[640,384]{1,0:T(8,128)(2,1)S(1)} %x1.5), channel_id=1, source_target_pairs={{0,2},{1,3},{2,0},{3,1},{4,6},{5,7},{6,4},{7,5},{8,10},{9,11},{10,... | collective-permute-start | bytes 1474568 | tf_op jit(solution)/shard_map/x1/ppermute | solution.py:55
  67.5 30.3 %collective-permute-start.30 = (bf16[640,384]{1,0:T(8,128)(2,1)S(1)}, bf16[640,384]{1,0:T(8,128)(2,1)S(1)}, u32[]{:S(2)}, u32[]{:S(2)}) collective-permute-start(bf16[640,384]{1,0:T(8,128)(2,1)S(1)} %x1.5), channel_id=1, source_target_pairs={{0,1},{1,0},{2,3},{3,2},{4,5},{5,4},{6,7},{7,6},{8,9},{9,8},{10,11... | collective-permute-start | bytes 1474568 | tf_op jit(solution)/shard_map/x1/ppermute | solution.py:55
  73.0 2.2 %collective-permute-start.19 = (bf16[640,512]{1,0:T(8,128)(2,1)S(1)}, bf16[640,512]{1,0:T(8,128)(2,1)S(1)}, u32[]{:S(2)}, u32[]{:S(2)}) collective-permute-start(bf16[640,512]{1,0:T(8,128)(2,1)S(1)} %collective-permute-done.18), channel_id=1, source_target_pairs={{0,1},{1,0},{2,3},{3,2},{4,5},{5,4},{6,7},{7,6},{8,9},{9,8},{10,11... | collective-permute-start | bytes 1966088 | tf_op jit(solution)/shard_map/x0/ppermute | solution.py:55
  73.4 6.0 %collective-permute-start.23 = (bf16[128,512]{1,0:T(8,128)(2,1)S(1)}, bf16[128,512]{1,0:T(8,128)(2,1)S(1)}, u32[]{:S(2)}, u32[]{:S(2)}) collective-permute-start(bf16[128,512]{1,0:T(8,128)(2,1)S(1)} %d0.4), channel_id=1, source_target_pairs={{0,4},{4,0},{8,12},{12,8},{16,20},{20,16},{24,28},{28,24},{1,5},{5... | collective-permute-start | bytes 393224 | tf_op jit(solution)/shard_map/d0/ppermute | solution.py:364
  75.1 7.2 %collective-permute-start.27 = (bf16[128,384]{1,0:T(8,128)(2,1)S(1)}, bf16[128,384]{1,0:T(8,128)(2,1)S(1)}, u32[]{:S(2)}, u32[]{:S(2)}) collective-permute-start(bf16[128,384]{1,0:T(8,128)(2,1)S(1)} %slice.135), channel_id=1, source_target_pairs={{0,16},{4,20},{8,0},{12,4},{16,24},{20,28},{24,8},{28,12},{1,17},{... | collective-permute-start | bytes 294920 | tf_op jit(solution)/shard_map/d1/ppermute | solution.py:55
  75.9 6.4 %collective-permute-start.28 = (bf16[128,384]{1,0:T(8,128)(2,1)S(1)}, bf16[128,384]{1,0:T(8,128)(2,1)S(1)}, u32[]{:S(2)}, u32[]{:S(2)}) collective-permute-start(bf16[128,384]{1,0:T(8,128)(2,1)S(1)} %slice.136), channel_id=1, source_target_pairs={{0,8},{4,12},{8,24},{12,28},{16,0},{20,4},{24,16},{28,20},{1,9},{5... | collective-permute-start | bytes 294920 | tf_op jit(solution)/shard_map/d1/ppermute | solution.py:55
  81.8 16.4 %collective-permute-start.25 = (bf16[640,512]{1,0:T(8,128)(2,1)S(1)}, bf16[640,512]{1,0:T(8,128)(2,1)S(1)}, u32[]{:S(2)}, u32[]{:S(2)}) collective-permute-start(bf16[640,512]{1,0:T(8,128)(2,1)S(1)} %d0.5), channel_id=1, source_target_pairs={{0,2},{1,3},{2,0},{3,1},{4,6},{5,7},{6,4},{7,5},{8,10},{9,11},{10,... | collective-permute-start | bytes 1966088 | tf_op jit(solution)/shard_map/d0/ppermute | solution.py:55
  82.4 19.9 %collective-permute-start.24 = (bf16[640,512]{1,0:T(8,128)(2,1)S(1)}, bf16[640,512]{1,0:T(8,128)(2,1)S(1)}, u32[]{:S(2)}, u32[]{:S(2)}) collective-permute-start(bf16[640,512]{1,0:T(8,128)(2,1)S(1)} %d0.5), channel_id=1, source_target_pairs={{0,1},{1,0},{2,3},{3,2},{4,5},{5,4},{6,7},{7,6},{8,9},{9,8},{10,11... | collective-permute-start | bytes 1966088 | tf_op jit(solution)/shard_map/d0/ppermute | solution.py:55
  82.4 9.9 %collective-permute-start.32 = (bf16[384,384]{1,0:T(8,128)(2,1)S(1)}, bf16[384,384]{1,0:T(8,128)(2,1)S(1)}, u32[]{:S(2)}, u32[]{:S(2)}) collective-permute-start(bf16[384,384]{1,0:T(8,128)(2,1)S(1)} %d1.3), channel_id=1, source_target_pairs={{0,4},{4,0},{8,12},{12,8},{16,20},{20,16},{24,28},{28,24},{1,5},{5... | collective-permute-start | bytes 884744 | tf_op jit(solution)/shard_map/d1/ppermute | solution.py:364
  84.7 9.2 %collective-permute-start.31 = (bf16[128,384]{1,0:T(8,128)(2,1)S(1)}, bf16[128,384]{1,0:T(8,128)(2,1)S(1)}, u32[]{:S(2)}, u32[]{:S(2)}) collective-permute-start(bf16[128,384]{1,0:T(8,128)(2,1)S(1)} %d1.4), channel_id=1, source_target_pairs={{0,4},{4,0},{8,12},{12,8},{16,20},{20,16},{24,28},{28,24},{1,5},{5... | collective-permute-start | bytes 294920 | tf_op jit(solution)/shard_map/d1/ppermute | solution.py:364
  85.3 13.4 %slice-start = ((s8[4358144]{0:T(1024)(128)(4,1)}), s8[4194304]{0:T(1024)(128)(4,1)S(1)}, s32[]{:S(2)}) async-start(s8[4358144]{0:T(1024)(128)(4,1)} %bitcast.79), calls=%async_computation | async-start | bytes 8388608
  85.4 13.3 %slice-start.1 = ((s8[4358144]{0:T(1024)(128)(4,1)}), s8[163840]{0:T(1024)(128)(4,1)S(1)}, s32[]{:S(2)}) async-start(s8[4358144]{0:T(1024)(128)(4,1)} %bitcast.79), calls=%async_computation.1 | async-start | bytes 327680
  92.3 5.8 %collective-permute-start.29 = (bf16[640,384]{1,0:T(8,128)(2,1)S(1)}, bf16[640,384]{1,0:T(8,128)(2,1)S(1)}, u32[]{:S(2)}, u32[]{:S(2)}) collective-permute-start(bf16[640,384]{1,0:T(8,128)(2,1)S(1)} %collective-permute-done.26), channel_id=1, source_target_pairs={{0,1},{1,0},{2,3},{3,2},{4,5},{5,4},{6,7},{7,6},{8,9},{9,8},{10,11... | collective-permute-start | bytes 1474568 | tf_op jit(solution)/shard_map/x1/ppermute | solution.py:55
  96.2 12.8 %collective-permute-start.35 = (bf16[640,384]{1,0:T(8,128)(2,1)S(1)}, bf16[640,384]{1,0:T(8,128)(2,1)S(1)}, u32[]{:S(2)}, u32[]{:S(2)}) collective-permute-start(bf16[640,384]{1,0:T(8,128)(2,1)S(1)} %d1.5), channel_id=1, source_target_pairs={{0,2},{1,3},{2,0},{3,1},{4,6},{5,7},{6,4},{7,5},{8,10},{9,11},{10,... | collective-permute-start | bytes 1474568 | tf_op jit(solution)/shard_map/d1/ppermute | solution.py:55
  97.8 11.3 %collective-permute-start.34 = (bf16[640,384]{1,0:T(8,128)(2,1)S(1)}, bf16[640,384]{1,0:T(8,128)(2,1)S(1)}, u32[]{:S(2)}, u32[]{:S(2)}) collective-permute-start(bf16[640,384]{1,0:T(8,128)(2,1)S(1)} %d1.5), channel_id=1, source_target_pairs={{0,1},{1,0},{2,3},{3,2},{4,5},{5,4},{6,7},{7,6},{8,9},{9,8},{10,11... | collective-permute-start | bytes 1474568 | tf_op jit(solution)/shard_map/d1/ppermute | solution.py:55
  98.2 4.2 %collective-permute-start.33 = (bf16[640,512]{1,0:T(8,128)(2,1)S(1)}, bf16[640,512]{1,0:T(8,128)(2,1)S(1)}, u32[]{:S(2)}, u32[]{:S(2)}) collective-permute-start(bf16[640,512]{1,0:T(8,128)(2,1)S(1)} %collective-permute-done.25), channel_id=1, source_target_pairs={{0,1},{1,0},{2,3},{3,2},{4,5},{5,4},{6,7},{7,6},{8,9},{9,8},{10,11... | collective-permute-start | bytes 1966088 | tf_op jit(solution)/shard_map/d0/ppermute | solution.py:55
  109.1 1.9 %collective-permute-start.36 = (bf16[640,384]{1,0:T(8,128)(2,1)S(1)}, bf16[640,384]{1,0:T(8,128)(2,1)S(1)}, u32[]{:S(2)}, u32[]{:S(2)}) collective-permute-start(bf16[640,384]{1,0:T(8,128)(2,1)S(1)} %collective-permute-done.35), channel_id=1, source_target_pairs={{0,1},{1,0},{2,3},{3,2},{4,5},{5,4},{6,7},{7,6},{8,9},{9,8},{10,11... | collective-permute-start | bytes 1474568 | tf_op jit(solution)/shard_map/d1/ppermute | solution.py:55
  116.3 3.0 %collective-permute-start.37 = (bf16[1280,384]{1,0:T(8,128)(2,1)S(1)}, bf16[1280,384]{1,0:T(8,128)(2,1)S(1)}, u32[]{:S(2)}, u32[]{:S(2)}) collective-permute-start(bf16[1280,384]{1,0:T(8,128)(2,1)S(1)} %pad_maximum_fusion), channel_id=1, source_target_pairs={{0,1},{1,0},{2,3},{3,2},{4,5},{5,4},{6,7},{7,6},{8,9},{9,8},{10,11... | collective-permute-start | bytes 2949128 | tf_op jit(solution)/shard_map/g0/ppermute | solution.py:55
  117.5 3.1 %collective-permute-start.40 = (bf16[1280,256]{1,0:T(8,128)(2,1)S(1)}, bf16[1280,256]{1,0:T(8,128)(2,1)S(1)}, u32[]{:S(2)}, u32[]{:S(2)}) collective-permute-start(bf16[1280,256]{1,0:T(8,128)(2,1)S(1)} %pad_maximum_fusion.2), channel_id=1, source_target_pairs={{0,1},{1,0},{2,3},{3,2},{4,5},{5,4},{6,7},{7,6},{8,9},{9,8},{10,11... | collective-permute-start | bytes 1966088 | tf_op jit(solution)/shard_map/g1/ppermute | solution.py:55
  120.3 4.7 %collective-permute-start.39 = (bf16[1280,256]{1,0:T(8,128)(2,1)S(1)}, bf16[1280,256]{1,0:T(8,128)(2,1)S(1)}, u32[]{:S(2)}, u32[]{:S(2)}) collective-permute-start(bf16[1280,256]{1,0:T(8,128)(2,1)S(1)} %pad_maximum_fusion.1), channel_id=1, source_target_pairs={{0,1},{1,0},{2,3},{3,2},{4,5},{5,4},{6,7},{7,6},{8,9},{9,8},{10,11... | collective-permute-start | bytes 1966088 | tf_op jit(solution)/shard_map/g2/ppermute | solution.py:55
  120.8 14.7 %collective-permute-start.38 = (bf16[640,384]{1,0:T(8,128)(2,1)S(1)}, bf16[640,384]{1,0:T(8,128)(2,1)S(1)}, u32[]{:S(2)}, u32[]{:S(2)}) collective-permute-start(bf16[640,384]{1,0:T(8,128)(2,1)S(1)} %slice.203), channel_id=1, source_target_pairs={{0,2},{1,3},{2,0},{3,1},{4,6},{5,7},{6,4},{7,5},{8,10},{9,11},{10,... | collective-permute-start | bytes 1474568 | tf_op jit(solution)/shard_map/g0/ppermute | solution.py:55
  123.5 18.3 %collective-permute-start.43 = (bf16[640,256]{1,0:T(8,128)(2,1)S(1)}, bf16[640,256]{1,0:T(8,128)(2,1)S(1)}, u32[]{:S(2)}, u32[]{:S(2)}) collective-permute-start(bf16[640,256]{1,0:T(8,128)(2,1)S(1)} %slice.204), channel_id=1, source_target_pairs={{0,2},{1,3},{2,0},{3,1},{4,6},{5,7},{6,4},{7,5},{8,10},{9,11},{10,... | collective-permute-start | bytes 983048 | tf_op jit(solution)/shard_map/g1/ppermute | solution.py:55
  137.2 4.6 %collective-permute-start.44 = (bf16[128,384]{1,0:T(8,128)(2,1)S(1)}, bf16[128,384]{1,0:T(8,128)(2,1)S(1)}, u32[]{:S(2)}, u32[]{:S(2)}) collective-permute-start(bf16[128,384]{1,0:T(8,128)(2,1)S(1)} %g0.5), channel_id=1, source_target_pairs={{0,4},{4,0},{8,12},{12,8},{16,20},{20,16},{24,28},{28,24},{1,5},{5... | collective-permute-start | bytes 294920 | tf_op jit(solution)/shard_map/g0/ppermute | solution.py:364
  138.9 9.5 %collective-permute-start.42 = (bf16[640,256]{1,0:T(8,128)(2,1)S(1)}, bf16[640,256]{1,0:T(8,128)(2,1)S(1)}, u32[]{:S(2)}, u32[]{:S(2)}) collective-permute-start(bf16[640,256]{1,0:T(8,128)(2,1)S(1)} %slice.205), channel_id=1, source_target_pairs={{0,2},{1,3},{2,0},{3,1},{4,6},{5,7},{6,4},{7,5},{8,10},{9,11},{10,... | collective-permute-start | bytes 983048 | tf_op jit(solution)/shard_map/g2/ppermute | solution.py:55
  140.4 10.2 %collective-permute-start.41 = (bf16[384,384]{1,0:T(8,128)(2,1)}, bf16[384,384]{1,0:T(8,128)(2,1)}, u32[]{:S(2)}, u32[]{:S(2)}) collective-permute-start(bf16[384,384]{1,0:T(8,128)(2,1)} %g0.4), channel_id=1, source_target_pairs={{0,4},{4,0},{8,12},{12,8},{16,20},{20,16},{24,28},{28,24},{1,5},{5... | collective-permute-start | bytes 884744 | tf_op jit(solution)/shard_map/g0/ppermute | solution.py:364
  143.3 7.3 %collective-permute-start.45 = (bf16[128,384]{1,0:T(8,128)(2,1)S(1)}, bf16[128,384]{1,0:T(8,128)(2,1)S(1)}, u32[]{:S(2)}, u32[]{:S(2)}) collective-permute-start(bf16[128,384]{1,0:T(8,128)(2,1)S(1)} %get-tuple-element.321), channel_id=1, source_target_pairs={{0,16},{4,20},{8,0},{12,4},{16,24},{20,28},{24,8},{28,12},{1,17},{... | collective-permute-start | bytes 294920 | tf_op jit(solution)/shard_map/g0/ppermute | solution.py:55
  144.0 6.7 %collective-permute-start.46 = (bf16[128,384]{1,0:T(8,128)(2,1)S(1)}, bf16[128,384]{1,0:T(8,128)(2,1)S(1)}, u32[]{:S(2)}, u32[]{:S(2)}) collective-permute-start(bf16[128,384]{1,0:T(8,128)(2,1)S(1)} %get-tuple-element.322), channel_id=1, source_target_pairs={{0,8},{4,12},{8,24},{12,28},{16,0},{20,4},{24,16},{28,20},{1,9},{5... | collective-permute-start | bytes 294920 | tf_op jit(solution)/shard_map/g0/ppermute | solution.py:55
  145.4 5.3 %collective-permute-start.50 = (bf16[128,256]{1,0:T(8,128)(2,1)S(1)}, bf16[128,256]{1,0:T(8,128)(2,1)S(1)}, u32[]{:S(2)}, u32[]{:S(2)}) collective-permute-start(bf16[128,256]{1,0:T(8,128)(2,1)S(1)} %g1.4), channel_id=1, source_target_pairs={{0,4},{4,0},{8,12},{12,8},{16,20},{20,16},{24,28},{28,24},{1,5},{5... | collective-permute-start | bytes 196616 | tf_op jit(solution)/shard_map/g1/ppermute | solution.py:364
  149.1 9.3 %collective-permute-start.49 = (bf16[128,256]{1,0:T(8,128)(2,1)S(1)}, bf16[128,256]{1,0:T(8,128)(2,1)S(1)}, u32[]{:S(2)}, u32[]{:S(2)}) collective-permute-start(bf16[128,256]{1,0:T(8,128)(2,1)S(1)} %g2.4), channel_id=1, source_target_pairs={{0,4},{4,0},{8,12},{12,8},{16,20},{20,16},{24,28},{28,24},{1,5},{5... | collective-permute-start | bytes 196616 | tf_op jit(solution)/shard_map/g2/ppermute | solution.py:364
  152.7 11.9 %collective-permute-start.47 = (bf16[256,384]{1,0:T(8,128)(2,1)S(1)}, bf16[256,384]{1,0:T(8,128)(2,1)S(1)}, u32[]{:S(2)}, u32[]{:S(2)}) collective-permute-start(bf16[256,384]{1,0:T(8,128)(2,1)S(1)} %pad_maximum_fusion.4), channel_id=1, source_target_pairs={{0,16},{4,20},{8,0},{12,4},{16,24},{20,28},{24,8},{28,12},{1,17},{... | collective-permute-start | bytes 589832 | tf_op jit(solution)/shard_map/g0/ppermute | solution.py:55
  153.3 11.6 %collective-permute-start.48 = (bf16[256,384]{1,0:T(8,128)(2,1)S(1)}, bf16[256,384]{1,0:T(8,128)(2,1)S(1)}, u32[]{:S(2)}, u32[]{:S(2)}) collective-permute-start(bf16[256,384]{1,0:T(8,128)(2,1)S(1)} %pad_maximum_fusion.5), channel_id=1, source_target_pairs={{0,8},{4,12},{8,24},{12,28},{16,0},{20,4},{24,16},{28,20},{1,9},{5... | collective-permute-start | bytes 589832 | tf_op jit(solution)/shard_map/g0/ppermute | solution.py:55
  154.8 10.2 %collective-permute-start.51 = (bf16[384,256]{1,0:T(8,128)(2,1)S(1)}, bf16[384,256]{1,0:T(8,128)(2,1)S(1)}, u32[]{:S(2)}, u32[]{:S(2)}) collective-permute-start(bf16[384,256]{1,0:T(8,128)(2,1)S(1)} %g1.5), channel_id=1, source_target_pairs={{0,4},{4,0},{8,12},{12,8},{16,20},{20,16},{24,28},{28,24},{1,5},{5... | collective-permute-start | bytes 589832 | tf_op jit(solution)/shard_map/g1/ppermute | solution.py:364
  155.9 11.7 %collective-permute-start.52 = (bf16[128,256]{1,0:T(8,128)(2,1)S(1)}, bf16[128,256]{1,0:T(8,128)(2,1)S(1)}, u32[]{:S(2)}, u32[]{:S(2)}) collective-permute-start(bf16[128,256]{1,0:T(8,128)(2,1)S(1)} %get-tuple-element.343), channel_id=1, source_target_pairs={{0,16},{4,20},{8,0},{12,4},{16,24},{20,28},{24,8},{28,12},{1,17},{... | collective-permute-start | bytes 196616 | tf_op jit(solution)/shard_map/g1/ppermute | solution.py:55
  158.4 9.3 %collective-permute-start.53 = (bf16[128,256]{1,0:T(8,128)(2,1)S(1)}, bf16[128,256]{1,0:T(8,128)(2,1)S(1)}, u32[]{:S(2)}, u32[]{:S(2)}) collective-permute-start(bf16[128,256]{1,0:T(8,128)(2,1)S(1)} %get-tuple-element.344), channel_id=1, source_target_pairs={{0,8},{4,12},{8,24},{12,28},{16,0},{20,4},{24,16},{28,20},{1,9},{5... | collective-permute-start | bytes 196616 | tf_op jit(solution)/shard_map/g1/ppermute | solution.py:55
  164.7 5.7 %collective-permute-start.56 = (bf16[384,256]{1,0:T(8,128)(2,1)S(1)}, bf16[384,256]{1,0:T(8,128)(2,1)S(1)}, u32[]{:S(2)}, u32[]{:S(2)}) collective-permute-start(bf16[384,256]{1,0:T(8,128)(2,1)S(1)} %g2.5), channel_id=1, source_target_pairs={{0,4},{4,0},{8,12},{12,8},{16,20},{20,16},{24,28},{28,24},{1,5},{5... | collective-permute-start | bytes 589832 | tf_op jit(solution)/shard_map/g2/ppermute | solution.py:364
  165.0 5.4 %collective-permute-start.57 = (bf16[128,256]{1,0:T(8,128)(2,1)S(1)}, bf16[128,256]{1,0:T(8,128)(2,1)S(1)}, u32[]{:S(2)}, u32[]{:S(2)}) collective-permute-start(bf16[128,256]{1,0:T(8,128)(2,1)S(1)} %get-tuple-element.359), channel_id=1, source_target_pairs={{0,16},{4,20},{8,0},{12,4},{16,24},{20,28},{24,8},{28,12},{1,17},{... | collective-permute-start | bytes 196616 | tf_op jit(solution)/shard_map/g2/ppermute | solution.py:55
  165.0 7.4 %collective-permute-start.58 = (bf16[128,256]{1,0:T(8,128)(2,1)S(1)}, bf16[128,256]{1,0:T(8,128)(2,1)S(1)}, u32[]{:S(2)}, u32[]{:S(2)}) collective-permute-start(bf16[128,256]{1,0:T(8,128)(2,1)S(1)} %get-tuple-element.360), channel_id=1, source_target_pairs={{0,8},{4,12},{8,24},{12,28},{16,0},{20,4},{24,16},{28,20},{1,9},{5... | collective-permute-start | bytes 196616 | tf_op jit(solution)/shard_map/g2/ppermute | solution.py:55
  167.8 7.7 %collective-permute-start.54 = (bf16[256,256]{1,0:T(8,128)(2,1)S(1)}, bf16[256,256]{1,0:T(8,128)(2,1)S(1)}, u32[]{:S(2)}, u32[]{:S(2)}) collective-permute-start(bf16[256,256]{1,0:T(8,128)(2,1)S(1)} %pad_maximum_fusion.6), channel_id=1, source_target_pairs={{0,16},{4,20},{8,0},{12,4},{16,24},{20,28},{24,8},{28,12},{1,17},{... | collective-permute-start | bytes 393224 | tf_op jit(solution)/shard_map/g1/ppermute | solution.py:55
  168.8 10.2 %collective-permute-start.55 = (bf16[256,256]{1,0:T(8,128)(2,1)S(1)}, bf16[256,256]{1,0:T(8,128)(2,1)S(1)}, u32[]{:S(2)}, u32[]{:S(2)}) collective-permute-start(bf16[256,256]{1,0:T(8,128)(2,1)S(1)} %pad_maximum_fusion.7), channel_id=1, source_target_pairs={{0,8},{4,12},{8,24},{12,28},{16,0},{20,4},{24,16},{28,20},{1,9},{5... | collective-permute-start | bytes 393224 | tf_op jit(solution)/shard_map/g1/ppermute | solution.py:55
  173.1 7.4 %collective-permute-start.59 = (bf16[256,256]{1,0:T(8,128)(2,1)S(1)}, bf16[256,256]{1,0:T(8,128)(2,1)S(1)}, u32[]{:S(2)}, u32[]{:S(2)}) collective-permute-start(bf16[256,256]{1,0:T(8,128)(2,1)S(1)} %pad_maximum_fusion.8), channel_id=1, source_target_pairs={{0,16},{4,20},{8,0},{12,4},{16,24},{20,28},{24,8},{28,12},{1,17},{... | collective-permute-start | bytes 393224 | tf_op jit(solution)/shard_map/g2/ppermute | solution.py:55
  173.2 8.7 %collective-permute-start.60 = (bf16[256,256]{1,0:T(8,128)(2,1)S(1)}, bf16[256,256]{1,0:T(8,128)(2,1)S(1)}, u32[]{:S(2)}, u32[]{:S(2)}) collective-permute-start(bf16[256,256]{1,0:T(8,128)(2,1)S(1)} %pad_maximum_fusion.9), channel_id=1, source_target_pairs={{0,8},{4,12},{8,24},{12,28},{16,0},{20,4},{24,16},{28,20},{1,9},{5... | collective-permute-start | bytes 393224 | tf_op jit(solution)/shard_map/g2/ppermute | solution.py:55
  (4 other events, 29.6 us)
